TPU v7x, 32 devices: a whole 2x2x4 slice. The times are simulated.
32 devices in a mesh: shards: 4 (over z), context: 2 (over x), tensor: 4 (over y, core).
Axes of the slice: x: 2, y: 2, z: 4, core: 2. Of those that a mesh axis runs over, the one named last changes fastest.
Arguments:
- block_input: bfloat16 [8, 1024, 2048], P('shards', 'context'), may hold values from -6 to 6
- output_grad: bfloat16 [8, 1024, 2048], P('shards', 'context'), may hold values from -6 to 6
- doc_lengths: int32 [8, 3], P('shards'), may hold values from 60 to 800, as said below
- norm_gain: bfloat16 [2048], P('shards'), may hold values from 0.5 to 1.5
- input_proj: bfloat16 [2048, 2, 4096], P('shards', None, 'tensor'), may hold values from -0.125 to 0.125
- conv_weight: bfloat16 [4096, 4], P(('tensor', 'shards')), may hold values from -3 to 3
- conv_bias: bfloat16 [4096], P(('tensor', 'shards')), may hold values from -3 to 3
- select_proj: bfloat16 [4096, 160], P(('tensor', 'shards')), may hold values from -0.09375 to 0.09375
- step_proj: bfloat16 [128, 4096], P('shards', 'tensor'), may hold values from -0.5 to 0.5
- step_bias: bfloat16 [4096], P(('tensor', 'shards')), may hold values from -7 to -3
- decay_log: bfloat16 [4096, 16], P(('tensor', 'shards')), may hold values from -4 to 0.5
- skip_weight: bfloat16 [4096], P(('tensor', 'shards')), may hold values from -4 to 4
- output_proj: bfloat16 [4096, 2048], P(('tensor', 'shards')), may hold values from -0.375 to 0.375
Outputs:
- block_output: bfloat16 [8, 1024, 2048], P('shards', 'context', 'tensor')
- input_grad: float32 [8, 1024, 2048], P('shards', 'context', 'tensor')
- norm_gain_grad: float32 [2048], P('shards')
- input_proj_grad: float32 [2048, 2, 4096], P('shards', None, 'tensor')
- conv_weight_grad: float32 [4096, 4], P(('tensor', 'shards'))
- conv_bias_grad: float32 [4096], P(('tensor', 'shards'))
- select_proj_grad: float32 [4096, 160], P(('tensor', 'shards'))
- step_proj_grad: float32 [128, 4096], P('shards', 'tensor')
- step_bias_grad: float32 [4096], P(('tensor', 'shards'))
- decay_log_grad: float32 [4096, 16], P(('tensor', 'shards'))
- skip_weight_grad: float32 [4096], P(('tensor', 'shards'))
- output_proj_grad: float32 [4096, 2048], P(('tensor', 'shards'))
Inputs may be any that keep to these rules, and one draw needn't show every extreme that they name: `doc_lengths`: each row holds the lengths of the three documents packed in order into one sequence; each row sums to 1024.
All inputs are finite; a program needn't handle non-finite values.
Results may differ from a plain program's by a relative error of at most 0.011.
Values may be sent and summed in bfloat16 or wider, within the bound.
No kernel may reach another device: no remote copies, remote signals or barrier semaphores. Data moves between devices by JAX's collectives and lax.ppermute only.
A program may use at most 256 MiB of HBM per device.

v0:
```python
import jax
import jax.numpy as jnp
from jax import lax
from jax.sharding import PartitionSpec as P

BLOCK = 128


EPS = 1e-05
HIGHEST = lax.Precision.HIGHEST


def shifted(array, axis, by):
    devices = lax.axis_size(axis)
    pairs = [(i, i + by) for i in range(devices) if 0 <= i + by < devices]
    return lax.ppermute(array, axis, pairs)


def entering(part, axis, combine, identity):
    place = lax.axis_index(axis)
    gathered = jax.tree.map(lambda a: lax.all_gather(a, axis), part)
    state = jax.tree.map(lambda a, e: jnp.zeros_like(a) + jnp.asarray(e, a.dtype), part, identity)

    def one(lap, state):
        return combine(
            state, jax.tree.map(lambda a: lax.dynamic_index_in_dim(a, lap, 0, False), gathered)
        )

    return lax.fori_loop(0, place, one, state)


def entering_2(array, axis, join, neutral):
    count = lax.axis_size(axis)
    place = lax.axis_index(axis)
    ahead = count - 1 - place
    gathered = jax.tree.map(
        lambda a, kind: lax.all_gather(a.astype(kind), axis), array, (jnp.bfloat16, jnp.bfloat16)
    )
    state = jax.tree.map(lambda a, e: jnp.zeros_like(a) + jnp.asarray(e, a.dtype), array, neutral)

    def one(lap, state):
        source = count - 1 - lap
        return join(
            state,
            jax.tree.map(
                lambda a, own: lax.dynamic_index_in_dim(a, source, 0, False).astype(own.dtype),
                gathered,
                array,
            ),
        )

    return lax.fori_loop(0, ahead, one, state)


def document_ids(lengths, positions):
    bounds = jnp.cumsum(lengths, axis=-1)[:, :2]
    passed = positions[None, :, None] >= bounds[:, None, :]
    return jnp.sum(passed.astype(jnp.int32), axis=-1)


def start_decay(step_block, doc_block, doc_prior, lower_ones, decay_rate):
    running = jnp.dot(lower_ones, step_block, precision=HIGHEST)
    keep_flag = (doc_block == doc_prior).astype(jnp.float32)
    carried = keep_flag[:, None, None] * jnp.exp(running[:, :, None] * decay_rate)
    return (running, carried)


def block_terms(step_block, value_block, in_block, doc_block, doc_prior, lower_ones, decay_rate):
    block_len = step_block.shape[0]
    running, carried = start_decay(step_block, doc_block, doc_prior, lower_ones, decay_rate)
    middle = running[block_len // 2]
    rise_factor = jnp.exp((running - middle)[:, :, None] * decay_rate)
    fall_factor = jnp.exp((middle - running)[:, :, None] * decay_rate)
    drive_term = (step_block * value_block)[:, :, None] * in_block[:, None, :]
    same_doc = ((doc_block[:, None] == doc_block[None, :]) & (lower_ones > 0)).astype(jnp.float32)
    weighted = (fall_factor * drive_term).reshape(block_len, -1)
    within = jnp.dot(same_doc, weighted, precision=HIGHEST).reshape(drive_term.shape)
    return (running, carried, rise_factor, fall_factor, drive_term, same_doc, within)


def on_device(
    block_input,
    output_grad,
    doc_lengths,
    norm_gain,
    input_proj,
    conv_weight,
    conv_bias,
    select_proj,
    step_proj,
    step_bias,
    decay_log,
    skip_weight,
    output_proj,
):
    seq_count, piece_len, model_width = block_input.shape
    gathered = (
        lax.all_gather(norm_gain, "shards", axis=0, tiled=True),
        lax.all_gather(input_proj, "shards", axis=0, tiled=True),
        lax.all_gather(conv_weight, "shards", axis=0, tiled=True),
        lax.all_gather(conv_bias, "shards", axis=0, tiled=True),
        lax.all_gather(select_proj, "shards", axis=0, tiled=True),
        lax.all_gather(step_proj, "shards", axis=0, tiled=True),
        lax.all_gather(step_bias, "shards", axis=0, tiled=True),
        lax.all_gather(decay_log, "shards", axis=0, tiled=True),
        lax.all_gather(skip_weight, "shards", axis=0, tiled=True),
        lax.all_gather(output_proj, "shards", axis=0, tiled=True),
    )
    (
        gain_full,
        proj_in,
        conv_taps,
        conv_shift,
        proj_select,
        proj_step,
        bias_step,
        log_decay,
        skip_local,
        proj_out,
    ) = gathered
    inner_local = proj_in.shape[2]
    rank_count = proj_step.shape[0]
    state_count = log_decay.shape[1]
    tap_count = conv_taps.shape[1]
    share_width = model_width // lax.axis_size("tensor")
    col_start = lax.axis_index("tensor") * share_width
    piece_start = lax.axis_index("context") * piece_len
    seq_length = piece_len * lax.axis_size("context")
    token_count = seq_count * piece_len
    block_len = BLOCK
    block_count = piece_len // block_len
    turn_count = seq_count * block_count
    positions = piece_start + jnp.arange(piece_len, dtype=jnp.int32)
    document = document_ids(doc_lengths, positions)
    before_pos = piece_start + jnp.arange(-(tap_count - 1), 0, dtype=jnp.int32)
    doc_before = jnp.where(before_pos[None, :] >= 0, document_ids(doc_lengths, before_pos), -1)
    after_pos = piece_start + piece_len + jnp.arange(tap_count - 1, dtype=jnp.int32)
    doc_after = jnp.where(after_pos[None, :] < seq_length, document_ids(doc_lengths, after_pos), -2)
    input_wide = block_input.astype(jnp.float32)
    inv_rms = lax.rsqrt(jnp.mean(input_wide * input_wide, axis=-1, keepdims=True) + EPS)
    unit_rows = input_wide * inv_rms
    gain_wide = gain_full.astype(jnp.float32)
    normed = (unit_rows * gain_wide).astype(jnp.bfloat16).reshape(token_count, model_width)
    in_matrix = proj_in.reshape(model_width, 2 * inner_local)
    projected_in = jnp.dot(normed, in_matrix, preferred_element_type=jnp.float32)
    x_part = (
        projected_in[:, :inner_local]
        .astype(jnp.bfloat16)
        .reshape(seq_count, piece_len, inner_local)
    )
    z_part = projected_in[:, inner_local:].astype(jnp.bfloat16)
    edge_in = shifted(x_part[:, piece_len - (tap_count - 1) :, :], "context", 1)
    x_extended = jnp.concatenate([edge_in, x_part], axis=1)
    doc_extended = jnp.concatenate([doc_before, document], axis=1)
    taps_wide = conv_taps.astype(jnp.float32)
    conv_pre = jnp.zeros((seq_count, piece_len, inner_local), jnp.float32) + conv_shift.astype(
        jnp.float32
    )
    tap_masks = []
    for offset in range(tap_count):
        same_doc = (doc_extended[:, offset : offset + piece_len] == document)[:, :, None]
        tap_masks.append(same_doc)
        conv_pre = (
            conv_pre
            + jnp.where(
                same_doc, x_extended[:, offset : offset + piece_len].astype(jnp.float32), 0.0
            )
            * taps_wide[:, offset]
        )
    values = jax.nn.silu(conv_pre).astype(jnp.bfloat16)
    value_rows = values.reshape(token_count, inner_local)
    partial_select = jnp.dot(value_rows, proj_select, preferred_element_type=jnp.float32)
    projected = lax.psum(partial_select, "tensor")
    step_low = projected[:, :rank_count].astype(jnp.bfloat16)
    state_in = projected[:, rank_count : rank_count + state_count]
    state_out = projected[:, rank_count + state_count :]
    step_pre = jnp.dot(step_low, proj_step, preferred_element_type=jnp.float32) + bias_step.astype(
        jnp.float32
    )
    step_size = jax.nn.softplus(step_pre)
    decay_rate = -jnp.exp(log_decay.astype(jnp.float32))

    def to_turns(source):
        return source.reshape((turn_count, block_len) + source.shape[1:])

    step_blocks = to_turns(step_size)
    value_blocks = to_turns(value_rows)
    in_blocks = to_turns(state_in)
    out_blocks = to_turns(state_out)
    doc_blocks = document.reshape(turn_count, block_len)
    doc_prior = jnp.concatenate(
        [doc_before[:, -1:], document[:, block_len - 1 : piece_len - 1 : block_len]], axis=1
    ).reshape(turn_count)
    block_place = jnp.arange(turn_count, dtype=jnp.int32) % block_count
    first_flag = block_place == 0
    last_flag = block_place == block_count - 1
    lower_ones = (jnp.arange(block_len)[:, None] >= jnp.arange(block_len)[None, :]).astype(
        jnp.float32
    )
    end_mask = (jnp.arange(block_len) == block_len - 1).astype(jnp.float32)[:, None, None]

    def forward_turn(carry_pair, inputs):
        state_run, decay_run = carry_pair
        step_block, value_block, in_block, out_block, doc_block, prior_doc, first_block = inputs
        state_run = jnp.where(first_block, 0.0, state_run)
        decay_run = jnp.where(first_block, 1.0, decay_run)
        running, carried, rise_factor, fall_factor, drive_term, same_doc, within = block_terms(
            step_block,
            value_block.astype(jnp.float32),
            in_block,
            doc_block,
            prior_doc,
            lower_ones,
            decay_rate,
        )
        states = rise_factor * within + carried * state_run
        output_block = jnp.sum(states * out_block[:, None, :], axis=-1)
        decay_end = decay_run * carried[-1]
        return (
            (states[-1], decay_end),
            (output_block, state_run, decay_run, states[-1], decay_end),
        )

    zero_state = jnp.zeros((inner_local, state_count), jnp.float32)
    _, (local_out, start_states, start_decays, end_states, end_decays) = lax.scan(
        forward_turn,
        (zero_state, zero_state + 1.0),
        (step_blocks, value_blocks, in_blocks, out_blocks, doc_blocks, doc_prior, first_flag),
    )
    piece_decay = end_decays.reshape(seq_count, block_count, inner_local, state_count)[:, -1]
    piece_state = end_states.reshape(seq_count, block_count, inner_local, state_count)[:, -1]

    def chain_forward(earlier, later):
        return (earlier[0] * later[0], later[0] * earlier[1] + later[1])

    identity = (jnp.ones_like(piece_decay), jnp.zeros_like(piece_state))
    _, state_entry = entering((piece_decay, piece_state), "context", chain_forward, identity)
    entry_turns = jnp.repeat(state_entry, block_count, axis=0)

    def entry_effect(inputs):
        step_block, out_block, doc_block, prior_doc, decay_start, entry_state = inputs
        _, carried = start_decay(step_block, doc_block, prior_doc, lower_ones, decay_rate)
        return jnp.sum(carried * (decay_start * entry_state)[None] * out_block[:, None, :], axis=-1)

    scan_out = local_out + lax.map(
        entry_effect, (step_blocks, out_blocks, doc_blocks, doc_prior, start_decays, entry_turns)
    )
    scan_rows = scan_out.reshape(token_count, inner_local)
    skip_wide = skip_local.astype(jnp.float32)
    ssm_out = scan_rows + skip_wide * value_rows.astype(jnp.float32)
    z_wide = z_part.astype(jnp.float32)
    z_sigmoid = jax.nn.sigmoid(z_wide)
    z_gate = z_wide * z_sigmoid
    gated_out = (ssm_out * z_gate).astype(jnp.bfloat16)
    partial_out = jnp.dot(gated_out, proj_out, preferred_element_type=jnp.float32).reshape(
        seq_count, piece_len, model_width
    )
    out_share = lax.psum_scatter(partial_out, "tensor", scatter_dimension=2, tiled=True)
    input_share = lax.dynamic_slice_in_dim(input_wide, col_start, share_width, 2)
    block_output = (input_share + out_share).astype(jnp.bfloat16)
    grad_rows = output_grad.reshape(token_count, model_width)
    grad_out_proj = jnp.einsum(
        "ti,td->id", gated_out, grad_rows, preferred_element_type=jnp.float32
    )
    grad_gated = jnp.einsum("td,id->ti", grad_rows, proj_out, preferred_element_type=jnp.float32)
    grad_ssm = grad_gated * z_gate
    grad_z = (grad_gated * ssm_out * z_sigmoid * (1.0 + z_wide * (1.0 - z_sigmoid))).astype(
        jnp.bfloat16
    )
    grad_skip = jnp.sum(grad_ssm * value_rows.astype(jnp.float32), axis=0)
    grad_blocks = to_turns(grad_ssm)

    def entry_pull(inputs):
        step_block, out_block, doc_block, prior_doc, decay_start, grad_block = inputs
        _, carried = start_decay(step_block, doc_block, prior_doc, lower_ones, decay_rate)
        return decay_start * jnp.sum(
            carried * grad_block[:, :, None] * out_block[:, None, :], axis=0
        )

    pull_blocks = lax.map(
        entry_pull, (step_blocks, out_blocks, doc_blocks, doc_prior, start_decays, grad_blocks)
    )
    piece_pull = jnp.sum(
        pull_blocks.reshape(seq_count, block_count, inner_local, state_count), axis=1
    )

    def chain_backward(earlier, later):
        return (later[0] * earlier[0], later[1] + later[0] * earlier[1])

    _, exit_grad = entering_2((piece_decay, piece_pull), "context", chain_backward, identity)
    exit_turns = jnp.repeat(exit_grad, block_count, axis=0)

    def backward_turn(grad_next, inputs):
        (
            step_block,
            value_block,
            in_block,
            out_block,
            doc_block,
            prior_doc,
            decay_start,
            state_start,
            entry_state,
            exit_value,
            last_block,
            grad_block,
        ) = inputs
        grad_end = jnp.where(last_block, exit_value, grad_next)
        value_wide = value_block.astype(jnp.float32)
        running, carried, rise_factor, fall_factor, drive_term, same_doc, within = block_terms(
            step_block, value_wide, in_block, doc_block, prior_doc, lower_ones, decay_rate
        )
        true_start = state_start + decay_start * entry_state
        states = rise_factor * within + carried * true_start
        grad_states = grad_block[:, :, None] * out_block[:, None, :] + end_mask * grad_end
        back_sum = jnp.dot(
            same_doc.T, (rise_factor * grad_states).reshape(block_len, -1), precision=HIGHEST
        ).reshape(grad_states.shape)
        grad_drive = fall_factor * back_sum
        grad_start = jnp.sum(carried * grad_states, axis=0)
        grad_log = grad_states * states - grad_drive * drive_term
        grad_run = jnp.sum(grad_log * decay_rate, axis=-1)
        grad_decay = jnp.sum(grad_log * running[:, :, None], axis=0)
        drive_in = jnp.sum(grad_drive * in_block[:, None, :], axis=-1)
        grad_step = jnp.dot(lower_ones.T, grad_run, precision=HIGHEST) + drive_in * value_wide
        grad_value = drive_in * step_block
        grad_in = jnp.sum(grad_drive * (step_block * value_wide)[:, :, None], axis=1)
        grad_out = jnp.sum(grad_block[:, :, None] * states, axis=1)
        return (grad_start, (grad_step, grad_value, grad_in, grad_out, grad_decay))

    _, (grad_step_blocks, grad_value_blocks, grad_in_blocks, grad_out_blocks, grad_decay_blocks) = (
        lax.scan(
            backward_turn,
            zero_state,
            (
                step_blocks,
                value_blocks,
                in_blocks,
                out_blocks,
                doc_blocks,
                doc_prior,
                start_decays,
                start_states,
                entry_turns,
                exit_turns,
                last_flag,
                grad_blocks,
            ),
            reverse=True,
        )
    )
    grad_step_rows = grad_step_blocks.reshape(token_count, inner_local)
    grad_value_scan = grad_value_blocks.reshape(token_count, inner_local)
    grad_decay_log = jnp.sum(grad_decay_blocks, axis=0) * decay_rate
    grad_step_pre = (grad_step_rows * jax.nn.sigmoid(step_pre)).astype(jnp.bfloat16)
    grad_step_bias = jnp.sum(grad_step_pre.astype(jnp.float32), axis=0)
    grad_step_proj = jnp.einsum(
        "tr,ti->ri", step_low, grad_step_pre, preferred_element_type=jnp.float32
    )
    grad_step_low = jnp.einsum(
        "ti,ri->tr", grad_step_pre, proj_step, preferred_element_type=jnp.float32
    )
    partial_grad_select = jnp.concatenate(
        [
            grad_step_low,
            grad_in_blocks.reshape(token_count, state_count),
            grad_out_blocks.reshape(token_count, state_count),
        ],
        axis=1,
    )
    grad_projected = lax.psum(partial_grad_select, "tensor").astype(jnp.bfloat16)
    grad_select = jnp.einsum(
        "ti,tr->ir", value_rows, grad_projected, preferred_element_type=jnp.float32
    )
    grad_values = (
        jnp.einsum("tr,ir->ti", grad_projected, proj_select, preferred_element_type=jnp.float32)
        + grad_value_scan
        + grad_ssm * skip_wide
    )
    conv_sigmoid = jax.nn.sigmoid(conv_pre)
    grad_conv = (
        grad_values.reshape(seq_count, piece_len, inner_local)
        * conv_sigmoid
        * (1.0 + conv_pre * (1.0 - conv_sigmoid))
    )
    edge_grad = shifted(grad_conv[:, : tap_count - 1, :], "context", -1)
    grad_extended = jnp.concatenate([grad_conv, edge_grad], axis=1)
    doc_following = jnp.concatenate([document, doc_after], axis=1)
    grad_x = jnp.zeros_like(grad_conv)
    tap_grads = []
    for offset in range(tap_count):
        distance = tap_count - 1 - offset
        same_doc = (doc_following[:, distance : distance + piece_len] == document)[:, :, None]
        grad_x = (
            grad_x
            + jnp.where(same_doc, grad_extended[:, distance : distance + piece_len], 0.0)
            * taps_wide[:, offset]
        )
        tap_grads.append(
            jnp.sum(
                jnp.where(
                    tap_masks[offset],
                    grad_conv * x_extended[:, offset : offset + piece_len].astype(jnp.float32),
                    0.0,
                ),
                axis=(0, 1),
            )
        )
    grad_conv_weight = jnp.stack(tap_grads, axis=1)
    grad_conv_bias = jnp.sum(grad_conv, axis=(0, 1))
    grad_x_rows = grad_x.astype(jnp.bfloat16).reshape(token_count, inner_local)
    grad_mixed = jnp.concatenate([grad_x_rows, grad_z], axis=1)
    grad_in_proj = jnp.einsum(
        "td,tk->dk", normed, grad_mixed, preferred_element_type=jnp.float32
    ).reshape(model_width, 2, inner_local)
    partial_normed = jnp.einsum(
        "tk,dk->td", grad_mixed, in_matrix, preferred_element_type=jnp.float32
    ).reshape(seq_count, piece_len, model_width)
    grad_share_out = lax.dynamic_slice_in_dim(output_grad, col_start, share_width, 2).astype(
        jnp.float32
    )
    unit_share = lax.dynamic_slice_in_dim(unit_rows, col_start, share_width, 2)
    grad_normed = lax.psum(partial_normed, "tensor")
    weighted = grad_normed * gain_wide
    grad_gain = jnp.sum(grad_normed * unit_rows, axis=(0, 1))
    row_dots = jnp.sum(unit_rows * weighted, axis=-1, keepdims=True)
    weighted_share = lax.dynamic_slice_in_dim(weighted, col_start, share_width, 2)
    grad_norm_in = inv_rms * (weighted_share - unit_share * (row_dots / model_width))
    input_grad = grad_share_out + grad_norm_in
    gradients = (
        grad_gain,
        grad_in_proj,
        grad_conv_weight,
        grad_conv_bias,
        grad_select,
        grad_step_proj,
        grad_step_bias,
        grad_decay_log,
        grad_skip,
        grad_out_proj,
    )
    reduced = (
        lax.psum_scatter(gradients[0], ("shards", "context"), scatter_dimension=0, tiled=True),
        lax.psum_scatter(gradients[1], ("shards", "context"), scatter_dimension=0, tiled=True),
        lax.psum_scatter(gradients[2], ("shards", "context"), scatter_dimension=0, tiled=True),
        lax.psum_scatter(gradients[3], ("shards", "context"), scatter_dimension=0, tiled=True),
        lax.psum_scatter(gradients[4], ("shards", "context"), scatter_dimension=0, tiled=True),
        lax.psum_scatter(gradients[5], ("shards", "context"), scatter_dimension=0, tiled=True),
        lax.psum_scatter(gradients[6], ("shards", "context"), scatter_dimension=0, tiled=True),
        lax.psum_scatter(gradients[7], ("shards", "context"), scatter_dimension=0, tiled=True),
        lax.psum_scatter(gradients[8], ("shards", "context"), scatter_dimension=0, tiled=True),
        lax.psum_scatter(gradients[9], ("shards", "context"), scatter_dimension=0, tiled=True),
    )
    finished = (
        lax.all_gather(reduced[0], "context", axis=0, tiled=True),
        lax.all_gather(reduced[1], "context", axis=0, tiled=True),
        lax.all_gather(reduced[2], "context", axis=0, tiled=True),
        lax.all_gather(reduced[3], "context", axis=0, tiled=True),
        lax.all_gather(reduced[4], "context", axis=0, tiled=True),
        lax.all_gather(reduced[5], "context", axis=0, tiled=True),
        lax.all_gather(reduced[6], "context", axis=0, tiled=True),
        lax.all_gather(reduced[7], "context", axis=0, tiled=True),
        lax.all_gather(reduced[8], "context", axis=0, tiled=True),
        lax.all_gather(reduced[9], "context", axis=0, tiled=True),
    )
    return (block_output, input_grad) + tuple(finished)


def solution(mesh):
    placed = (
        P("shards", "context", None),
        P("shards", "context", None),
        P("shards", None),
        P("shards"),
        P("shards", None, "tensor"),
        P(("tensor", "shards"), None),
        P(("tensor", "shards")),
        P(("tensor", "shards"), None),
        P("shards", "tensor"),
        P(("tensor", "shards")),
        P(("tensor", "shards"), None),
        P(("tensor", "shards")),
        P(("tensor", "shards"), None),
    )
    return jax.shard_map(
        on_device,
        mesh=mesh,
        in_specs=placed,
        out_specs=(
            P("shards", "context", "tensor"),
            P("shards", "context", "tensor"),
            P("shards"),
            P("shards", None, "tensor"),
            P(("tensor", "shards"), None),
            P(("tensor", "shards")),
            P(("tensor", "shards"), None),
            P("shards", "tensor"),
            P(("tensor", "shards")),
            P(("tensor", "shards"), None),
            P(("tensor", "shards")),
            P(("tensor", "shards"), None),
        ),
        check_vma=False,
    )
```

profile of v0, /device:TPU:0, one launch (start us, length us, event | category | flops | bytes accessed | tf_op | source)
XLA Modules:
  0.0 2614.6 jit_solution(1158287100744193348)
XLA Ops:
  8.6 13.5 all-gather.5
  23.1 15.6 all_gather.77
  45.9 116.2 %all-gather.17.cloned.1.call-done = bf16[2048,2,1024]{2,1,0:T(2,128)(2,1)} async-done(((bf16[512,2,1024]{2,1,0:T(2,128)(2,1)}), bf16[2048,2,1024]{2,1,0:T(2,128)(2,1)}) %all-gather.17.cloned.1.call-update) | async-done | bytes 8388624 | tf_op jit(solution)/shard_map/all_gather | solution.py:99
  187.4 14.7 all_gather.78
  219.9 13.9 all_gather.81
  253.5 14.8 all_gather.79
  286.1 270.2 %while.105 = (s32[]{:T(128)}, f32[1024,16]{0,1:T(8,128)S(1)}, f32[1024,16]{0,1:T(8,128)S(1)}, f32[8,128,1024]{2,1,0:T(8,128)}, f32[8,1024,16]{1,2,0:T(8,128)S(1)...) while((s32[]{:T(128)}, f32[1024,16]{0,1:T(8,128)S(1)}, ...), condition=%wide.wide.region_7.8_spmd.clone.clone, body=%wide.wide.region_5.7_spmd.clone.clone.sunk | while | flops 3450388736 | bytes 63112972 | solution.py:225
  573.7 76.9 %while.102 = (s32[]{:T(128)}, f32[8,128,1024]{2,1,0:T(8,128)}, s32[8,128]{1,0:T(8,128)S(1)}, s32[8]{0:T(128)}, f32[8,128,1024]{2,1,0:T(8,128)}, /*index=5*/f32[1...) while((s32[]{:T(128)}, f32[8,128,1024]{2,1,0:T(8,128)}, ...), condition=%wide.region_12.13_spmd.clone, body=%wide.region_10.12_spmd.clone.sunk | while | flops 211730688 | bytes 4564625 | solution.py:245
  657.6 14.2 fusion.81
  671.8 73.2 %while.103 = (s32[]{:T(128)}, f32[8,1024,16]{1,2,0:T(8,128)S(1)}, f32[8,1024,16]{1,2,0:T(8,128)}, s32[8,128]{1,0:T(8,128)S(1)}, s32[8]{0:T(128)}, /*index=5*/f32...) while((s32[]{:T(128)}, f32[8,1024,16]{1,2,0:T(8,128)S(1)}, ...), condition=%wide.region_17.18_spmd.clone, body=%wide.region_15.17_spmd.clone.sunk | while | flops 211845376 | bytes 4564625 | solution.py:280
  773.9 886.4 %while.104 = (s32[]{:T(128)}, f32[1024,16]{0,1:T(8,128)S(1)}, f32[8,128,1024]{2,1,0:T(8,128)}, f32[8,128,1024]{2,1,0:T(8,128)}, f32[8,128,16]{1,0,2:T(8,128)}, /...) while((s32[]{:T(128)}, f32[1024,16]{0,1:T(8,128)S(1)}, ...), condition=%wide.wide.region_28.29_spmd.clone.clone, body=%wide.wide.region_21.28_spmd.clone.clone.sunk | while | flops 6942618112 | bytes 186964048 | solution.py:332
  815.1 12.8 fusion.213
  843.2 19.5 multiply_subtract_fusion.3
  862.8 14.5 multiply_reduce_fusion.20
  926.2 12.7 fusion.213
  954.2 19.4 multiply_subtract_fusion.3
  973.6 14.5 multiply_reduce_fusion.20
  1036.8 12.7 fusion.213
  1064.8 19.4 multiply_subtract_fusion.3
  1084.2 14.5 multiply_reduce_fusion.20
  1147.4 12.7 fusion.213
  1175.5 19.4 multiply_subtract_fusion.3
  1194.8 14.5 multiply_reduce_fusion.20
  1258.0 12.7 fusion.213
  1286.1 19.4 multiply_subtract_fusion.3
  1305.5 14.5 multiply_reduce_fusion.20
  1368.7 12.7 fusion.213
  1396.7 19.4 multiply_subtract_fusion.3
  1416.1 14.5 multiply_reduce_fusion.20
  1479.3 12.7 fusion.213
  1507.3 19.4 multiply_subtract_fusion.3
  1526.7 14.5 multiply_reduce_fusion.20
  1589.9 12.7 fusion.213
  1618.0 19.4 multiply_subtract_fusion.3
  1637.3 14.5 multiply_reduce_fusion.20
  1667.6 17.9 all-reduce.12
  1717.8 15.3 fusion.139
  1737.8 15.4 reshape.449
  1754.7 14.7 fusion.100
  1780.6 232.6 %reduce-scatter.12.cloned.1.call-done = f32[256,2,1024]{2,0,1:T(8,128)} async-done(((f32[2048,2,1024]{2,0,1:T(8,128)}), f32[256,2,1024]{2,0,1:T(8,128)}) %reduce-scatter.12.cloned.1.call-update) | async-done | bytes 2097168 | tf_op jit(solution)/shard_map/reduce_scatter | solution.py:444
  2021.7 56.4 %reduce-scatter.22.cloned.1.call-done = f32[128,4]{1,0:T(8,128)} async-done(((f32[1024,4]{1,0:T(8,128)}), f32[128,4]{1,0:T(8,128)}) %reduce-scatter.22.cloned.1.call-update) | async-done | bytes 2064
  2083.3 59.4 %reduce-scatter.18.cloned.1.call-done = f32[128,16]{1,0:T(8,128)} async-done(((f32[1024,16]{1,0:T(8,128)}), f32[128,16]{1,0:T(8,128)}) %reduce-scatter.18.cloned.1.call-update) | async-done | bytes 8208 | tf_op jit(solution)/shard_map/reduce_scatter | solution.py:450
  2148.5 58.5 %reduce-scatter.16.cloned.1.call-done = f32[16,1024]{1,0:T(8,128)} async-done(((f32[128,1024]{1,0:T(8,128)}), f32[16,1024]{1,0:T(8,128)}) %reduce-scatter.16.cloned.1.call-update) | async-done | bytes 65552 | tf_op jit(solution)/shard_map/reduce_scatter | solution.py:448
  2212.1 60.9 %reduce-scatter.14.cloned.1.call-done = f32[128,160]{0,1:T(8,128)} async-done(((f32[1024,160]{0,1:T(8,128)}), f32[128,160]{0,1:T(8,128)}) %reduce-scatter.14.cloned.1.call-update) | async-done | bytes 81936 | tf_op jit(solution)/shard_map/reduce_scatter | solution.py:447
  2278.4 148.9 %all-reduce.11.cloned.1.call-done = f32[2,512,2048]{2,1,0:T(8,128)} async-done(((f32[2,512,2048]{2,1,0:T(8,128)}), f32[2,512,2048]{2,1,0:T(8,128)}) %all-reduce.11.cloned.1.call-update) | async-done | bytes 8388624 | tf_op jit(solution)/shard_map/psum | solution.py:423
  2437.7 36.8 %all-reduce.4 = (f32[2048]{0:T(1024)S(1)}, f32[1024]{0:T(1024)S(1)}, f32[1024]{0:T(1024)S(1)}, f32[1024]{0:T(1024)S(1)}) all-reduce(f32[2048]{0:T(1024)S(1)} %get-tuple-element.1360, f32[1024]{0:T(1024)S(1)} %get-tuple-element.1362, ...), channel_id=7, replica_groups=mesh['shards'=4,'context'=2,'tensor'=4] {'shards','context'}, use_global_device_ids=true, to_apply=%region_33.34.clone | all-reduce | flops 5120 | bytes 40960
  2505.4 31.1 %all-gather.23.cloned.1.call-done = f32[256,2048]{1,0:T(8,128)} async-done(((f32[128,2048]{1,0:T(8,128)}), f32[256,2048]{1,0:T(8,128)}) %all-gather.23.cloned.1.call-update) | async-done | bytes 2097168 | tf_op jit(solution)/shard_map/all_gather | solution.py:464
  2536.4 58.4 %all-gather.21.cloned.1.call-done = f32[512,2,1024]{2,0,1:T(8,128)} async-done(((f32[256,2,1024]{2,0,1:T(8,128)}), f32[512,2,1024]{2,0,1:T(8,128)}) %all-gather.21.cloned.1.call-update) | async-done | bytes 4194320 | tf_op jit(solution)/shard_map/all_gather | solution.py:456
  (1023 shorter events, 1213.3 us)
Async XLA Ops:
  7.2 154.9 %all-gather.17.cloned.1.call-start = ((), (), s32[]{:S(2)}) async-start(), calls=%async_computation.7 | async-start | bytes 10485760 | tf_op jit(solution)/shard_map/all_gather | solution.py:99
  7.9 265.0 %all-reduce.9.cloned.1.call-start = ((), (), s32[]{:S(2)}) async-start(), calls=%async_computation.8 | async-start | bytes 1310720 | tf_op jit(solution)/shard_map/psum | solution.py:173
  22.2 23.7 copy-start.27
  23.1 19.7 copy-start.2
  42.7 167.1 %copy-start.46 = (pred[2,512]{1,0:T(4,128)(4,1)}, pred[2,512]{1,0:T(4,128)(4,1)S(1)}, u32[]{:S(2)}) copy-start(pred[2,512]{1,0:T(4,128)(4,1)S(1)} %get-tuple-element.1551) | copy-start | bytes 3076
  42.7 167.1 %copy-start.48 = (pred[2,512]{1,0:T(4,128)(4,1)}, pred[2,512]{1,0:T(4,128)(4,1)S(1)}, u32[]{:S(2)}) copy-start(pred[2,512]{1,0:T(4,128)(4,1)S(1)} %get-tuple-element.1552) | copy-start | bytes 3076
  42.7 167.1 %copy-start.50 = (pred[2,512]{1,0:T(4,128)(4,1)}, pred[2,512]{1,0:T(4,128)(4,1)S(1)}, u32[]{:S(2)}) copy-start(pred[2,512]{1,0:T(4,128)(4,1)S(1)} %get-tuple-element.1553) | copy-start | bytes 3076
  42.8 167.1 %copy-start.38 = (f32[1024,1]{0,1:T(1,128)}, f32[1024,1]{0,1:T(1,128)S(1)}, u32[]{:S(2)}) copy-start(f32[1024,1]{0,1:T(1,128)S(1)} %get-tuple-element.1541) | copy-start | bytes 12292
  42.8 167.1 %copy-start.40 = (f32[1024,1]{0,1:T(1,128)}, f32[1024,1]{0,1:T(1,128)S(1)}, u32[]{:S(2)}) copy-start(f32[1024,1]{0,1:T(1,128)S(1)} %get-tuple-element.1542) | copy-start | bytes 12292
  42.8 167.1 %copy-start.42 = (f32[1024,1]{0,1:T(1,128)}, f32[1024,1]{0,1:T(1,128)S(1)}, u32[]{:S(2)}) copy-start(f32[1024,1]{0,1:T(1,128)S(1)} %get-tuple-element.1543) | copy-start | bytes 12292
  42.8 167.1 %copy-start.44 = (f32[1024,1]{0,1:T(1,128)}, f32[1024,1]{0,1:T(1,128)S(1)}, u32[]{:S(2)}) copy-start(f32[1024,1]{0,1:T(1,128)S(1)} %get-tuple-element.1544) | copy-start | bytes 12292
  183.7 31.6 %copy-start.10 = (bf16[1024,2048]{1,0:T(8,128)(2,1)}, bf16[1024,2048]{1,0:T(8,128)(2,1)S(1)}, u32[]{:S(2)}) copy-start(bf16[1024,2048]{1,0:T(8,128)(2,1)S(1)} %convolution_convert_fusion) | copy-start | bytes 12582916
  183.7 18.4 copy-start.61
  183.9 31.3 %copy-start.5 = (bf16[1024,1024]{1,0:T(8,128)(2,1)}, bf16[1024,1024]{1,0:T(8,128)(2,1)S(1)}, u32[]{:S(2)}) copy-start(bf16[1024,1024]{1,0:T(8,128)(2,1)S(1)} %slice.157) | copy-start | bytes 6291460
  184.0 25.8 collective-permute-start
  215.2 20.5 copy-start.62
  215.3 30.6 %copy-start.63 = (bf16[256]{0:T(256)(128)(2,1)S(1)}, bf16[256]{0:T(256)(128)(2,1)}, u32[]{:S(2)}) copy-start(bf16[256]{0:T(256)(128)(2,1)} %param.34) | copy-start | bytes 1540
  215.3 38.2 %copy-start.29 = (bf16[32,1024]{1,0:T(8,128)(2,1)S(1)}, bf16[32,1024]{1,0:T(8,128)(2,1)}, u32[]{:S(2)}) copy-start(bf16[32,1024]{1,0:T(8,128)(2,1)} %param.33) | copy-start | bytes 196612
  218.2 439.4 %all-gather.19.cloned.1.call-start = ((), (), s32[]{:S(2)}) async-start(), calls=%async_computation.9 | async-start | bytes 5242880 | tf_op jit(solution)/shard_map/all_gather | solution.py:107
  219.0 1561.1 %reduce-scatter.20.cloned.1.call-start = ((), (), s32[]{:S(2)}) async-start(), calls=%async_computation.17 | async-start | bytes 9437184 | tf_op jit(solution)/shard_map/reduce_scatter | solution.py:452
  253.5 28.4 %copy-start.54 = (f32[4,1,256]{2,1,0:T(1,128)}, f32[4,1,256]{2,1,0:T(1,128)S(1)}, u32[]{:S(2)}) copy-start(f32[4,1,256]{2,1,0:T(1,128)S(1)} %convert_element_type.273) | copy-start | bytes 12292
  268.3 13.5 copy-start.22
  556.3 17.4 copy-start.21
  765.8 1247.4 %reduce-scatter.12.cloned.1.call-start = ((), (), s32[]{:S(2)}) async-start(), calls=%async_computation.12 | async-start | bytes 18874368 | tf_op jit(solution)/shard_map/reduce_scatter | solution.py:444
  795.7 47.6 %copy-start.34 = (f32[128]{0:T(128)}, f32[128]{0:T(128)S(1)}, u32[]{:S(2)}) copy-start(f32[128]{0:T(128)S(1)} %fusion.212) | copy-start | bytes 1540 | tf_op jit(solution)/shard_map/while
  907.0 47.2 %copy-start.34 = (f32[128]{0:T(128)}, f32[128]{0:T(128)S(1)}, u32[]{:S(2)}) copy-start(f32[128]{0:T(128)S(1)} %fusion.212) | copy-start | bytes 1540 | tf_op jit(solution)/shard_map/while
  1017.6 47.2 %copy-start.34 = (f32[128]{0:T(128)}, f32[128]{0:T(128)S(1)}, u32[]{:S(2)}) copy-start(f32[128]{0:T(128)S(1)} %fusion.212) | copy-start | bytes 1540 | tf_op jit(solution)/shard_map/while
  1128.2 47.2 %copy-start.34 = (f32[128]{0:T(128)}, f32[128]{0:T(128)S(1)}, u32[]{:S(2)}) copy-start(f32[128]{0:T(128)S(1)} %fusion.212) | copy-start | bytes 1540 | tf_op jit(solution)/shard_map/while
  1238.9 47.2 %copy-start.34 = (f32[128]{0:T(128)}, f32[128]{0:T(128)S(1)}, u32[]{:S(2)}) copy-start(f32[128]{0:T(128)S(1)} %fusion.212) | copy-start | bytes 1540 | tf_op jit(solution)/shard_map/while
  1349.5 47.2 %copy-start.34 = (f32[128]{0:T(128)}, f32[128]{0:T(128)S(1)}, u32[]{:S(2)}) copy-start(f32[128]{0:T(128)S(1)} %fusion.212) | copy-start | bytes 1540 | tf_op jit(solution)/shard_map/while
  1460.1 47.2 %copy-start.34 = (f32[128]{0:T(128)}, f32[128]{0:T(128)S(1)}, u32[]{:S(2)}) copy-start(f32[128]{0:T(128)S(1)} %fusion.212) | copy-start | bytes 1540 | tf_op jit(solution)/shard_map/while
  1570.8 47.2 %copy-start.34 = (f32[128]{0:T(128)}, f32[128]{0:T(128)S(1)}, u32[]{:S(2)}) copy-start(f32[128]{0:T(128)S(1)} %fusion.212) | copy-start | bytes 1540 | tf_op jit(solution)/shard_map/while
  1666.7 18.8 copy-start.13
  1666.7 18.8 copy-start.53
  1697.1 5.9 collective-permute-start.1
  1733.1 345.0 %reduce-scatter.22.cloned.1.call-start = ((), (), s32[]{:S(2)}) async-start(), calls=%async_computation.19 | async-start | bytes 589824
  1734.4 408.3 %reduce-scatter.18.cloned.1.call-start = ((), (), s32[]{:S(2)}) async-start(), calls=%async_computation.16 | async-start | bytes 589824 | tf_op jit(solution)/shard_map/reduce_scatter | solution.py:450
  1735.4 471.6 %reduce-scatter.16.cloned.1.call-start = ((), (), s32[]{:S(2)}) async-start(), calls=%async_computation.15 | async-start | bytes 589824 | tf_op jit(solution)/shard_map/reduce_scatter | solution.py:448
  1737.8 15.4 copy-start.4
  1737.8 535.3 %reduce-scatter.14.cloned.1.call-start = ((), (), s32[]{:S(2)}) async-start(), calls=%async_computation.14 | async-start | bytes 737280 | tf_op jit(solution)/shard_map/reduce_scatter | solution.py:447
  1754.6 672.7 %all-reduce.11.cloned.1.call-start = ((), (), s32[]{:S(2)}) async-start(), calls=%async_computation.11 | async-start | bytes 16777216 | tf_op jit(solution)/shard_map/psum | solution.py:423
  1769.4 732.5 %reduce-scatter.10.cloned.1.call-start = ((), (), s32[]{:S(2)}) async-start(), calls=%async_computation.10 | async-start | bytes 10485760 | tf_op jit(solution)/shard_map/reduce_scatter | solution.py:258
  1780.0 756.4 %all-gather.23.cloned.1.call-start = ((), (), s32[]{:S(2)}) async-start(), calls=%async_computation.18 | async-start | bytes 3145728 | tf_op jit(solution)/shard_map/all_gather | solution.py:464
  1780.6 814.3 %all-gather.21.cloned.1.call-start = ((), (), s32[]{:S(2)}) async-start(), calls=%async_computation.13 | async-start | bytes 6291456 | tf_op jit(solution)/shard_map/all_gather | solution.py:456
  2013.3 414.0 %copy-start.28 = (f32[4,1,512]{2,1,0:T(1,128)S(1)}, f32[4,1,512]{2,1,0:T(1,128)}, u32[]{:S(2)}) copy-start(f32[4,1,512]{2,1,0:T(1,128)} %copy-done.27) | copy-start | bytes 24580
  2013.3 414.0 %copy-start.33 = (f32[2,512]{1,0:T(2,128)S(1)}, f32[2,512]{1,0:T(2,128)}, u32[]{:S(2)}) copy-start(f32[2,512]{1,0:T(2,128)} %copy-done.32) | copy-start | bytes 12292
  2278.4 159.3 %copy-start.60 = (f32[1024]{0:T(1024)S(1)}, f32[1024]{0:T(1024)}, u32[]{:S(2)}) copy-start(f32[1024]{0:T(1024)} %get-tuple-element.1509) | copy-start | bytes 12292
  2536.4 70.0 %copy-start.18 = (f32[256,2048]{1,0:T(8,128)S(1)}, f32[256,2048]{1,0:T(8,128)}, u32[]{:S(2)}) copy-start(f32[256,2048]{1,0:T(8,128)} %all-gather.23.cloned.1.call-done) | copy-start | bytes 6291460
  (105 other events, 735.6 us)
Sparse Core Ops, SparseCore 0:
  9.6 152.4 all-gather.16
  218.4 32.5 all-reduce.8
  252.5 81.2 all-gather.18
  766.0 148.1 reduce-scatter.19
  1733.2 280.0 reduce-scatter.11
  2017.0 60.9 reduce-scatter.21
  2081.8 60.9 reduce-scatter.17
  2146.1 60.8 reduce-scatter.15
  2211.3 61.7 reduce-scatter.13
  2275.4 151.9 all-reduce.10
  2429.9 71.8 reduce-scatter.9
  2503.3 33.1 all-gather.22
  2538.1 56.7 all-gather.20
where the time goes:
time: 2640 us; the launch traced here: 2610 us
  waiting for transfers between devices  835 us (32%)
  other arithmetic  584 us (22%)
  matrix products  482 us (18%)
  local copies, waits for them, and re-layouts  478 us (18%)
  blocking collectives  210 us (8%)
    reduce_scatter x1, waiting for transfers between devices, on_device(): lax.psum_scatter(gradients[1], ('shards', 'context'), scatter_dimension=0...  233 us
    dot_general x16, matrix products, block_terms(): jnp.dot(same_doc, weighted, precision=HIGHEST).reshape(drive_term.shape)  176 us
    dot_general x8, matrix products, backward_turn(): jnp.dot(same_doc.T, (rise_factor * grad_states).reshape(block_len, -1), p...  155 us
    psum x1, waiting for transfers between devices, on_device(): grad_normed = lax.psum(partial_normed, 'tensor')  149 us
    all_gather x1, waiting for transfers between devices, on_device(): lax.all_gather(input_proj, 'shards', axis=0, tiled=True)  116 us
    reduce_sum x8, other arithmetic, backward_turn(): grad_out = jnp.sum(grad_block[:, :, None] * states, axis=1)  116 us
    mul x8, other arithmetic, backward_turn(): rise_factor * grad_states  102 us
    mul x24, local copies, waits for them, and re-layouts, block_terms(): drive_term = (step_block * value_block)[:, :, None] * in_block[:, None, :]  89.8 us
  transfers between devices with their start and end apart: 15, of which 11 were waited for; matrix products, arithmetic and copies ran while one was open for 53% of the time, Pallas kernels for 0%

commit v1 on v0

v1 whole, which is shorter than its diff:
```python
import functools

import jax
import jax.numpy as jnp
from jax import lax
from jax.experimental import pallas as pl
from jax.experimental.pallas import tpu as pltpu
from jax.sharding import PartitionSpec as P

EPS = 1e-05
LANE = 128
LOG2E = 1.4426950408889634
BREAK = 1e6
f32 = jnp.float32
bf16 = jnp.bfloat16


def row8(ref, s, i, k, g):
    return jnp.broadcast_to(ref[s, i, k:k+1, g*LANE:(g+1)*LANE], (8, LANE))

def spread(bct_ref, hot_ref, wide, S, blocks):
    for s in range(S):
        rows = bct_ref[s].reshape(blocks*32, LANE)
        wide[s] = jnp.dot(rows, hot_ref[...], preferred_element_type=f32).reshape(blocks, 32, 8*LANE)

def fwd_kernel(S, G, L, se_ref, su_ref, bct_ref, rate_ref, hot_ref, sel_ref, y_ref, start_ref, h_s, wide, w_s):
    blocks = L//8
    @pl.when(pl.program_id(0) == 0)
    def _(): h_s[...] = jnp.zeros_like(h_s)
    start_ref[0] = h_s[...]
    spread(bct_ref, hot_ref, wide, S, blocks)
    def collect(i):
        for s in range(S):
            y_ref[s, i] = jnp.dot(sel_ref[...], w_s[i, s], preferred_element_type=f32)[0:8]
    def body(i, carry):
        hs = dict(zip([(s,g,j) for s in range(S) for g in range(G) for j in range(2)], carry))
        terms = {}
        for k in range(8):
            for s in range(S):
                b = [wide[s, i, j*8:(j+1)*8, k*LANE:(k+1)*LANE] for j in range(2)]
                c = [wide[s, i, 16+j*8:16+(j+1)*8, k*LANE:(k+1)*LANE] for j in range(2)]
                for g in range(G):
                    se = row8(se_ref, s, i, k, g); su = row8(su_ref, s, i, k, g)
                    prod = []
                    for j in range(2):
                        a = jnp.exp2(se*rate_ref[g, j*8:(j+1)*8])
                        h = a*hs[s,g,j] + su*b[j]
                        hs[s,g,j] = h
                        prod.append(c[j]*h)
                    w_s[i, s, k*16:(k+1)*16, g*LANE:(g+1)*LANE] = jnp.concatenate(prod, 0).astype(bf16)
        return tuple(hs.values())
    n = S*G*2
    out = lax.fori_loop(0, blocks, body, tuple(h_s[q*8:(q+1)*8] for q in range(n)))
    for i in range(blocks): collect(i)
    for q in range(n): h_s[q*8:(q+1)*8] = out[q]

def bwd_kernel(S, G, L, se_ref, su_ref, ds_ref, bct_ref, rate_ref, rate2_ref, hot_ref, sel_ref, start_ref,
               s_ref, q_ref, dbc_ref, dlog_ref, ag_s, h_s, wide):
    blocks = L//8
    keys = [(s,g,j) for s in range(S) for g in range(G) for j in range(2)]
    @pl.when(pl.program_id(0) == 0)
    def _():
        ag_s[...] = jnp.zeros_like(ag_s)
        dlog_ref[...] = jnp.zeros_like(dlog_ref)
    spread(bct_ref, hot_ref, wide, S, blocks)
    def again(i, carry):
        hs = dict(zip(keys, carry))
        for k in range(8):
            for s in range(S):
                b = [wide[s, i, j*8:(j+1)*8, k*LANE:(k+1)*LANE] for j in range(2)]
                for g in range(G):
                    se = row8(se_ref, s, i, k, g); su = row8(su_ref, s, i, k, g)
                    h_s[i*8+k, s*G+g] = jnp.concatenate([hs[s,g,0], hs[s,g,1]], 0).astype(bf16)
                    for j in range(2):
                        a = jnp.exp2(se*rate_ref[g, j*8:(j+1)*8])
                        hs[s,g,j] = a*hs[s,g,j] + su*b[j]
        return tuple(hs.values())
    n = S*G*2
    out = lax.fori_loop(0, blocks, again, tuple(start_ref[0, q*8:(q+1)*8] for q in range(n)))
    for s in range(S):
        for g in range(G):
            q = (s*G+g)*2
            h_s[L, s*G+g] = jnp.concatenate([out[q], out[q+1]], 0).astype(bf16)
    two = lambda v: jnp.concatenate([v, v], 0).astype(bf16)
    def body(r, carry):
        i = blocks - 1 - r
        ags = dict(zip(keys, carry))
        tq, ts, tl, tb, tc = {}, {}, {}, {}, {}
        for k in reversed(range(8)):
            for s in range(S):
                b16 = wide[s, i, 0:16, k*LANE:(k+1)*LANE].astype(bf16)
                c = [wide[s, i, 16+j*8:16+(j+1)*8, k*LANE:(k+1)*LANE] for j in range(2)]
                for g in range(G):
                    se = row8(se_ref, s, i, k, g); su = row8(su_ref, s, i, k, g); ds = row8(ds_ref, s, i, k, g)
                    a = [jnp.exp2(se*rate_ref[g, j*8:(j+1)*8]) for j in range(2)]
                    gr = [c[j]*ds + ags[s,g,j] for j in range(2)]
                    for j in range(2): ags[s,g,j] = a[j]*gr[j]
                    gb = jnp.concatenate(gr, 0).astype(bf16)
                    ab = jnp.concatenate(a, 0).astype(bf16)
                    gq = gb*(ab*h_s[i*8+k, s*G+g])
                    tq[s,g,k] = gq*rate2_ref[g]
                    tl[s,g,k] = gq*two(se)
                    ts[s,g,k] = gb*b16
                    tb[s,g,k] = gb*two(su)
                    tc[s,g,k] = h_s[i*8+k+1, s*G+g]*two(ds)
        def mat(t, s): return jnp.concatenate([jnp.concatenate([t[s,g,k] for k in range(8)], 0) for g in range(G)], 1)
        one = jnp.ones((16, G*LANE), bf16)
        for s in range(S):
            q_ref[s, i] = jnp.dot(sel_ref[...], mat(tq, s), preferred_element_type=f32)[0:8]
            s_ref[s, i] = jnp.dot(sel_ref[...], mat(ts, s), preferred_element_type=f32)[0:8]
            dlog_ref[...] += jnp.dot(hot16_of(sel_ref), mat(tl, s), preferred_element_type=f32)
            nt = (((1,), (1,)), ((), ()))
            dbc_ref[s, i, 0:1] = lax.dot_general(one, mat(tb, s), nt, preferred_element_type=f32)[0:1]
            dbc_ref[s, i, 1:2] = lax.dot_general(one, mat(tc, s), nt, preferred_element_type=f32)[0:1]
        return tuple(ags.values())
    ags = lax.fori_loop(0, blocks, body, tuple(ag_s[q*8:(q+1)*8] for q in range(n)))
    for q in range(n): ag_s[q*8:(q+1)*8] = ags[q]

def hot16_of(sel_ref):
    r = lax.broadcasted_iota(jnp.int32, (16, 128), 0); c = lax.broadcasted_iota(jnp.int32, (16, 128), 1)
    return (lax.rem(c, 16) == r).astype(bf16)

def constants():
    hot = (jnp.arange(128)[:,None] % 8 == (jnp.arange(8*LANE)//LANE)[None,:]) & (jnp.arange(128)[:,None] < 24)
    sel = jnp.arange(16)[:,None] == (jnp.arange(128)//16)[None,:]
    return hot.astype(bf16), sel.astype(bf16)

def by_eights(bc):
    S, T = bc.shape[:2]
    x = bc.reshape(S, T//8, 8, 32).swapaxes(2, 3)
    hi = lax.reduce_precision(x, 8, 7); mid = lax.reduce_precision(x - hi, 8, 7); lo = x - hi - mid
    hi, mid, lo = (v.astype(bf16) for v in (hi, mid, lo))
    return jnp.concatenate([hi, mid, lo, jnp.zeros(hi.shape[:3]+(104,), bf16)], -1)

def tok(S, L, C, rev=None):
    im = (lambda i: (0, i, 0, 0)) if rev is None else (lambda i: (0, rev-1-i, 0, 0))
    return pl.BlockSpec((S, L//8, 8, C), im)
def whole(*shape): return pl.BlockSpec(shape, lambda i: (0,)*len(shape))

def scan_forward(se, su, bct, rate2e, hot, sel, L=64):
    S, T, C = se.shape; G = C//LANE
    v = lambda x: x.reshape(S, T//8, 8, C)
    y, start = pl.pallas_call(functools.partial(fwd_kernel, S, G, L), grid=(T//L,),
        in_specs=[tok(S,L,C), tok(S,L,C), pl.BlockSpec((S, L//8, 32, LANE), lambda i: (0,i,0,0)), whole(G,16,LANE), whole(128, 8*LANE), whole(16,128)],
        out_specs=[tok(S,L,C), pl.BlockSpec((1, S*G*16, LANE), lambda i: (i,0,0))],
        out_shape=[jax.ShapeDtypeStruct((S,T//8,8,C), f32), jax.ShapeDtypeStruct((T//L, S*G*16, LANE), f32)],
        scratch_shapes=[pltpu.VMEM((S*G*16, LANE), f32), pltpu.VMEM((S, L//8, 32, 8*LANE), f32), pltpu.VMEM((L//8, S, LANE, C), bf16)],
        compiler_params=pltpu.CompilerParams(vmem_limit_bytes=56<<20))(v(se), v(su), bct, rate2e, hot, sel)
    return y.reshape(S,T,C), start

def scan_backward(se, su, ds, bct, rate2e, rate, hot, sel, start, L=64):
    S, T, C = se.shape; G = C//LANE; nb = T//L
    v = lambda x: x.reshape(S, T//8, 8, C)
    t = tok(S,L,C,nb)
    sg, q, dbc, dlog = pl.pallas_call(functools.partial(bwd_kernel, S, G, L), grid=(nb,),
        in_specs=[t, t, t, pl.BlockSpec((S, L//8, 32, LANE), lambda i: (0,nb-1-i,0,0)), whole(G,16,LANE), whole(G,16,LANE), whole(128, 8*LANE), whole(16,128),
                  pl.BlockSpec((1, S*G*16, LANE), lambda i: (nb-1-i,0,0))],
        out_specs=[t, t, pl.BlockSpec((S, L//8, 2, LANE), lambda i: (0,nb-1-i,0,0)), whole(16, C)],
        out_shape=[jax.ShapeDtypeStruct((S,T//8,8,C), f32)]*2 + [jax.ShapeDtypeStruct((S,T//8,2,LANE), f32), jax.ShapeDtypeStruct((16,C), f32)],
        scratch_shapes=[pltpu.VMEM((S*G*16, LANE), f32), pltpu.VMEM((L+1, S*G, 16, LANE), bf16), pltpu.VMEM((S, L//8, 32, 8*LANE), f32)],
        compiler_params=pltpu.CompilerParams(vmem_limit_bytes=56<<20))(v(se), v(su), v(ds), bct, rate2e, rate.astype(bf16), hot, sel, start)
    dbc = dbc.reshape(S, T//8, 2, 8, 16).swapaxes(2, 3).reshape(S, T, 32)
    return sg.reshape(S,T,C), q.reshape(S,T,C), dbc, dlog


def after(array, earlier_one):
    return lax.optimization_barrier((array, earlier_one))[0]


def line_gather(array, axis):
    count = lax.axis_size(axis)
    place = lax.axis_index(axis)
    right, left = array, array
    window = [array]
    for step in range(1, count):
        right = lax.ppermute(right, axis, [(i, i + 1) for i in range(step - 1, count - 1)])
        left = lax.ppermute(left, axis, [(i, i - 1) for i in range(1, count - step + 1)])
        window = [right] + window + [left]
    window = jnp.stack(window)
    return lax.dynamic_slice_in_dim(window, count - 1 - place, count, 0)


def line_gather_at_once(array, axis):
    count = lax.axis_size(axis)
    return lax.all_to_all(jnp.broadcast_to(array[None], (count,) + array.shape), axis, 0, 0)


def line_scatter(blocks, axis):
    return jnp.sum(lax.all_to_all(blocks, axis, 0, 0).astype(f32), axis=0)


class Paired:
    def __init__(self):
        self.context = lax.axis_index("context")
        self.tensor = lax.axis_index("tensor")
        self.core = self.tensor % 2

    def across(self, array):
        return lax.ppermute(array, "context", [(0, 1), (1, 0)])

    def near(self, array):
        return lax.ppermute(array, "tensor", [(0, 1), (1, 0), (2, 3), (3, 2)])

    def far(self, array):
        return lax.ppermute(array, "tensor", [(0, 2), (2, 0), (1, 3), (3, 1)])

    def pieces_soon(self, array):
        rows = array.shape[0]
        side = rows * 11 // 32
        middle = rows - 2 * side
        chip = self.tensor // 2

        def outer(chip, core):
            return chip * (side + middle) + core * (side // 2)

        def inner(core):
            return side + core * (middle // 2)

        one = self.across(lax.dynamic_slice_in_dim(array, outer(chip, self.core), side // 2, 0))
        two = self.across(lax.dynamic_slice_in_dim(array, inner(self.core), middle // 2, 0))
        three = self.far(one)
        out = jnp.zeros_like(array)
        for block, start, other in (
            (one, outer(chip, self.core), outer(chip, 1 - self.core)),
            (two, inner(self.core), inner(1 - self.core)),
            (three, outer(1 - chip, self.core), outer(1 - chip, 1 - self.core)),
        ):
            out = lax.dynamic_update_slice_in_dim(out, block, start, 0)
            out = lax.dynamic_update_slice_in_dim(out, self.near(block), other, 0)
        return [array, out]

    def pieces(self, array, dependency):
        half = array.shape[0] // 2
        block = self.across(after(lax.dynamic_slice_in_dim(array, self.core * half, half, 0), dependency))
        out = lax.dynamic_update_slice_in_dim(jnp.zeros_like(array), block, self.core * half, 0)
        out = lax.dynamic_update_slice_in_dim(out, self.near(block), (1 - self.core) * half, 0)
        return [array, out]

    def in_order(self, arrays, seqs):
        own, other = (a.reshape(seqs, -1, a.shape[-1]) for a in arrays)
        first = self.context == 0
        return jnp.concatenate([jnp.where(first, own, other), jnp.where(first, other, own)], axis=1)

    def own_first(self, array):
        piece = array.shape[1] // 2
        early, late = array[:, :piece], array[:, piece:]
        first = self.context == 0
        return [
            jnp.where(first, early, late).reshape(-1, array.shape[-1]),
            jnp.where(first, late, early).reshape(-1, array.shape[-1]),
        ]

    def total(self, array):
        half = array.shape[0] // 2
        mine = lax.dynamic_slice_in_dim(array, self.core * half, half, 0)
        other = lax.dynamic_slice_in_dim(array, (1 - self.core) * half, half, 0).astype(bf16)
        mine = mine + self.near(other).astype(f32)
        first, second = mine[: half // 2], mine[half // 2 :]
        first = first + self.far(first.astype(bf16)).astype(f32)
        second = second + self.across(second.astype(bf16)).astype(f32)
        first = first + self.across(first.astype(bf16)).astype(f32)
        second = second + self.far(second.astype(bf16)).astype(f32)
        mine = jnp.concatenate([first, second], axis=0)
        other = self.near(mine.astype(bf16)).astype(f32)
        zero = self.core == 0
        return jnp.concatenate([jnp.where(zero, mine, other), jnp.where(zero, other, mine)])

    def share(self, product):
        keep = product((self.tensor, self.tensor ^ 2))
        give = product((self.tensor ^ 1, self.tensor ^ 3))
        rows, width = keep[0].shape
        half, width = rows // 2, width // 2
        own, other = ((k.astype(f32) + self.near(g).astype(f32)) for k, g in zip(keep, give))
        far = self.far(jnp.stack([own[:half, width:], other[:half, width:]]).astype(bf16))
        across = self.across(other[half:].astype(bf16))
        first = own[:half, :width] + far[0].astype(f32)
        give = other[:half, :width] + far[1].astype(f32)
        second = own[half:] + across.astype(f32)
        first = first + self.across(give.astype(bf16)).astype(f32)
        second = second[:, :width] + self.far(second[:, width:].astype(bf16)).astype(f32)
        return jnp.concatenate([first, second], axis=0)

    def row_total(self, array):
        array = array + self.near(array)
        return array + self.far(array)

    def vector_total(self, array):
        return self.row_total(array + self.across(array))

    def both(self, array):
        other = self.across(array)
        zero = self.context == 0
        return jnp.stack([jnp.where(zero, array, other), jnp.where(zero, other, array)])


class General:
    def pieces_soon(self, array):
        return [lax.all_gather(array, "context", tiled=True)]

    def pieces(self, array, dependency):
        return self.pieces_soon(array)

    def in_order(self, arrays, seqs):
        array = arrays[0].reshape(lax.axis_size("context"), seqs, -1, arrays[0].shape[-1])
        return array.swapaxes(0, 1).reshape(seqs, -1, array.shape[-1])

    def own_first(self, array):
        width = array.shape[-1]
        array = array.reshape(array.shape[0], lax.axis_size("context"), -1, width)
        return [array.swapaxes(0, 1).reshape(-1, width)]

    def total(self, array):
        return lax.psum(array, ("context", "tensor"))

    def share(self, product):
        blocks = [product((block,))[0].astype(f32) for block in range(lax.axis_size("tensor"))]
        parts = lax.psum_scatter(jnp.concatenate(blocks, axis=-1), "context", scatter_dimension=0, tiled=True)
        return lax.psum_scatter(parts, "tensor", scatter_dimension=1, tiled=True)

    def row_total(self, array):
        return lax.psum(array, "tensor")

    def vector_total(self, array):
        return lax.psum(array, ("context", "tensor"))

    def both(self, array):
        return lax.all_gather(array, "context")


def document_ids(lengths, positions):
    bounds = jnp.cumsum(lengths, axis=-1)[:, :2]
    passed = positions[None, :, None] >= bounds[:, None, :]
    return jnp.sum(passed.astype(jnp.int32), axis=-1)


def earlier(array, by):
    return jnp.pad(array, ((0, 0), (by, 0), (0, 0)))[:, : array.shape[1]]


def later(array, by):
    return jnp.pad(array, ((0, 0), (0, by), (0, 0)))[:, by:]


def dot(a, b, out=f32):
    return jnp.dot(a, b, preferred_element_type=f32).astype(out)


def dot_t(a, b, out=f32):
    return lax.dot_general(a, b, (((1,), (1,)), ((), ())), preferred_element_type=f32).astype(out)


def t_dot(a, b, out=f32):
    return lax.dot_general(a, b, (((0,), (0,)), ((), ())), preferred_element_type=f32).astype(out)


def on_device(
    block_input,
    output_grad,
    doc_lengths,
    norm_gain,
    input_proj,
    conv_weight,
    conv_bias,
    select_proj,
    step_proj,
    step_bias,
    decay_log,
    skip_weight,
    output_proj,
):
    seqs, piece, model_width = block_input.shape
    shards, contexts, tensors = (lax.axis_size(axis) for axis in ("shards", "context", "tensor"))
    shard, context, tensor = (lax.axis_index(axis) for axis in ("shards", "context", "tensor"))
    moves = Paired() if (contexts, tensors) == (2, 4) else General()
    length = piece * contexts
    tokens = seqs * length
    depth = input_proj.shape[0]
    part = conv_weight.shape[0] // contexts
    inner = part * shards
    states = decay_log.shape[1]
    rank = step_proj.shape[0] * shards
    selected = select_proj.shape[1]
    taps = conv_weight.shape[1]
    share_width = model_width // tensors

    def mine(array):
        return lax.dynamic_slice_in_dim(array, context * part, part, 0)

    def my_columns(array):
        blocks = [
            lax.dynamic_slice_in_dim(array, (block * contexts + context) * part, part, array.ndim - 1)
            for block in range(shards)
        ]
        return jnp.concatenate(blocks, axis=-1)

    in_x = my_columns(input_proj[:, 0])
    in_z = my_columns(input_proj[:, 1])
    vectors = jnp.concatenate(
        [
            mine(select_proj),
            mine(conv_weight),
            mine(decay_log),
            mine(conv_bias)[:, None],
            mine(step_bias)[:, None],
            mine(skip_weight)[:, None],
        ],
        axis=1,
    )
    vectors = jnp.pad(vectors, ((0, 0), (0, 2 * LANE - vectors.shape[1])))
    flat = [in_x, my_columns(step_proj), vectors.reshape(-1, inner), norm_gain.reshape(-1, inner)]
    counts = [f.shape[0] for f in flat]
    starts_at = [sum(counts[:i]) for i in range(len(counts) + 1)]
    first_weights = line_gather(jnp.concatenate(flat, axis=0), "shards")

    def taken(i):
        return first_weights[:, starts_at[i] : starts_at[i + 1]]

    proj_x = taken(0).reshape(model_width, inner)
    proj_step = taken(1).reshape(rank, inner)
    vectors = taken(2).reshape(inner, 2 * LANE)
    gain = taken(3).reshape(model_width).astype(f32)
    proj_select = vectors[:, :selected]
    rest = vectors[:, selected:].astype(f32)
    conv_taps = rest[:, :taps].T
    decay_rate = -jnp.exp(rest[:, taps : taps + states])
    conv_shift, bias_step, skip = (rest[:, taps + states + i] for i in range(3))

    rows_all = moves.pieces_soon(block_input.reshape(seqs * piece, model_width))
    grad_all = moves.pieces(output_grad.reshape(seqs * piece, model_width), rows_all[-1])

    proj_z = line_gather_at_once(after(in_z, first_weights), "shards").reshape(model_width, inner)
    proj_out = line_gather_at_once(after(mine(output_proj), proj_z), "shards").reshape(inner, model_width)

    def normalised(array):
        wide = array.astype(f32)
        inv_rms = lax.rsqrt(jnp.mean(wide * wide, axis=-1, keepdims=True) + EPS)
        return wide * inv_rms, inv_rms

    normed = [(normalised(r)[0] * gain).astype(bf16) for r in rows_all]

    def to_channels(arrays, weights, product, out):
        return moves.in_order([product(a, weights, out) for a in arrays], seqs)

    document = document_ids(doc_lengths, jnp.arange(length, dtype=jnp.int32))
    doc_before = [jnp.pad(document, ((0, 0), (by, 0)), constant_values=-1)[:, :length] for by in range(taps)]
    doc_after = [jnp.pad(document, ((0, 0), (0, by)), constant_values=-1)[:, by:] for by in range(taps)]
    joined = [(b == document)[:, :, None] for b in doc_before]
    joins = [(a == document)[:, :, None] for a in doc_after]

    x_part = to_channels(normed, proj_x, dot, bf16)
    x_wide = x_part.astype(f32)
    conv_pre = conv_shift + x_wide * conv_taps[taps - 1]
    for by in range(1, taps):
        conv_pre = conv_pre + jnp.where(joined[by], earlier(x_wide, by), 0.0) * conv_taps[taps - 1 - by]
    values = jax.nn.silu(conv_pre).astype(bf16)
    value_rows = values.reshape(tokens, inner)
    projected = moves.total(dot(value_rows, proj_select))
    step_low = projected[:, :rank].astype(bf16)
    state_vectors = projected[:, rank:].reshape(seqs, length, 2 * states)
    step_pre = dot(step_low, proj_step).reshape(seqs, length, inner) + bias_step
    step = jax.nn.softplus(step_pre)
    values_wide = values.astype(f32)
    drive = step * values_wide
    step_keep = jnp.where(joined[1], step, BREAK)

    rate = decay_rate.T.reshape(states, inner // LANE, LANE).swapaxes(0, 1)
    hot, sel = constants()
    spread_in = by_eights(state_vectors)
    scanned, starts = scan_forward(step_keep, drive, spread_in, rate * LOG2E, hot, sel)

    z_part = to_channels(normed, proj_z, dot, bf16)
    grad_gated = to_channels(grad_all, proj_out, dot_t, f32)
    z_wide = z_part.astype(f32)
    z_sigmoid = jax.nn.sigmoid(z_wide)
    z_gate = z_wide * z_sigmoid
    ssm_out = scanned + skip * values_wide
    gated = moves.own_first((ssm_out * z_gate).astype(bf16))
    grad_ssm = grad_gated * z_gate
    grad_z = moves.own_first(
        (grad_gated * ssm_out * z_sigmoid * (1.0 + z_wide * (1.0 - z_sigmoid))).astype(bf16)
    )
    grad_skip = jnp.sum(grad_ssm * values_wide, axis=(0, 1))

    def weight_grad(lefts, rights):
        return sum(t_dot(a, b) for a, b in zip(lefts, rights)).astype(bf16)

    grad_in_z = line_scatter(weight_grad(normed, grad_z).reshape(shards, depth, inner), "shards")
    grad_out_proj = weight_grad(gated, grad_all).reshape(shards, part, model_width)
    grad_out_proj = line_scatter(after(grad_out_proj, grad_in_z), "shards")

    def chosen(weights, blocks, axis):
        return jnp.concatenate(
            [lax.dynamic_slice_in_dim(weights, b * share_width, share_width, axis) for b in blocks], axis
        )

    out_share = moves.share(lambda blocks: [dot(g, chosen(proj_out, blocks, 1), bf16) for g in gated])
    own_columns = tensor * share_width
    input_share = lax.dynamic_slice_in_dim(block_input, own_columns, share_width, 2).astype(f32)
    block_output = (input_share + out_share.reshape(input_share.shape)).astype(bf16)

    sums, pulls, grad_vectors, grad_decay = scan_backward(
        step_keep, drive, grad_ssm, spread_in, rate * LOG2E, rate, hot, sel, starts
    )
    grad_decay_log = grad_decay.T * decay_rate
    grad_step = pulls + values_wide * sums
    grad_step_pre = (grad_step * jax.nn.sigmoid(step_pre)).astype(bf16).reshape(tokens, inner)
    grad_step_bias = jnp.sum(grad_step_pre.astype(f32), axis=0)
    grad_step_proj = t_dot(step_low, grad_step_pre)
    grad_step_low = dot_t(grad_step_pre, proj_step)
    grad_projected = moves.total(
        jnp.concatenate([grad_step_low, grad_vectors.reshape(tokens, 2 * states)], axis=1)
    ).astype(bf16)
    grad_select = t_dot(value_rows, grad_projected)
    grad_values = dot_t(grad_projected, proj_select).reshape(seqs, length, inner) + step * sums + grad_ssm * skip
    conv_sigmoid = jax.nn.sigmoid(conv_pre)
    grad_conv = grad_values * conv_sigmoid * (1.0 + conv_pre * (1.0 - conv_sigmoid))
    grad_x = grad_conv * conv_taps[taps - 1]
    tap_grads = [jnp.sum(grad_conv * x_wide, axis=(0, 1))]
    for by in range(1, taps):
        grad_x = grad_x + jnp.where(joins[by], later(grad_conv, by), 0.0) * conv_taps[taps - 1 - by]
        tap_grads.insert(0, jnp.sum(jnp.where(joined[by], earlier(x_wide, by), 0.0) * grad_conv, axis=(0, 1)))
    grad_conv_bias = jnp.sum(grad_conv, axis=(0, 1))
    grad_x = moves.own_first(grad_x.astype(bf16))

    def normed_part(blocks):
        by_x, by_z = chosen(proj_x, blocks, 0), chosen(proj_z, blocks, 0)
        return [(dot_t(x, by_x) + dot_t(z, by_z)).astype(bf16) for x, z in zip(grad_x, grad_z)]

    grad_normed = moves.share(normed_part).reshape(seqs, piece, share_width)
    unit, inv_rms = normalised(block_input)
    unit_share = lax.dynamic_slice_in_dim(unit, own_columns, share_width, 2)
    weighted = grad_normed * lax.dynamic_slice_in_dim(gain, own_columns, share_width, 0)
    row_dots = moves.row_total(jnp.sum(unit_share * weighted, axis=-1))[:, :, None]
    grad_share = lax.dynamic_slice_in_dim(output_grad, own_columns, share_width, 2).astype(f32)
    input_grad = grad_share + inv_rms * (weighted - unit_share * (row_dots / model_width))

    small = jnp.concatenate(
        [
            grad_select,
            jnp.stack(tap_grads, axis=1),
            grad_decay_log,
            grad_conv_bias[:, None],
            grad_step_bias[:, None],
            grad_skip[:, None],
        ],
        axis=1,
    ).astype(bf16)
    small = jnp.pad(small, ((0, 0), (0, 2 * LANE - small.shape[1])))
    late = jnp.concatenate(
        [
            weight_grad(normed, grad_x).reshape(shards, depth, inner),
            grad_step_proj.astype(bf16).reshape(shards, -1, inner),
            small.reshape(shards, -1, inner),
        ],
        axis=1,
    )
    late = line_scatter(late, "shards")
    grad_in_x = late[:depth]
    gain_part = jnp.sum(in_x.astype(f32) * grad_in_x, axis=1) + jnp.sum(in_z.astype(f32) * grad_in_z, axis=1)
    grad_gain = moves.vector_total(gain_part) / norm_gain.astype(f32)

    def columns_of(pair):
        pair = pair.astype(f32).reshape(pair.shape[:-1] + (shards, part))
        return jnp.moveaxis(pair, 0, -2).reshape(pair.shape[1], -1)

    grad_in_z = moves.both(grad_in_z.astype(bf16))
    grad_out_proj = moves.both(grad_out_proj.astype(bf16))
    late = moves.both(late.astype(bf16))
    grad_in = jnp.stack([columns_of(late[:, :depth]), columns_of(grad_in_z)], axis=1)
    grad_step_proj = columns_of(late[:, depth : depth + step_proj.shape[0]])
    small = late[:, depth + step_proj.shape[0] :].reshape(contexts * part, 2 * LANE).astype(f32)
    at = selected + taps + states
    return (
        block_output,
        input_grad,
        grad_gain,
        grad_in,
        small[:, selected : selected + taps],
        small[:, at],
        small[:, :selected],
        grad_step_proj,
        small[:, at + 1],
        small[:, selected + taps : at],
        small[:, at + 2],
        grad_out_proj.reshape(contexts * part, model_width).astype(f32),
    )


def solution(mesh):
    placed = (
        P("shards", "context", None),
        P("shards", "context", None),
        P("shards", None),
        P("shards"),
        P("shards", None, "tensor"),
        P(("tensor", "shards"), None),
        P(("tensor", "shards")),
        P(("tensor", "shards"), None),
        P("shards", "tensor"),
        P(("tensor", "shards")),
        P(("tensor", "shards"), None),
        P(("tensor", "shards")),
        P(("tensor", "shards"), None),
    )
    return jax.shard_map(
        on_device,
        mesh=mesh,
        in_specs=placed,
        out_specs=(
            P("shards", "context", "tensor"),
            P("shards", "context", "tensor"),
            P("shards"),
            P("shards", None, "tensor"),
            P(("tensor", "shards"), None),
            P(("tensor", "shards")),
            P(("tensor", "shards"), None),
            P("shards", "tensor"),
            P(("tensor", "shards")),
            P(("tensor", "shards"), None),
            P(("tensor", "shards")),
            P(("tensor", "shards"), None),
        ),
        check_vma=False,
    )
```

time: 2640 us -> 664 us (0.25)
  waiting for transfers between devices: 835 us -> 129 us
  other arithmetic: 584 us -> 116 us
  matrix products: 482 us -> 96.7 us
  local copies, waits for them, and re-layouts: 478 us -> 129 us
  blocking collectives: 210 us -> 0 us
  Pallas kernels: 0 us -> 110 us
  starting transfers between devices: 5.32 us -> 68.3 us
    reduce_scatter x6 -> x0, waiting for transfers between devices: 417 us -> none  [the longest x1 233 us: on_device(): lax.psum_scatter(gradients[1], ('shards', 'context'), scatter_dimension=0...]
    dot_general x76 -> x30, matrix products: 482 us -> 96.7 us  [the longest x12 36.4 us: dot_t(): lax.dot_general(a, b, (((1,), (1,)), ((), ())), preferred_element_type=f32)]
    mul x89 -> x2, other arithmetic: 284 us -> 8.18 us  [the longest x1 5.56 us: normalised(): return (wide * inv_rms, inv_rms)]
    mul x106 -> x1, local copies, waits for them, and re-layouts: 216 us -> 0.6 us  [on_device(): rate * LOG2E]
    all_gather x4 -> x0, waiting for transfers between devices: 206 us -> none  [the longest x1 116 us: on_device(): lax.all_gather(input_proj, 'shards', axis=0, tiled=True)]
    all_gather x20 -> x0, blocking collectives: 156 us -> none  [the longest x1 15.6 us: on_device(): lax.all_gather(conv_weight, 'shards', axis=0, tiled=True)]
    psum x2 -> x0, waiting for transfers between devices: 149 us -> none  [the longest x1 149 us: on_device(): grad_normed = lax.psum(partial_normed, 'tensor')]
    reduce_sum x29 -> x9, other arithmetic: 175 us -> 27.1 us  [the longest x1 7.38 us: on_device(): grad_skip = jnp.sum(grad_ssm * values_wide, axis=(0, 1))]
  transfers between devices with their start and end apart: 15 -> 51, of which waited for: 11 -> 19; matrix products, arithmetic and copies ran while one was open for 53% -> 37% of each run, Pallas kernels for 0% -> 12%
where the time goes in v1:
time: 664 us; the launch traced here: 653 us
  local copies, waits for them, and re-layouts  129 us (19%)
  waiting for transfers between devices  129 us (19%)
  other arithmetic  116 us (17%)
  Pallas kernels  110 us (17%)
  matrix products  96.7 us (15%)
  starting transfers between devices  68.3 us (10%)
    pallas_call x1, Pallas kernels, scan_backward(): pl.pallas_call(functools.partial(bwd_kernel, S, G, L), grid=(nb,), in_spe...  77.9 us
    ppermute x15, waiting for transfers between devices, across(): return lax.ppermute(array, 'context', [(0, 1), (1, 0)])  55.9 us
    ppermute x3, waiting for transfers between devices, line_gather(): lax.ppermute(left, axis, [(i, i - 1) for i in range(1, count - step + 1)])  39.3 us
    dot_general x12, matrix products, dot_t(): lax.dot_general(a, b, (((1,), (1,)), ((), ())), preferred_element_type=f32)  36.4 us
    pallas_call x1, Pallas kernels, scan_forward(): pl.pallas_call(functools.partial(fwd_kernel, S, G, L), grid=(T // L,), in...  31.9 us
    dot_general x10, matrix products, dot(): return jnp.dot(a, b, preferred_element_type=f32).astype(out)  31.1 us
    unnamed x274, local copies, waits for them, and re-layouts  30.9 us
    dot_general x8, matrix products, t_dot(): lax.dot_general(a, b, (((0,), (0,)), ((), ())), preferred_element_type=f32)  29.1 us
  transfers between devices with their start and end apart: 51, of which 19 were waited for; matrix products, arithmetic and copies ran while one was open for 37% of the time, Pallas kernels for 12%

profile of v1, /device:TPU:0, one launch (start us, length us, event | category | flops | bytes accessed | tf_op | source)
XLA Modules:
  0.0 653.3 jit_solution(11523708688005751762)
XLA Ops:
  5.4 6.5 fusion.115
  11.9 4.3 constant_dynamic-slice_fusion.21
  19.8 5.8 collective-permute-start
  35.3 5.9 all-to-all-start
  66.1 24.5 %collective-permute-done.4 = bf16[609,512]{1,0:T(8,128)(2,1)} collective-permute-done((bf16[609,512]{1,0:T(8,128)(2,1)}, bf16[609,512]{1,0:T(8,128)(2,1)}, u32[]{:S(2)}, u32[]{:S(2)}) %collective-permute-start.4) | collective-permute-done | bytes 623648 | tf_op jit(solution)/shard_map/ppermute | solution.py:177
  102.7 14.8 %collective-permute-done.5 = bf16[609,512]{1,0:T(8,128)(2,1)S(1)} collective-permute-done((bf16[609,512]{1,0:T(8,128)(2,1)}, bf16[609,512]{1,0:T(8,128)(2,1)S(1)}, u32[]{:S(2)}, u32[]{:S(2)}) %collective-permute-start.5) | collective-permute-done | bytes 623648 | tf_op jit(solution)/shard_map/ppermute | solution.py:177
  120.9 3.5 constant_dynamic-slice_fusion.1
  125.0 5.6 convert_multiply_fusion.2
  139.1 6.4 all-to-all-start.1
  145.5 5.4 convolution_convert_fusion.4
  156.1 22.7 %collective-permute-done.24 = bf16[512,2048]{1,0:T(8,128)(2,1)} collective-permute-done((bf16[512,2048]{1,0:T(8,128)(2,1)}, bf16[512,2048]{1,0:T(8,128)(2,1)}, u32[]{:S(2)}, u32[]{:S(2)}) %collective-permute-start.24) | collective-permute-done | bytes 2097184 | tf_op jit(solution)/shard_map/ppermute | solution.py:199
  181.2 5.5 broadcast_select_fusion.1
  192.4 6.5 convolution_bitcast_fusion
  201.1 3.2 constant_dynamic-update-slice_fusion
  204.2 5.4 broadcast_select_fusion.9
  209.7 7.4 %fusion.29 = (bf16[512]{0:T(512)(128)(2,1)S(1)}, bf16[2,1024,512]{2,1,0:T(8,128)(2,1)S(1)}, f32[2,1024,512]{2,1,0:T(8,128)}) fusion(bf16[2,512,512]{2,1,0:T(8,128)(2,1)S(1)} %bitcast.283, bf16[2,512,512]{2,1,0:T(8,128)(2,1)S(1)} %bitcast.278, f32[2,512,512]{2,1,0:T(8,128)S(1)} %get-tuple-element.107, f32[2,512,512]{2,1,0:T(8,128)S(1)} %get-tuple-element.106, ...), kind=kLoop, calls=%fused_computation.54 | loop fusion | flops 30408192 | bytes 16794624 | tf_op jit(solution)/shard_map/reduce_sum | solution.py:482
  245.2 3.7 copy.116
  248.9 5.8 reduce-precision_convert_fusion.1
  258.5 5.6 fusion.24
  265.7 3.4 maximum_maximum_fusion.bct_ref
  269.1 31.9 %shard_map.220 = (f32[2,128,8,512]{3,2,1,0:T(8,128)}, f32[16,128,128]{2,1,0:T(8,128)}) custom-call(f32[2,128,8,512]{3,2,1,0:T(8,128)} %get-tuple-element.102.se_ref, f32[2,128,8,512]{3,2,1,0:T(8,128)} %get-tuple-element.101.su_ref, bf16[2,128,32,128]{3,2,1,0:T(8,128)(2,1)} %maximum_maximum_fusion.bct_ref, f32[4,16,128]{2,1,0:T(8,128)} %bitcast.351, ...), custom_call_target="tpu_custom_call" | custom-call | tf_op jit(solution)/shard_map/pallas_call | solution.py:143
  301.0 4.2 fusion.35
  308.1 4.4 fusion.127
  318.0 6.3 fusion.37
  324.2 4.9 all-to-all-start.3
  329.1 77.9 %shard_map.221 = (f32[2,128,8,512]{3,2,1,0:T(8,128)}, f32[2,128,8,512]{3,2,1,0:T(8,128)}, f32[2,128,2,128]{3,2,1,0:T(2,128)}, f32[16,512]{1,0:T(8,128)}) custom-call(f32[2,128,8,512]{3,2,1,0:T(8,128)} %get-tuple-element.102.se_ref, f32[2,128,8,512]{3,2,1,0:T(8,128)} %get-tuple-element.101.su_ref, f32[2,128,8,512]{3,2,1,0:T(8,128)} %fusion.22.ds_ref, ...), custom_call_target="tpu_custom_call" | custom-call | tf_op jit(solution)/shard_map/pallas_call | solution.py:155
  408.8 3.7 copy.122
  412.5 3.3 reshape_reshape.7
  418.1 5.6 fusion.112
  425.9 6.1 fusion.36
  452.8 11.5 %fusion.111 = (bf16[512]{0:T(512)(128)(2,1)S(1)}, bf16[512]{0:T(512)(128)(2,1)S(1)}, bf16[512]{0:T(512)(128)(2,1)S(1)}, bf16[512]{0:T(512)(128)(2,1)S(1)}, bf16[...) fusion(bf16[2,512,512]{2,1,0:T(8,128)(2,1)} %bitcast.315, bf16[2,512,512]{2,1,0:T(8,128)(2,1)} %bitcast.313, ...), kind=kLoop, calls=%fused_computation.352 | loop fusion | flops 47183360 | bytes 33569792 | tf_op jit(solution)/shard_map/reduce_sum | solution.py:522
  464.5 3.4 fusion.14
  470.5 6.5 fusion.38
  485.6 3.3 fusion.54
  492.1 4.5 fusion.55
  499.0 4.9 fusion.121
  514.1 4.8 all-to-all-start.2
  518.9 4.6 fusion.122
  528.1 10.8 %collective-permute-done.22 = bf16[512,1024]{1,0:T(8,128)(2,1)} collective-permute-done((bf16[512,1024]{1,0:T(8,128)(2,1)}, bf16[512,1024]{1,0:T(8,128)(2,1)}, u32[]{:S(2)}, u32[]{:S(2)}) %collective-permute-start.22) | collective-permute-done | bytes 1048608 | tf_op jit(solution)/shard_map/ppermute | solution.py:199
  547.9 22.6 %collective-permute-done.23 = bf16[512,512]{1,0:T(8,128)(2,1)S(1)} collective-permute-done((bf16[512,512]{1,0:T(8,128)(2,1)S(1)}, bf16[512,512]{1,0:T(8,128)(2,1)S(1)}, u32[]{:S(2)}, u32[]{:S(2)}) %collective-permute-start.23) | collective-permute-done | bytes 524320 | tf_op jit(solution)/shard_map/ppermute | solution.py:205
  579.3 5.0 all-to-all-start.4
  584.4 3.3 add_convert_fusion.4
  587.7 6.6 %collective-permute-done.35 = bf16[512,512]{1,0:T(8,128)(2,1)} collective-permute-done((bf16[512,512]{1,0:T(8,128)(2,1)S(1)}, bf16[512,512]{1,0:T(8,128)(2,1)}, u32[]{:S(2)}, u32[]{:S(2)}) %collective-permute-start.35) | collective-permute-done | bytes 524320 | tf_op jit(solution)/shard_map/ppermute | solution.py:199
  614.7 3.7 multiply_add_fusion.1
  618.9 8.2 %collective-permute-done.43 = bf16[608,512]{1,0:T(8,128)(2,1)S(1)} collective-permute-done((bf16[608,512]{1,0:T(8,128)(2,1)S(1)}, bf16[608,512]{1,0:T(8,128)(2,1)S(1)}, u32[]{:S(2)}, u32[]{:S(2)}) %collective-permute-start.43) | collective-permute-done | bytes 622624 | tf_op jit(solution)/shard_map/ppermute | solution.py:199
  627.2 3.9 all-to-all-done.4
  638.2 3.5 maximum_convert_fusion.1
  641.7 7.4 %copy.133 = f32[512,2,1024]{2,1,0:T(2,128)} copy(f32[512,2,1024]{0,2,1:T(8,128)} %maximum_convert_fusion.1) | data formatting | bytes 8388608
  (530 shorter events, 231.4 us)
Async XLA Ops:
  19.8 30.3 %collective-permute-start = (bf16[609,512]{1,0:T(8,128)(2,1)}, bf16[609,512]{1,0:T(8,128)(2,1)}, u32[]{:S(2)}, u32[]{:S(2)}) collective-permute-start(bf16[609,512]{1,0:T(8,128)(2,1)} %pad_maximum_fusion.29), channel_id=1, source_target_pairs={{0,8},{8,16},{16,24},{1,9},{9,17},{17,25},{2,10},{10,18},{18,26},{... | collective-permute-start | bytes 1870856 | tf_op jit(solution)/shard_map/ppermute | solution.py:176
  25.5 26.1 %collective-permute-start.3 = (bf16[609,512]{1,0:T(8,128)(2,1)}, bf16[609,512]{1,0:T(8,128)(2,1)}, u32[]{:S(2)}, u32[]{:S(2)}) collective-permute-start(bf16[609,512]{1,0:T(8,128)(2,1)} %pad_maximum_fusion.29), channel_id=1, source_target_pairs={{8,0},{16,8},{24,16},{9,1},{17,9},{25,17},{10,2},{18,10},{26,18},{... | collective-permute-start | bytes 1870856 | tf_op jit(solution)/shard_map/ppermute | solution.py:177
  28.9 24.0 %collective-permute-start.6 = (bf16[176,2048]{1,0:T(8,128)(2,1)}, bf16[176,2048]{1,0:T(8,128)(2,1)}, u32[]{:S(2)}, u32[]{:S(2)}) collective-permute-start(bf16[176,2048]{1,0:T(8,128)(2,1)} %constant_dynamic-slice_fusion.23), channel_id=1, source_target_pairs={{0,4},{4,0},{1,5},{5,1},{2,6},{6,2},{3,7},{7,3},{8,12},{12,8},{9,1... | collective-permute-start | bytes 2162696 | tf_op jit(solution)/shard_map/ppermute | solution.py:199
  32.4 28.5 %collective-permute-start.8 = (bf16[160,2048]{1,0:T(8,128)(2,1)}, bf16[160,2048]{1,0:T(8,128)(2,1)}, u32[]{:S(2)}, u32[]{:S(2)}) collective-permute-start(bf16[160,2048]{1,0:T(8,128)(2,1)} %constant_dynamic-slice_fusion.22), channel_id=1, source_target_pairs={{0,4},{4,0},{1,5},{5,1},{2,6},{6,2},{3,7},{7,3},{8,12},{12,8},{9,1... | collective-permute-start | bytes 1966088 | tf_op jit(solution)/shard_map/ppermute | solution.py:199
  35.3 102.1 %all-to-all-start = ((bf16[4,512,512]{2,1,0:T(8,128)(2,1)}), bf16[4,512,512]{2,1,0:T(8,128)(2,1)S(1)}, u32[]{:S(2)}, u32[]{:S(2)}) async-start(bf16[4,512,512]{2,1,0:T(8,128)(2,1)} %broadcast_in_dim.125), calls=%async_computation | async-start | bytes 4194304 | tf_op jit(solution)/shard_map/all_to_all | solution.py:185
  50.1 15.3 %collective-permute-start.1 = (bf16[609,512]{1,0:T(8,128)(2,1)}, bf16[609,512]{1,0:T(8,128)(2,1)}, u32[]{:S(2)}, u32[]{:S(2)}) collective-permute-start(bf16[609,512]{1,0:T(8,128)(2,1)} %collective-permute-done), channel_id=1, source_target_pairs={{8,16},{16,24},{9,17},{17,25},{10,18},{18,26},{11,19},{19,27},{12,... | collective-permute-start | bytes 1870856 | tf_op jit(solution)/shard_map/ppermute | solution.py:176
  51.6 39.0 %collective-permute-start.4 = (bf16[609,512]{1,0:T(8,128)(2,1)}, bf16[609,512]{1,0:T(8,128)(2,1)}, u32[]{:S(2)}, u32[]{:S(2)}) collective-permute-start(bf16[609,512]{1,0:T(8,128)(2,1)} %collective-permute-done.3), channel_id=1, source_target_pairs={{8,0},{16,8},{9,1},{17,9},{10,2},{18,10},{11,3},{19,11},{12,4},{20... | collective-permute-start | bytes 1870856 | tf_op jit(solution)/shard_map/ppermute | solution.py:177
  52.9 39.1 %collective-permute-start.7 = (bf16[176,2048]{1,0:T(8,128)(2,1)}, bf16[176,2048]{1,0:T(8,128)(2,1)S(1)}, u32[]{:S(2)}, u32[]{:S(2)}) collective-permute-start(bf16[176,2048]{1,0:T(8,128)(2,1)} %collective-permute-done.6), channel_id=1, source_target_pairs={{0,1},{1,0},{2,3},{3,2},{4,5},{5,4},{6,7},{7,6},{8,9},{9,8},{10,11... | collective-permute-start | bytes 2162696 | tf_op jit(solution)/shard_map/ppermute | solution.py:202
  53.0 38.9 %collective-permute-start.10 = (bf16[176,2048]{1,0:T(8,128)(2,1)}, bf16[176,2048]{1,0:T(8,128)(2,1)}, u32[]{:S(2)}, u32[]{:S(2)}) collective-permute-start(bf16[176,2048]{1,0:T(8,128)(2,1)} %collective-permute-done.6), channel_id=1, source_target_pairs={{0,2},{2,0},{1,3},{3,1},{4,6},{6,4},{5,7},{7,5},{8,10},{10,8},{9,1... | collective-permute-start | bytes 2162696 | tf_op jit(solution)/shard_map/ppermute | solution.py:205
  60.8 34.2 %collective-permute-start.9 = (bf16[160,2048]{1,0:T(8,128)(2,1)}, bf16[160,2048]{1,0:T(8,128)(2,1)S(1)}, u32[]{:S(2)}, u32[]{:S(2)}) collective-permute-start(bf16[160,2048]{1,0:T(8,128)(2,1)} %collective-permute-done.8), channel_id=1, source_target_pairs={{0,1},{1,0},{2,3},{3,2},{4,5},{5,4},{6,7},{7,6},{8,9},{9,8},{10,11... | collective-permute-start | bytes 1966088 | tf_op jit(solution)/shard_map/ppermute | solution.py:202
  65.4 32.6 %collective-permute-start.2 = (bf16[609,512]{1,0:T(8,128)(2,1)}, bf16[609,512]{1,0:T(8,128)(2,1)S(1)}, u32[]{:S(2)}, u32[]{:S(2)}) collective-permute-start(bf16[609,512]{1,0:T(8,128)(2,1)} %collective-permute-done.1), channel_id=1, source_target_pairs={{16,24},{17,25},{18,26},{19,27},{20,28},{21,29},{22,30},{23,31}} | collective-permute-start | bytes 1870856 | tf_op jit(solution)/shard_map/ppermute | solution.py:176
  90.6 26.8 %collective-permute-start.5 = (bf16[609,512]{1,0:T(8,128)(2,1)}, bf16[609,512]{1,0:T(8,128)(2,1)S(1)}, u32[]{:S(2)}, u32[]{:S(2)}) collective-permute-start(bf16[609,512]{1,0:T(8,128)(2,1)} %collective-permute-done.4), channel_id=1, source_target_pairs={{8,0},{9,1},{10,2},{11,3},{12,4},{13,5},{14,6},{15,7}} | collective-permute-start | bytes 1870856 | tf_op jit(solution)/shard_map/ppermute | solution.py:177
  91.9 38.7 %collective-permute-start.11 = (bf16[176,2048]{1,0:T(8,128)(2,1)}, bf16[176,2048]{1,0:T(8,128)(2,1)}, u32[]{:S(2)}, u32[]{:S(2)}) collective-permute-start(bf16[176,2048]{1,0:T(8,128)(2,1)} %collective-permute-done.10), channel_id=1, source_target_pairs={{0,1},{1,0},{2,3},{3,2},{4,5},{5,4},{6,7},{7,6},{8,9},{9,8},{10,11... | collective-permute-start | bytes 2162696 | tf_op jit(solution)/shard_map/ppermute | solution.py:202
  132.8 46.1 %collective-permute-start.24 = (bf16[512,2048]{1,0:T(8,128)(2,1)}, bf16[512,2048]{1,0:T(8,128)(2,1)}, u32[]{:S(2)}, u32[]{:S(2)}) collective-permute-start(bf16[512,2048]{1,0:T(8,128)(2,1)} %constant_dynamic-slice_fusion.12), channel_id=1, source_target_pairs={{0,4},{4,0},{1,5},{5,1},{2,6},{6,2},{3,7},{7,3},{8,12},{12,8},{9,1... | collective-permute-start | bytes 6291464 | tf_op jit(solution)/shard_map/ppermute | solution.py:199
  139.1 53.3 %all-to-all-start.1 = ((bf16[4,128,2048]{2,1,0:T(8,128)(2,1)}), bf16[4,128,2048]{2,1,0:T(8,128)(2,1)}, u32[]{:S(2)}, u32[]{:S(2)}) async-start(bf16[4,128,2048]{2,1,0:T(8,128)(2,1)} %broadcast_in_dim.126), calls=%async_computation.1 | async-start | bytes 4194304 | tf_op jit(solution)/shard_map/all_to_all | solution.py:185
  178.8 22.2 %collective-permute-start.25 = (bf16[512,2048]{1,0:T(8,128)(2,1)}, bf16[512,2048]{1,0:T(8,128)(2,1)}, u32[]{:S(2)}, u32[]{:S(2)}) collective-permute-start(bf16[512,2048]{1,0:T(8,128)(2,1)} %collective-permute-done.24), channel_id=1, source_target_pairs={{0,1},{1,0},{2,3},{3,2},{4,5},{5,4},{6,7},{7,6},{8,9},{9,8},{10,11... | collective-permute-start | bytes 6291464 | tf_op jit(solution)/shard_map/ppermute | solution.py:202
  218.0 5.5 collective-permute-start.12
  223.7 6.3 collective-permute-start.13
  225.3 6.0 collective-permute-start.15
  231.4 5.5 collective-permute-start.14
  232.9 5.3 collective-permute-start.16
  324.2 189.8 %all-to-all-start.3 = ((bf16[4,512,512]{2,1,0:T(8,128)(2,1)}), bf16[4,512,512]{2,1,0:T(8,128)(2,1)}, u32[]{:S(2)}, u32[]{:S(2)}) async-start(bf16[4,512,512]{2,1,0:T(8,128)(2,1)} %bitcast.333), calls=%async_computation.3 | async-start | bytes 4194304 | tf_op jit(solution)/shard_map/all_to_all | solution.py:189
  424.6 7.9 %collective-permute-start.26 = (bf16[1024,160]{0,1:T(8,128)(2,1)S(1)}, bf16[1024,160]{0,1:T(8,128)(2,1)S(1)}, u32[]{:S(2)}, u32[]{:S(2)}) collective-permute-start(bf16[1024,160]{0,1:T(8,128)(2,1)S(1)} %fusion.59), channel_id=1, source_target_pairs={{0,1},{1,0},{2,3},{3,2},{4,5},{5,4},{6,7},{7,6},{8,9},{9,8},{10,11... | collective-permute-start | bytes 983048 | tf_op jit(solution)/shard_map/ppermute | solution.py:202
  432.6 6.6 %collective-permute-start.27 = (bf16[512,160]{0,1:T(8,128)(2,1)S(1)}, bf16[512,160]{0,1:T(8,128)(2,1)S(1)}, u32[]{:S(2)}, u32[]{:S(2)}) collective-permute-start(bf16[512,160]{0,1:T(8,128)(2,1)S(1)} %get-tuple-element.156), channel_id=1, source_target_pairs={{0,2},{2,0},{1,3},{3,1},{4,6},{6,4},{5,7},{7,5},{8,10},{10,8},{9,1... | collective-permute-start | bytes 491528 | tf_op jit(solution)/shard_map/ppermute | solution.py:205
  433.2 6.3 collective-permute-start.29
  436.3 62.0 %collective-permute-start.19 = (bf16[1024,1024]{1,0:T(8,128)(2,1)}, bf16[1024,1024]{1,0:T(8,128)(2,1)}, u32[]{:S(2)}, u32[]{:S(2)}) collective-permute-start(bf16[1024,1024]{1,0:T(8,128)(2,1)} %convolution_convert_fusion), channel_id=1, source_target_pairs={{0,1},{1,0},{2,3},{3,2},{4,5},{5,4},{6,7},{7,6},{8,9},{9,8},{10,11... | collective-permute-start | bytes 6291464 | tf_op jit(solution)/shard_map/ppermute | solution.py:202
  439.5 5.6 collective-permute-start.28
  440.1 5.3 collective-permute-start.30
  445.6 3.7 collective-permute-start.31
  448.4 56.7 %collective-permute-start.18 = (bf16[1024,1024]{1,0:T(8,128)(2,1)}, bf16[1024,1024]{1,0:T(8,128)(2,1)}, u32[]{:S(2)}, u32[]{:S(2)}) collective-permute-start(bf16[1024,1024]{1,0:T(8,128)(2,1)} %convolution_convert_fusion.1), channel_id=1, source_target_pairs={{0,1},{1,0},{2,3},{3,2},{4,5},{5,4},{6,7},{7,6},{8,9},{9,8},{10,11... | collective-permute-start | bytes 6291464 | tf_op jit(solution)/shard_map/ppermute | solution.py:202
  481.2 37.7 %collective-permute-start.33 = (bf16[1024,1024]{1,0:T(8,128)(2,1)}, bf16[1024,1024]{1,0:T(8,128)(2,1)}, u32[]{:S(2)}, u32[]{:S(2)}) collective-permute-start(bf16[1024,1024]{1,0:T(8,128)(2,1)} %add_convert_fusion), channel_id=1, source_target_pairs={{0,1},{1,0},{2,3},{3,2},{4,5},{5,4},{6,7},{7,6},{8,9},{9,8},{10,11... | collective-permute-start | bytes 6291464 | tf_op jit(solution)/shard_map/ppermute | solution.py:202
  485.6 37.9 %collective-permute-start.32 = (bf16[1024,1024]{1,0:T(8,128)(2,1)}, bf16[1024,1024]{1,0:T(8,128)(2,1)}, u32[]{:S(2)}, u32[]{:S(2)}) collective-permute-start(bf16[1024,1024]{1,0:T(8,128)(2,1)} %add_convert_fusion.2), channel_id=1, source_target_pairs={{0,1},{1,0},{2,3},{3,2},{4,5},{5,4},{6,7},{7,6},{8,9},{9,8},{10,11... | collective-permute-start | bytes 6291464 | tf_op jit(solution)/shard_map/ppermute | solution.py:202
  511.1 30.2 %collective-permute-start.20 = (bf16[2,512,512]{2,1,0:T(8,128)(2,1)}, bf16[2,512,512]{2,1,0:T(8,128)(2,1)}, u32[]{:S(2)}, u32[]{:S(2)}) collective-permute-start(bf16[2,512,512]{2,1,0:T(8,128)(2,1)} %pad_maximum_fusion.7), channel_id=1, source_target_pairs={{0,2},{2,0},{1,3},{3,1},{4,6},{6,4},{5,7},{7,5},{8,10},{10,8},{9,1... | collective-permute-start | bytes 3145736 | tf_op jit(solution)/shard_map/ppermute | solution.py:205
  512.6 26.3 %collective-permute-start.22 = (bf16[512,1024]{1,0:T(8,128)(2,1)}, bf16[512,1024]{1,0:T(8,128)(2,1)}, u32[]{:S(2)}, u32[]{:S(2)}) collective-permute-start(bf16[512,1024]{1,0:T(8,128)(2,1)} %slice.328), channel_id=1, source_target_pairs={{0,4},{4,0},{1,5},{5,1},{2,6},{6,2},{3,7},{7,3},{8,12},{12,8},{9,1... | collective-permute-start | bytes 3145736 | tf_op jit(solution)/shard_map/ppermute | solution.py:199
  514.1 65.2 %all-to-all-start.2 = ((bf16[4,608,512]{2,1,0:T(8,128)(2,1)}), bf16[4,608,512]{2,1,0:T(8,128)(2,1)S(1)}, u32[]{:S(2)}, u32[]{:S(2)}) async-start(bf16[4,608,512]{2,1,0:T(8,128)(2,1)} %pad_maximum_fusion.1), calls=%async_computation.2 | async-start | bytes 4980736 | tf_op jit(solution)/shard_map/all_to_all | solution.py:189
  527.0 48.3 %collective-permute-start.34 = (bf16[2,512,512]{2,1,0:T(8,128)(2,1)S(1)}, bf16[2,512,512]{2,1,0:T(8,128)(2,1)S(1)}, u32[]{:S(2)}, u32[]{:S(2)}) collective-permute-start(bf16[2,512,512]{2,1,0:T(8,128)(2,1)S(1)} %pad_maximum_fusion.12), channel_id=1, source_target_pairs={{0,2},{2,0},{1,3},{3,1},{4,6},{6,4},{5,7},{7,5},{8,10},{10,8},{9,1... | collective-permute-start | bytes 3145736 | tf_op jit(solution)/shard_map/ppermute | solution.py:205
  527.5 49.5 %collective-permute-start.36 = (bf16[512,1024]{1,0:T(8,128)(2,1)S(1)}, bf16[512,1024]{1,0:T(8,128)(2,1)S(1)}, u32[]{:S(2)}, u32[]{:S(2)}) collective-permute-start(bf16[512,1024]{1,0:T(8,128)(2,1)S(1)} %slice.344), channel_id=1, source_target_pairs={{0,4},{4,0},{1,5},{5,1},{2,6},{6,2},{3,7},{7,3},{8,12},{12,8},{9,1... | collective-permute-start | bytes 3145736 | tf_op jit(solution)/shard_map/ppermute | solution.py:199
  540.7 29.8 %collective-permute-start.23 = (bf16[512,512]{1,0:T(8,128)(2,1)S(1)}, bf16[512,512]{1,0:T(8,128)(2,1)S(1)}, u32[]{:S(2)}, u32[]{:S(2)}) collective-permute-start(bf16[512,512]{1,0:T(8,128)(2,1)S(1)} %slice.545), channel_id=1, source_target_pairs={{0,2},{2,0},{1,3},{3,1},{4,6},{6,4},{5,7},{7,5},{8,10},{10,8},{9,1... | collective-permute-start | bytes 1572872 | tf_op jit(solution)/shard_map/ppermute | solution.py:205
  542.8 29.7 %collective-permute-start.21 = (bf16[512,512]{1,0:T(8,128)(2,1)S(1)}, bf16[512,512]{1,0:T(8,128)(2,1)S(1)}, u32[]{:S(2)}, u32[]{:S(2)}) collective-permute-start(bf16[512,512]{1,0:T(8,128)(2,1)S(1)} %fusion.50), channel_id=1, source_target_pairs={{0,4},{4,0},{1,5},{5,1},{2,6},{6,2},{3,7},{7,3},{8,12},{12,8},{9,1... | collective-permute-start | bytes 1572872 | tf_op jit(solution)/shard_map/ppermute | solution.py:199
  547.4 52.2 %collective-permute-start.44 = (bf16[512,512]{1,0:T(8,128)(2,1)}, bf16[512,512]{1,0:T(8,128)(2,1)}, u32[]{:S(2)}, u32[]{:S(2)}) collective-permute-start(bf16[512,512]{1,0:T(8,128)(2,1)} %get-tuple-element.146), channel_id=1, source_target_pairs={{0,4},{4,0},{1,5},{5,1},{2,6},{6,2},{3,7},{7,3},{8,12},{12,8},{9,1... | collective-permute-start | bytes 1572872 | tf_op jit(solution)/shard_map/ppermute | solution.py:199
  575.4 18.9 %collective-permute-start.35 = (bf16[512,512]{1,0:T(8,128)(2,1)S(1)}, bf16[512,512]{1,0:T(8,128)(2,1)}, u32[]{:S(2)}, u32[]{:S(2)}) collective-permute-start(bf16[512,512]{1,0:T(8,128)(2,1)S(1)} %fusion.48), channel_id=1, source_target_pairs={{0,4},{4,0},{1,5},{5,1},{2,6},{6,2},{3,7},{7,3},{8,12},{12,8},{9,1... | collective-permute-start | bytes 1572872 | tf_op jit(solution)/shard_map/ppermute | solution.py:199
  578.8 17.1 %collective-permute-start.37 = (bf16[512,512]{1,0:T(8,128)(2,1)}, bf16[512,512]{1,0:T(8,128)(2,1)}, u32[]{:S(2)}, u32[]{:S(2)}) collective-permute-start(bf16[512,512]{1,0:T(8,128)(2,1)} %slice.544), channel_id=1, source_target_pairs={{0,2},{2,0},{1,3},{3,1},{4,6},{6,4},{5,7},{7,5},{8,10},{10,8},{9,1... | collective-permute-start | bytes 1572872 | tf_op jit(solution)/shard_map/ppermute | solution.py:205
  579.3 51.8 %all-to-all-start.4 = ((bf16[4,128,2048]{2,1,0:T(8,128)(2,1)}), bf16[4,128,2048]{2,1,0:T(8,128)(2,1)}, u32[]{:S(2)}, u32[]{:S(2)}) async-start(bf16[4,128,2048]{2,1,0:T(8,128)(2,1)} %bitcast.309), calls=%async_computation.4 | async-start | bytes 4194304 | tf_op jit(solution)/shard_map/all_to_all | solution.py:189
  599.6 6.4 collective-permute-start.38
  606.0 6.0 collective-permute-start.39
  611.2 15.9 %collective-permute-start.43 = (bf16[608,512]{1,0:T(8,128)(2,1)S(1)}, bf16[608,512]{1,0:T(8,128)(2,1)S(1)}, u32[]{:S(2)}, u32[]{:S(2)}) collective-permute-start(bf16[608,512]{1,0:T(8,128)(2,1)S(1)} %convert_element_type.470), channel_id=1, source_target_pairs={{0,4},{4,0},{1,5},{5,1},{2,6},{6,2},{3,7},{7,3},{8,12},{12,8},{9,1... | collective-permute-start | bytes 1867784 | tf_op jit(solution)/shard_map/ppermute | solution.py:199
  613.2 5.2 collective-permute-start.42
  633.2 16.8 %collective-permute-start.45 = (bf16[128,2048]{1,0:T(8,128)(2,1)S(1)}, bf16[128,2048]{1,0:T(8,128)(2,1)}, u32[]{:S(2)}, u32[]{:S(2)}) collective-permute-start(bf16[128,2048]{1,0:T(8,128)(2,1)S(1)} %reduce_sum.166), channel_id=1, source_target_pairs={{0,4},{4,0},{1,5},{5,1},{2,6},{6,2},{3,7},{7,3},{8,12},{12,8},{9,1... | collective-permute-start | bytes 1572872 | tf_op jit(solution)/shard_map/ppermute | solution.py:199
  (130 other events, 1735.5 us)

commit v2 on v1

v2 whole, which is shorter than its diff:
```python
import functools

import jax
import jax.numpy as jnp
from jax import lax
from jax.experimental import pallas as pl
from jax.experimental.pallas import tpu as pltpu
from jax.sharding import PartitionSpec as P

EPS = 1e-05
LANE = 128
LOG2E = 1.4426950408889634
BREAK = 1e6
f32 = jnp.float32
bf16 = jnp.bfloat16


def row8(ref, s, i, k, g):
    return jnp.broadcast_to(ref[s, i, k : k + 1, g * LANE : (g + 1) * LANE], (8, LANE))


def mm(a, b):
    return jnp.dot(a, b, preferred_element_type=f32)


def mm_t(a, b):
    return lax.dot_general(a, b, (((1,), (1,)), ((), ())), preferred_element_type=f32)


def iota(shape, axis):
    return lax.broadcasted_iota(jnp.int32, shape, axis)


def cost(us):
    return pl.CostEstimate(flops=int(us * 1.15e8), bytes_accessed=int(us * 3.6e5), transcendentals=0)


PARAMS = pltpu.CompilerParams(vmem_limit_bytes=58 << 20)


def whole(*shape):
    return pl.BlockSpec(shape, lambda *_: (0,) * len(shape))


def rms(rows, gain):
    wide = rows.astype(f32)
    inv_rms = lax.rsqrt(jnp.mean(wide * wide, axis=-1, keepdims=True) + EPS)
    return (wide * inv_rms * gain).astype(bf16)


def joined_halves(first, second, place, gain=None):
    half, width = first.shape
    size = min(half, 128)
    count = half // size

    def kernel(place_ref, first_ref, second_ref, *rest):
        out_ref = rest[-1]
        this = (pl.program_id(0) // count) == place_ref[0]

        def put(ref):
            out_ref[...] = ref[...] if gain is None else rms(ref[...], rest[0][...])

        @pl.when(this)
        def _():
            put(first_ref)

        @pl.when(jnp.logical_not(this))
        def _():
            put(second_ref)

    def spec(which):
        def index(i, place):
            start = (place[0] ^ which) * count
            return (jnp.clip(i - start, 0, count - 1), 0)

        return pl.BlockSpec((size, width), index)

    extra = [] if gain is None else [gain.reshape(1, width)]
    return pl.pallas_call(
        kernel,
        grid_spec=pltpu.PrefetchScalarGridSpec(
            num_scalar_prefetch=1,
            grid=(2 * count,),
            in_specs=[spec(0), spec(1)] + [whole(1, width) for _ in extra],
            out_specs=pl.BlockSpec((size, width), lambda i, place: (i, 0)),
        ),
        out_shape=jax.ShapeDtypeStruct((2 * half, width), bf16),
        cost_estimate=cost(4),
        compiler_params=PARAMS,
    )(place, first, second, *extra)


def normalised_rows(rows, gain):
    count, width = rows.shape
    size = min(count, 256)

    def kernel(in_ref, gain_ref, out_ref, inv_ref):
        wide = in_ref[...].astype(f32)
        inv_rms = lax.rsqrt(jnp.mean(wide * wide, axis=-1, keepdims=True) + EPS)
        out_ref[...] = (wide * inv_rms * gain_ref[...]).astype(bf16)
        inv_ref[...] = jnp.broadcast_to(inv_rms, inv_ref.shape)

    by_rows = lambda w: pl.BlockSpec((size, w), lambda i: (i, 0))
    return pl.pallas_call(
        kernel,
        grid=(count // size,),
        in_specs=[by_rows(width), whole(1, width)],
        out_specs=[by_rows(width), by_rows(LANE)],
        out_shape=[jax.ShapeDtypeStruct(rows.shape, bf16), jax.ShapeDtypeStruct((count, LANE), f32)],
        cost_estimate=cost(4),
        compiler_params=PARAMS,
    )(rows, gain.reshape(1, width))


def unpacked(window, counts, place):
    slots = len(window)
    count = (slots + 1) // 2
    width = window[0].shape[1]
    starts = [sum(counts[:i]) for i in range(len(counts))]

    def kernel(place_ref, *refs):
        ins, outs = refs[:slots], refs[slots:]
        wanted = pl.program_id(0) + count - 1 - place_ref[0]
        for slot, ref in enumerate(ins):

            @pl.when(wanted == slot)
            def _(ref=ref):
                for out, start, rows in zip(outs, starts, counts):
                    out[0] = ref[start : start + rows]

    return pl.pallas_call(
        kernel,
        grid_spec=pltpu.PrefetchScalarGridSpec(
            num_scalar_prefetch=1,
            grid=(count,),
            in_specs=[whole(*window[0].shape) for _ in window],
            out_specs=[pl.BlockSpec((1, rows, width), lambda j, place: (j, 0, 0)) for rows in counts],
        ),
        out_shape=[jax.ShapeDtypeStruct((count, rows, width), bf16) for rows in counts],
        cost_estimate=cost(3),
        compiler_params=PARAMS,
    )(place, *window)


def products(lefts, more_lefts, right, more_right, blocks, width):
    n = len(lefts)
    count, inner = lefts[0].shape
    size = min(count, 512)

    def kernel(blocks_ref, *refs):
        a, b, (w, v), outs = refs[:n], refs[n : 2 * n], refs[2 * n : 2 * n + 2], refs[2 * n + 2 :]
        for i in range(n):
            outs[i][...] = (mm_t(a[i][...], w[...]) + mm_t(b[i][...], v[...])).astype(bf16)

    rows = pl.BlockSpec((size, inner), lambda j, i, blocks: (i, 0))
    weights = pl.BlockSpec((width, inner), lambda j, i, blocks: (blocks[j], 0))
    return pl.pallas_call(
        kernel,
        grid_spec=pltpu.PrefetchScalarGridSpec(
            num_scalar_prefetch=1,
            grid=(blocks.shape[0], count // size),
            in_specs=[rows] * (2 * n) + [weights] * 2,
            out_specs=[pl.BlockSpec((size, width), lambda j, i, blocks: (i, j))] * n,
        ),
        out_shape=[jax.ShapeDtypeStruct((count, width * blocks.shape[0]), bf16)] * n,
        cost_estimate=cost(5),
        compiler_params=PARAMS,
    )(blocks, *lefts, *more_lefts, right, more_right)


def interleaved(first, second, depth, part):
    contexts, _, inner = first.shape
    shards = inner // part
    size = 64

    def kernel(a_ref, b_ref, out_ref):
        for which, ref in enumerate((a_ref, b_ref)):
            columns = [
                ref[c, :, s * part : (s + 1) * part].astype(f32) for s in range(shards) for c in range(contexts)
            ]
            out_ref[:, which, :] = jnp.concatenate(columns, axis=1)

    return pl.pallas_call(
        kernel,
        grid=(depth // size,),
        in_specs=[pl.BlockSpec((contexts, size, inner), lambda i: (0, i, 0))] * 2,
        out_specs=pl.BlockSpec((size, 2, contexts * inner), lambda i: (i, 0, 0)),
        out_shape=jax.ShapeDtypeStruct((depth, 2, contexts * inner), f32),
        cost_estimate=cost(5),
        compiler_params=PARAMS,
    )(first, second)


class Rows:
    def __init__(self, seqs, length, arrays, size, reverse=False):
        self.pieces = arrays
        self.size = size
        self.count = length // size
        self.per = self.count // arrays
        self.grid = (seqs, self.count)
        self.reverse = reverse

    def at(self, i):
        return self.count - 1 - i if self.reverse else i

    def spec(self, which, width):
        def index(s, i, place):
            low = (place[0] ^ which) * self.per
            return (s * self.per + jnp.clip(self.at(i) - low, 0, self.per - 1), 0)

        return pl.BlockSpec((self.size, width), index)

    def is_turn(self, which, place_ref):
        return (self.at(pl.program_id(1)) // self.per) == (place_ref[0] ^ which)

    def block(self, width):
        return pl.BlockSpec((1, self.size, width), lambda s, i, place: (s, self.at(i), 0))

    def packed(self, rows):
        return pl.BlockSpec((1, self.size // LANE, rows, LANE), lambda s, i, place: (s, self.at(i), 0, 0))


def convolved(xs, masks_ref, vec_ref, size, taps):
    total = vec_ref[taps : taps + 1]
    for by in range(taps):
        term = xs[8 - by : 8 - by + size] * vec_ref[taps - 1 - by : taps - by]
        total = total + (term * masks_ref[0, :, by : by + 1] if by else term)
    return total


def convolve(normed, proj_x, vec, masks, select_low, select_state, place, taps):
    seqs, length = masks.shape[:2]
    width, inner = proj_x.shape
    size = min(256, length)
    rows = Rows(seqs, length, len(normed), size)
    packed = select_low.shape[1] + select_state.shape[0]

    def kernel(place_ref, *refs):
        ins, (w_ref, vec_ref, masks_ref, low_ref, state_ref, x_ref, u_ref, p_ref, xs) = (
            refs[: len(normed)],
            refs[len(normed) :],
        )
        fresh = pl.program_id(1) == 0

        @pl.when(fresh)
        def _():
            xs[0:8] = jnp.zeros((8, inner), f32)

        @pl.when(jnp.logical_not(fresh))
        def _():
            xs[0:8] = xs[size : size + 8]

        for which, ref in enumerate(ins):

            @pl.when(rows.is_turn(which, place_ref))
            def _(ref=ref):
                x = mm(ref[...], w_ref[...]).astype(bf16)
                x_ref[0] = x
                xs[8 : 8 + size] = x.astype(f32)

        pre = convolved(xs, masks_ref, vec_ref, size, taps)
        u = (pre / (1.0 + jnp.exp(-pre))).astype(bf16)
        u_ref[0] = u
        low = mm(u, low_ref[...])
        state = mm_t(state_ref[...], u)
        for j in range(size // LANE):
            p_ref[0, j, 0:LANE] = low[j * LANE : (j + 1) * LANE]
            p_ref[0, j, LANE:packed] = state[:, j * LANE : (j + 1) * LANE]

    return pl.pallas_call(
        kernel,
        grid_spec=pltpu.PrefetchScalarGridSpec(
            num_scalar_prefetch=1,
            grid=rows.grid,
            in_specs=[rows.spec(i, width) for i in range(len(normed))]
            + [whole(width, inner), whole(8, inner), rows.block(LANE), whole(*select_low.shape), whole(*select_state.shape)],
            out_specs=[rows.block(inner), rows.block(inner), rows.packed(packed)],
            scratch_shapes=[pltpu.VMEM((size + 8, inner), f32)],
        ),
        out_shape=[
            jax.ShapeDtypeStruct((seqs, length, inner), bf16),
            jax.ShapeDtypeStruct((seqs, length, inner), bf16),
            jax.ShapeDtypeStruct((seqs, length // LANE, packed, LANE), f32),
        ],
        cost_estimate=cost(9),
        compiler_params=PARAMS,
    )(place, *normed, proj_x, vec, masks, select_low, select_state)


def gates(normed, grads, proj_z, proj_out, ssm_out, place):
    seqs, length, inner = ssm_out.shape
    width = proj_z.shape[0]
    size = min(256, length)
    rows = Rows(seqs, length, len(normed), size)
    n = len(normed)

    def kernel(place_ref, *refs):
        a_refs, g_refs, (z_ref, o_ref, s_ref), outs = refs[:n], refs[n : 2 * n], refs[2 * n : 2 * n + 3], refs[2 * n + 3 :]
        for which in range(n):

            @pl.when(rows.is_turn(which, place_ref))
            def _(which=which):
                z = mm(a_refs[which][...], z_ref[...]).astype(bf16).astype(f32)
                grad = mm_t(g_refs[which][...], o_ref[...])
                ssm = s_ref[0]
                sigmoid = 1.0 / (1.0 + jnp.exp(-z))
                gate = z * sigmoid
                outs[which][...] = (ssm * gate).astype(bf16)
                outs[n + which][...] = (grad * ssm * sigmoid * (1.0 + z * (1.0 - sigmoid))).astype(bf16)
                outs[2 * n][0] = grad * gate

    total = seqs * length // n
    outs = pl.pallas_call(
        kernel,
        grid_spec=pltpu.PrefetchScalarGridSpec(
            num_scalar_prefetch=1,
            grid=rows.grid,
            in_specs=[rows.spec(i, width) for i in range(n)] * 2
            + [whole(width, inner), whole(inner, width), rows.block(inner)],
            out_specs=[rows.spec(i, inner) for i in range(n)] * 2 + [rows.block(inner)],
        ),
        out_shape=[jax.ShapeDtypeStruct((total, inner), bf16)] * (2 * n) + [jax.ShapeDtypeStruct((seqs, length, inner), f32)],
        cost_estimate=cost(14),
        compiler_params=PARAMS,
    )(place, *normed, *grads, proj_z, proj_out, ssm_out)
    return outs[:n], outs[n : 2 * n], outs[2 * n]


def convolve_back(packed, direct, x_part, vec, masks, select_low, select_state, place, n, taps):
    seqs, length, inner = x_part.shape
    size = min(256, length)
    rows = Rows(seqs, length, n, size, reverse=True)
    states = (packed.shape[2] - LANE) // 2

    def kernel(place_ref, p_ref, d_ref, x_ref, edge_ref, vec_ref, masks_ref, low_ref, state_ref, *rest):
        outs, (sum_ref, tok_ref, xs, ds) = rest[:n], rest[n:]
        fresh = pl.program_id(1) == 0

        @pl.when(jnp.logical_and(fresh, pl.program_id(0) == 0))
        def _():
            sum_ref[...] = jnp.zeros_like(sum_ref)

        @pl.when(fresh)
        def _():
            ds[size : size + 8] = jnp.zeros((8, inner), f32)

        @pl.when(jnp.logical_not(fresh))
        def _():
            ds[size : size + 8] = ds[0:8]

        copy = (iota((LANE, 16), 0) // 8 == iota((LANE, 16), 1)).astype(bf16)
        place_of = (iota((LANE, LANE), 1) // 16) == lax.rem(iota((LANE, LANE), 0), 8)
        by_state = lax.rem(iota((LANE, LANE), 0), 16)
        for j in range(size // LANE):
            at = slice(j * LANE, (j + 1) * LANE)
            tok_ref[0, at, 0:LANE] = p_ref[0, j, 0:LANE].astype(bf16)
            token = jnp.zeros((LANE, LANE), f32)
            for q in range(2):
                part = p_ref[0, j, LANE + q * states : LANE + (q + 1) * states].astype(bf16)
                spread = jnp.where(place_of, mm(copy, part), 0.0).astype(bf16)
                token = token + mm(spread, (by_state + q * states == iota((LANE, LANE), 1)).astype(bf16))
            tok_ref[0, at, LANE : 2 * LANE] = token.astype(bf16)
        xs[0:8] = edge_ref[0, 8:16].astype(f32)
        xs[8 : 8 + size] = x_ref[0].astype(f32)
        pre = convolved(xs, masks_ref, vec_ref, size, taps)
        sigmoid = 1.0 / (1.0 + jnp.exp(-pre))
        grad = mm_t(tok_ref[0, :, 0:LANE], low_ref[...]) + mm_t(tok_ref[0, :, LANE : 2 * LANE], state_ref[...]) + d_ref[0]
        grad = grad * sigmoid * (1.0 + pre * (1.0 - sigmoid))
        ds[0:size] = grad
        total = grad * vec_ref[taps - 1 : taps]
        sum_ref[taps : taps + 1] += jnp.sum(grad, axis=0, keepdims=True)
        sum_ref[taps - 1 : taps] += jnp.sum(grad * xs[8 : 8 + size], axis=0, keepdims=True)
        for by in range(1, taps):
            tap = taps - 1 - by
            total = total + ds[by : by + size] * masks_ref[0, :, taps + by : taps + by + 1] * vec_ref[tap : tap + 1]
            joint = grad * xs[8 - by : 8 - by + size] * masks_ref[0, :, by : by + 1]
            sum_ref[tap : tap + 1] += jnp.sum(joint, axis=0, keepdims=True)
        for which in range(n):

            @pl.when(rows.is_turn(which, place_ref))
            def _(which=which):
                outs[which][...] = total.astype(bf16)

    edge = pl.BlockSpec((1, 16, inner), lambda s, i, place: (s, jnp.maximum(rows.at(i) * (size // 16) - 1, 0), 0))
    outs = pl.pallas_call(
        kernel,
        grid_spec=pltpu.PrefetchScalarGridSpec(
            num_scalar_prefetch=1,
            grid=rows.grid,
            in_specs=[
                rows.packed(packed.shape[2]),
                rows.block(inner),
                rows.block(inner),
                edge,
                whole(8, inner),
                rows.block(LANE),
                whole(inner, LANE),
                whole(inner, LANE),
            ],
            out_specs=[rows.spec(i, inner) for i in range(n)] + [whole(8, inner), rows.block(2 * LANE)],
            scratch_shapes=[pltpu.VMEM((size + 8, inner), f32)] * 2,
        ),
        out_shape=[jax.ShapeDtypeStruct((seqs * length // n, inner), bf16)] * n
        + [jax.ShapeDtypeStruct((8, inner), f32), jax.ShapeDtypeStruct((seqs, length, 2 * LANE), bf16)],
        cost_estimate=cost(10),
        compiler_params=PARAMS,
    )(place, packed, direct, x_part, x_part, vec, masks, select_low, select_state)
    return outs[:n], outs[n], outs[n + 1]


def log_one_plus(v):
    small = v * (1.0 - v * (0.5 - v * (1.0 / 3.0 - v * 0.25)))
    return jnp.where(v < 0.01, small, jnp.log(1.0 + v))


def softplus(v):
    return jnp.maximum(v, 0.0) + log_one_plus(jnp.exp(-jnp.abs(v)))


def sigmoid_of_step(step):
    small = step * (1.0 - step * (0.5 - step * (1.0 / 6.0 - step * (1.0 / 24.0))))
    return jnp.where(step < 0.02, small, 1.0 - jnp.exp(-step))


def hot_rows():
    row, col = iota((LANE, 8 * LANE), 0), iota((LANE, 8 * LANE), 1)
    return ((lax.rem(row, 8) == col // LANE) & (row < 16)).astype(bf16)


def spread(state, hot, wide, s, blocks):
    high = state.astype(bf16).astype(f32)
    rest = state - high
    lane = iota(state.shape, 1)
    parts = []
    for i in range(blocks):
        a = pltpu.roll(high, (LANE - 8 * i) % LANE, 1)
        b = pltpu.roll(rest, (LANE + 8 - 8 * i) % LANE, 1)
        parts.append(jnp.where(lane < 8, a, b).astype(bf16))
    wide[s] = mm(jnp.concatenate(parts, axis=0), hot).reshape(blocks, state.shape[0], 8 * LANE)


def forward_kernel(
    S, G, p_ref, u_ref, masks_ref, proj_ref, vec_ref, rate_ref, hot_ref, y_ref, step_ref, start_ref, h_s, wide, w_s, se_s, su_s
):
    blocks = LANE // 8
    C = G * LANE

    @pl.when(pl.program_id(0) == 0)
    def _():
        h_s[...] = jnp.zeros_like(h_s)

    start_ref[0] = h_s[...]
    for s in range(S):
        step = softplus(mm(p_ref[s, 0, 0:LANE].astype(bf16), proj_ref[...]) + vec_ref[0:1])
        step_ref[s] = step
        u = u_ref[s].astype(f32)
        se_s[s] = jnp.where(masks_ref[s, :, 1:2] > 0.5, step, BREAK).reshape(blocks, 8, C)
        su_s[s] = (step * u).reshape(blocks, 8, C)
        spread(p_ref[s, 0, LANE : LANE + 32], hot_ref[...], wide, s, blocks)
    keys = [(s, g, j) for s in range(S) for g in range(G) for j in range(2)]

    def body(i, carry):
        hs = dict(zip(keys, carry))
        for k in range(8):
            for s in range(S):
                lanes = slice(k * LANE, (k + 1) * LANE)
                b = [wide[s, i, j * 8 : (j + 1) * 8, lanes] for j in range(2)]
                c = [wide[s, i, 16 + j * 8 : 16 + (j + 1) * 8, lanes] for j in range(2)]
                for g in range(G):
                    se, su = row8(se_s, s, i, k, g), row8(su_s, s, i, k, g)
                    prod = []
                    for j in range(2):
                        a = jnp.exp2(se * rate_ref[g, j * 8 : (j + 1) * 8])
                        hs[s, g, j] = a * hs[s, g, j] + su * b[j]
                        prod.append(c[j] * hs[s, g, j])
                    w_s[i, s, k * 16 : (k + 1) * 16, g * LANE : (g + 1) * LANE] = jnp.concatenate(prod, 0).astype(bf16)
        return tuple(hs.values())

    out = lax.fori_loop(0, blocks, body, tuple(h_s[q * 8 : (q + 1) * 8] for q in range(len(keys))))
    pick = (iota((16, 2 * LANE), 0) == iota((16, 2 * LANE), 1) // 16).astype(bf16)
    for s in range(S):
        for i in range(blocks // 2):
            both = jnp.concatenate([w_s[2 * i, s], w_s[2 * i + 1, s]], axis=0)
            y_ref[s, i * 16 : (i + 1) * 16] = mm(pick, both)
        y_ref[s] = y_ref[s] + vec_ref[1:2] * u_ref[s].astype(f32)
    for q in range(len(keys)):
        h_s[q * 8 : (q + 1) * 8] = out[q]


def backward_kernel(
    S, G, p_ref, u_ref, step_ref, ds_ref, masks_ref, proj_ref, vec_ref, rate_ref, rate2_ref, hot_ref, start_ref,
    dsp_ref, du_ref, p2_ref, dlog_ref, sum_ref, ag_s, h_s, wide, se_s, su_s, s_s, q_s, d_s, r_s
):
    blocks = LANE // 8
    C = G * LANE
    keys = [(s, g, j) for s in range(S) for g in range(G) for j in range(2)]

    @pl.when(pl.program_id(0) == 0)
    def _():
        ag_s[...] = jnp.zeros_like(ag_s)
        dlog_ref[...] = jnp.zeros_like(dlog_ref)
        sum_ref[...] = jnp.zeros_like(sum_ref)

    for s in range(S):
        step = step_ref[s]
        u = u_ref[s].astype(f32)
        se_s[s] = jnp.where(masks_ref[s, :, 1:2] > 0.5, step, BREAK).reshape(blocks, 8, C)
        su_s[s] = (step * u).reshape(blocks, 8, C)
        d_s[s] = ds_ref[s].reshape(blocks, 8, C)
        spread(p_ref[s, 0, LANE : LANE + 32], hot_ref[...], wide, s, blocks)

    def again(i, carry):
        hs = dict(zip(keys, carry))
        for k in range(8):
            for s in range(S):
                b = [wide[s, i, j * 8 : (j + 1) * 8, k * LANE : (k + 1) * LANE] for j in range(2)]
                for g in range(G):
                    se, su = row8(se_s, s, i, k, g), row8(su_s, s, i, k, g)
                    h_s[i * 8 + k, s * G + g] = jnp.concatenate([hs[s, g, 0], hs[s, g, 1]], 0).astype(bf16)
                    for j in range(2):
                        a = jnp.exp2(se * rate_ref[g, j * 8 : (j + 1) * 8])
                        hs[s, g, j] = a * hs[s, g, j] + su * b[j]
        return tuple(hs.values())

    out = lax.fori_loop(0, blocks, again, tuple(start_ref[0, q * 8 : (q + 1) * 8] for q in range(len(keys))))
    for s in range(S):
        for g in range(G):
            q = (s * G + g) * 2
            h_s[LANE, s * G + g] = jnp.concatenate([out[q], out[q + 1]], 0).astype(bf16)

    def two(v):
        return jnp.concatenate([v, v], 0).astype(bf16)

    pick = (iota((16, 2 * LANE), 0) == iota((16, 2 * LANE), 1) // 16).astype(bf16)
    fold = (lax.rem(iota((16, 2 * LANE), 1), 16) == iota((16, 2 * LANE), 0)).astype(bf16)
    one = jnp.ones((16, LANE), bf16)
    lane, row = iota((8, LANE), 1), iota((8, LANE), 0)

    def across_rows(product):
        found = product[0:8]
        for v in range(1, 16):
            found = jnp.where(lane >= 8 * v, product[8 * v : 8 * v + 8], found)
        found = jnp.sum(jnp.where(lax.rem(lane, 8) == row, found, 0.0), axis=0, keepdims=True)
        return jnp.broadcast_to(found, (8, LANE))

    def body(r, carry):
        low = blocks - 2 - 2 * r
        ags = dict(zip(keys, carry))
        tq, ts, tl, tb, tc = {}, {}, {}, {}, {}
        for t in reversed(range(16)):
            i, k = low + t // 8, t % 8
            for s in range(S):
                lanes = slice(k * LANE, (k + 1) * LANE)
                b16 = wide[s, i, 0:16, lanes].astype(bf16)
                c = [wide[s, i, 16 + j * 8 : 16 + (j + 1) * 8, lanes] for j in range(2)]
                for g in range(G):
                    se, su, ds = row8(se_s, s, i, k, g), row8(su_s, s, i, k, g), row8(d_s, s, i, k, g)
                    a = [jnp.exp2(se * rate_ref[g, j * 8 : (j + 1) * 8]) for j in range(2)]
                    gr = [c[j] * ds + ags[s, g, j] for j in range(2)]
                    for j in range(2):
                        ags[s, g, j] = a[j] * gr[j]
                    gb = jnp.concatenate(gr, 0).astype(bf16)
                    ab = jnp.concatenate(a, 0).astype(bf16)
                    gq = gb * (ab * h_s[i * 8 + k, s * G + g])
                    tq[s, g, t] = gq * rate2_ref[g]
                    tl[s, g, t] = gq * two(se)
                    ts[s, g, t] = gb * b16
                    tb[s, g, t] = gb * two(su)
                    tc[s, g, t] = h_s[i * 8 + k + 1, s * G + g] * two(ds)

        def mat(m, s):
            return jnp.concatenate([jnp.concatenate([m[s, g, t] for t in range(16)], 0) for g in range(G)], 1)

        def msum(m, s):
            return jnp.concatenate([sum(m[s, g, t] for g in range(G)) for t in range(16)], 0)

        for s in range(S):
            q = mm(pick, mat(tq, s))
            v = mm(pick, mat(ts, s))
            for h in range(2):
                q_s[s, low + h] = q[h * 8 : (h + 1) * 8]
                s_s[s, low + h] = v[h * 8 : (h + 1) * 8]
            dlog_ref[...] += mm(fold, mat(tl, s))
            for kind, m in enumerate((tb, tc)):
                found = mm_t(one, msum(m, s))[0:8]
                for h in range(2):
                    r_s[s, kind, low + h] = found[:, h * LANE : (h + 1) * LANE]
        return tuple(ags.values())

    ags = lax.fori_loop(0, blocks // 2, body, tuple(ag_s[q * 8 : (q + 1) * 8] for q in range(len(keys))))
    for q in range(len(keys)):
        ag_s[q * 8 : (q + 1) * 8] = ags[q]
    for s in range(S):
        step = step_ref[s]
        u = u_ref[s].astype(f32)
        ds = ds_ref[s]
        sums = s_s[s].reshape(LANE, C)
        dsp = ((q_s[s].reshape(LANE, C) + u * sums) * sigmoid_of_step(step)).astype(bf16)
        dsp_ref[s] = dsp
        du_ref[s] = step * sums + ds * vec_ref[1:2]
        p2_ref[s, 0, 0:LANE] = mm_t(dsp, proj_ref[...])
        for kind in range(2):
            for i in range(blocks):
                p2_ref[s, 0, LANE + 16 * kind + i : LANE + 16 * kind + i + 1] = r_s[s, kind, i, 0:1]
        sum_ref[0:1] += jnp.sum(dsp.astype(f32), axis=0, keepdims=True)
        sum_ref[1:2] += jnp.sum(ds * u, axis=0, keepdims=True)


def scan_specs(S, T, C, reverse):
    at = (lambda i: T // LANE - 1 - i) if reverse else (lambda i: i)
    return dict(
        packed=pl.BlockSpec((S, 1, LANE + 32, LANE), lambda i: (0, at(i), 0, 0)),
        block=pl.BlockSpec((S, LANE, C), lambda i: (0, at(i), 0)),
        masks=pl.BlockSpec((S, LANE, LANE), lambda i: (0, at(i), 0)),
        start=pl.BlockSpec((1, S * C // LANE * 16, LANE), lambda i: (at(i), 0, 0)),
    )


def scan_forward(packed, u, masks, proj_step, vec, rate2e, hot):
    S, T, C = u.shape
    G = C // LANE
    sp = scan_specs(S, T, C, False)
    by_token = pltpu.VMEM((S, LANE // 8, 8, C), f32)
    return pl.pallas_call(
        functools.partial(forward_kernel, S, G),
        grid=(T // LANE,),
        in_specs=[
            sp["packed"], sp["block"], sp["masks"], whole(LANE, C), whole(8, C), whole(G, 16, LANE), whole(LANE, 8 * LANE)
        ],
        out_specs=[sp["block"], sp["block"], sp["start"]],
        out_shape=[jax.ShapeDtypeStruct((S, T, C), f32)] * 2 + [jax.ShapeDtypeStruct((T // LANE, S * G * 16, LANE), f32)],
        scratch_shapes=[
            pltpu.VMEM((S * G * 16, LANE), f32),
            pltpu.VMEM((S, LANE // 8, 32, 8 * LANE), f32),
            pltpu.VMEM((LANE // 8, S, LANE, C), bf16),
            by_token,
            by_token,
        ],
        cost_estimate=cost(30),
        compiler_params=PARAMS,
    )(packed, u, masks, proj_step, vec, rate2e, hot)


def scan_backward(packed, u, step, ds, masks, proj_step, vec, rate2e, rate, hot, starts):
    S, T, C = u.shape
    G = C // LANE
    sp = scan_specs(S, T, C, True)
    by_token = pltpu.VMEM((S, LANE // 8, 8, C), f32)
    return pl.pallas_call(
        functools.partial(backward_kernel, S, G),
        grid=(T // LANE,),
        in_specs=[
            sp["packed"], sp["block"], sp["block"], sp["block"], sp["masks"], whole(LANE, C), whole(8, C),
            whole(G, 16, LANE), whole(G, 16, LANE), whole(LANE, 8 * LANE), sp["start"]
        ],
        out_specs=[sp["block"], sp["block"], sp["packed"], whole(16, C), whole(8, C)],
        out_shape=[
            jax.ShapeDtypeStruct((S, T, C), bf16),
            jax.ShapeDtypeStruct((S, T, C), f32),
            jax.ShapeDtypeStruct((S, T // LANE, LANE + 32, LANE), f32),
            jax.ShapeDtypeStruct((16, C), f32),
            jax.ShapeDtypeStruct((8, C), f32),
        ],
        scratch_shapes=[
            pltpu.VMEM((S * G * 16, LANE), f32),
            pltpu.VMEM((LANE + 1, S * G, 16, LANE), bf16),
            pltpu.VMEM((S, LANE // 8, 32, 8 * LANE), f32),
        ]
        + [by_token] * 5
        + [pltpu.VMEM((S, 2, LANE // 8, 8, LANE), f32)],
        cost_estimate=cost(85),
        compiler_params=PARAMS,
    )(packed, u, step, ds, masks, proj_step, vec, rate2e, rate.astype(bf16), hot, starts)


def after(*arrays):
    def kernel(*refs):
        refs[-1][0] = 0

    return pl.pallas_call(
        kernel,
        in_specs=[pl.BlockSpec(memory_space=pl.ANY) for _ in arrays],
        out_specs=pl.BlockSpec(memory_space=pltpu.SMEM),
        out_shape=jax.ShapeDtypeStruct((1,), jnp.int32),
    )(*arrays)[0]


def line_gather(array, axis):
    count = lax.axis_size(axis)
    right, left = array, array
    window = [array]
    for step in range(1, count):
        right = lax.ppermute(right, axis, [(i, i + 1) for i in range(step - 1, count - 1)])
        left = lax.ppermute(left, axis, [(i, i - 1) for i in range(1, count - step + 1)])
        window = [right] + window + [left]
    return window


def line_gather_at_once(array, axis):
    count = lax.axis_size(axis)
    return lax.all_to_all(jnp.broadcast_to(array[None], (count,) + array.shape), axis, 0, 0)


def line_scatter(blocks, axis):
    return jnp.sum(lax.all_to_all(blocks, axis, 0, 0).astype(f32), axis=0)


class Paired:
    def __init__(self):
        self.context = lax.axis_index("context")
        self.tensor = lax.axis_index("tensor")
        self.core = self.tensor % 2
        self.place = self.context[None]

    def across(self, array):
        return lax.ppermute(array, "context", [(0, 1), (1, 0)])

    def near(self, array):
        return lax.ppermute(array, "tensor", [(0, 1), (1, 0), (2, 3), (3, 2)])

    def far(self, array):
        return lax.ppermute(array, "tensor", [(0, 2), (2, 0), (1, 3), (3, 1)])

    def pieces(self, array, begin):
        half = array.shape[0] // 2
        mine = lax.dynamic_slice_in_dim(array, (self.core + begin) * half, half, 0)
        return self.across(mine), mine

    def pieces_done(self, array, block):
        return [array, joined_halves(block, self.near(block), self.core[None])]

    def normed(self, array, block, gain):
        own, inv_rms = normalised_rows(array, gain)
        return [own, joined_halves(block, self.near(block), self.core[None], gain)], inv_rms

    def total(self, array, begin):
        half = array.shape[0] // 2
        mine = lax.dynamic_slice_in_dim(array, self.core * half, half, 0)
        other = lax.dynamic_slice_in_dim(array, (1 - self.core + begin) * half, half, 0).astype(bf16)
        mine = mine + self.near(other).astype(f32)
        first, second = mine[: half // 2], mine[half // 2 :]
        first = first + self.far(first.astype(bf16)).astype(f32)
        second = second + self.across(second.astype(bf16)).astype(f32)
        first = first + self.across(first.astype(bf16)).astype(f32)
        second = second + self.far(second.astype(bf16)).astype(f32)
        mine = jnp.concatenate([first, second], axis=0)
        other = self.near(mine.astype(bf16)).astype(f32)
        zero = self.core == 0
        return jnp.concatenate([jnp.where(zero, mine, other), jnp.where(zero, other, mine)])

    def share_begin(self, product):
        keep = product((self.tensor, self.tensor ^ 2))
        give = product((self.tensor ^ 1, self.tensor ^ 3))
        return [(k.astype(f32) + self.near(g).astype(f32)) for k, g in zip(keep, give)]

    def share_middle(self, sums):
        own, other = sums
        rows, width = own.shape
        half, width = rows // 2, width // 2
        far = self.far(jnp.stack([own[:half, width:], other[:half, width:]]).astype(bf16))
        across = self.across(other[half:].astype(bf16))
        first = own[:half, :width] + far[0].astype(f32)
        give = other[:half, :width] + far[1].astype(f32)
        second = own[half:] + across.astype(f32)
        return first, give, second

    def share_end(self, sums):
        first, give, second = sums
        width = first.shape[1]
        first = first + self.across(give.astype(bf16)).astype(f32)
        second = second[:, :width] + self.far(second[:, width:].astype(bf16)).astype(f32)
        return jnp.concatenate([first, second], axis=0)

    def row_total(self, array):
        array = array + self.near(array)
        return array + self.far(array)

    def vector_total(self, array):
        return self.row_total(array + self.across(array))

    def both(self, array):
        other = self.across(array)
        zero = self.context == 0
        return jnp.stack([jnp.where(zero, array, other), jnp.where(zero, other, array)])


class General:
    def __init__(self, seqs):
        self.seqs = seqs
        self.place = jnp.zeros((1,), jnp.int32)

    def pieces(self, array, begin):
        return lax.all_gather(array, "context", tiled=True), array

    def pieces_done(self, array, block):
        return [self.in_order([block], self.seqs).reshape(block.shape)]

    def normed(self, array, block, gain):
        inv_rms = normalised_rows(array, gain)[1]
        return [normalised_rows(self.pieces_done(array, block)[0], gain)[0]], inv_rms

    def in_order(self, arrays, seqs):
        array = arrays[0].reshape(lax.axis_size("context"), seqs, -1, arrays[0].shape[-1])
        return array.swapaxes(0, 1).reshape(seqs, -1, array.shape[-1])

    def total(self, array, begin):
        return lax.psum(array, ("context", "tensor"))

    def share_begin(self, product):
        return [product((block,))[0].astype(f32) for block in range(lax.axis_size("tensor"))]

    def share_middle(self, sums):
        return sums

    def share_end(self, sums):
        parts = jnp.concatenate(sums, axis=-1)
        shape = parts.shape
        parts = parts.reshape(self.seqs, lax.axis_size("context"), -1, shape[-1]).swapaxes(0, 1).reshape(shape)
        parts = lax.psum_scatter(parts, "context", scatter_dimension=0, tiled=True)
        return lax.psum_scatter(parts, "tensor", scatter_dimension=1, tiled=True)

    def row_total(self, array):
        return lax.psum(array, "tensor")

    def vector_total(self, array):
        return lax.psum(array, ("context", "tensor"))

    def both(self, array):
        return lax.all_gather(array, "context")


def document_ids(lengths, positions):
    bounds = jnp.cumsum(lengths, axis=-1)[:, :2]
    passed = positions[None, :, None] >= bounds[:, None, :]
    return jnp.sum(passed.astype(jnp.int32), axis=-1)


def dot(a, b, out=f32):
    return jnp.dot(a, b, preferred_element_type=f32).astype(out)


def dot_t(a, b, out=f32):
    return lax.dot_general(a, b, (((1,), (1,)), ((), ())), preferred_element_type=f32).astype(out)


def t_dot(a, b, out=f32):
    return lax.dot_general(a, b, (((0,), (0,)), ((), ())), preferred_element_type=f32).astype(out)


def on_device(
    block_input,
    output_grad,
    doc_lengths,
    norm_gain,
    input_proj,
    conv_weight,
    conv_bias,
    select_proj,
    step_proj,
    step_bias,
    decay_log,
    skip_weight,
    output_proj,
):
    seqs, piece, model_width = block_input.shape
    shards, contexts, tensors = (lax.axis_size(axis) for axis in ("shards", "context", "tensor"))
    shard, context, tensor = (lax.axis_index(axis) for axis in ("shards", "context", "tensor"))
    moves = Paired() if (contexts, tensors) == (2, 4) else General(seqs)
    length = piece * contexts
    tokens = seqs * length
    depth = input_proj.shape[0]
    part = conv_weight.shape[0] // contexts
    inner = part * shards
    states = decay_log.shape[1]
    rank = step_proj.shape[0] * shards
    selected = select_proj.shape[1]
    taps = conv_weight.shape[1]
    share_width = model_width // tensors

    def mine(array):
        return lax.dynamic_slice_in_dim(array, context * part, part, 0)

    def my_columns(array, begin):
        blocks = [
            lax.dynamic_slice_in_dim(array, (block * contexts + context + begin) * part, part, array.ndim - 1)
            for block in range(shards)
        ]
        return jnp.concatenate(blocks, axis=-1)

    rows_flat = block_input.reshape(seqs * piece, model_width)
    row_block, row_slice = moves.pieces(rows_flat, 0)
    in_x = my_columns(input_proj[:, 0], after(row_slice))
    vectors = jnp.concatenate(
        [
            mine(select_proj),
            mine(conv_weight),
            mine(decay_log),
            mine(conv_bias)[:, None],
            mine(step_bias)[:, None],
            mine(skip_weight)[:, None],
        ],
        axis=1,
    )
    vectors = jnp.pad(vectors, ((0, 0), (0, 2 * LANE - vectors.shape[1])))
    flat = [in_x, my_columns(step_proj, 0), vectors.reshape(-1, inner), norm_gain.reshape(-1, inner)]
    flat = [jnp.pad(f, ((0, -f.shape[0] % 16), (0, 0))) for f in flat]
    window = line_gather(jnp.concatenate(flat, axis=0), "shards")
    proj_x, proj_step, vectors, gain = unpacked(window, [f.shape[0] for f in flat], shard[None])
    proj_x = proj_x.reshape(model_width, inner)
    proj_step = proj_step[:, : step_proj.shape[0]].reshape(rank, inner)
    vectors = vectors[:, : 2 * LANE * part // inner].reshape(inner, 2 * LANE)
    gain = gain[:, : norm_gain.shape[0] // inner].reshape(model_width).astype(f32)
    proj_select = vectors[:, :selected]
    rest = vectors[:, selected:].astype(f32)
    decay_rate = -jnp.exp(rest[:, taps : taps + states])
    at = taps + states
    conv_vec = jnp.concatenate([rest[:, :taps].T, rest[:, at][None], jnp.zeros((7 - taps, inner), f32)], axis=0)
    scan_vec = jnp.concatenate([rest[:, at + 1 : at + 3].T, jnp.zeros((6, inner), f32)], axis=0)
    select_low, select_state = proj_select[:, :rank], proj_select[:, rank:]

    normed, inv_rms = moves.normed(rows_flat, row_block, gain)
    grad_flat = output_grad.reshape(seqs * piece, model_width)
    grad_block = moves.pieces(grad_flat, after(row_block))[0]

    in_z = my_columns(input_proj[:, 1], after(window[len(window) // 2 - 1]))
    out_own = mine(output_proj)
    out_own = [out_own[:, i * inner : (i + 1) * inner] for i in range(model_width // inner)]
    others = jnp.concatenate([in_z] + out_own + [jnp.zeros((16, inner), bf16)], axis=0)
    others = lax.dynamic_slice_in_dim(others, after(proj_x) * 16, others.shape[0] - 16, 0)
    others = line_gather_at_once(others, "shards")

    document = document_ids(doc_lengths, jnp.arange(length, dtype=jnp.int32))
    masks = [jnp.pad(document, ((0, 0), (by, 0)), constant_values=-1)[:, :length] for by in range(taps)]
    masks += [jnp.pad(document, ((0, 0), (0, by)), constant_values=-1)[:, by:] for by in range(taps)]
    masks = jnp.stack([m == document for m in masks], axis=-1).astype(f32)
    masks = jnp.pad(masks, ((0, 0), (0, 0), (0, LANE - 2 * taps)))

    x_part, values, projected = convolve(
        normed, proj_x, conv_vec, masks, select_low, select_state.T, moves.place, taps
    )

    def total(packed, begin):
        return moves.total(packed.reshape(-1, LANE), begin).reshape(packed.shape)

    projected = total(projected, 0)

    hot = hot_rows()

    def by_group(array, begin=0.0):
        return (array.T + begin).reshape(states, inner // LANE, LANE).swapaxes(0, 1)

    ssm_out, step, starts = scan_forward(
        projected, values, masks, proj_step, scan_vec, by_group(decay_rate * LOG2E), hot
    )

    proj_z = others[:, :depth].reshape(model_width, inner)
    proj_out = jnp.concatenate(
        [others[:, depth + i * part : depth + (i + 1) * part] for i in range(model_width // inner)], axis=-1
    ).reshape(inner, model_width)
    grad_all = moves.pieces_done(grad_flat, grad_block)
    gated, grad_z, grad_ssm = gates(normed, grad_all, proj_z, proj_out, ssm_out, moves.place)

    def weight_grad(lefts, rights):
        return sum(t_dot(a, b) for a, b in zip(lefts, rights)).astype(bf16)

    early = [weight_grad(normed, grad_z).reshape(shards, depth, inner)]
    for i in range(model_width // inner):
        columns = [g[:, i * inner : (i + 1) * inner] for g in grad_all]
        early.append(weight_grad(gated, columns).reshape(shards, part, inner))
    early = line_scatter(jnp.concatenate(early, axis=1), "shards")
    grad_in_z = early[:depth]
    early_pair = moves.both(early.astype(bf16))
    in_z_pair, out_pair = early_pair[:, :depth], early_pair[:, depth:]

    def chosen(weights, blocks, axis, begin=0):
        return jnp.concatenate(
            [lax.dynamic_slice_in_dim(weights, (b + begin) * share_width, share_width, axis) for b in blocks], axis
        )

    out_sums = moves.share_begin(lambda blocks: [dot(g, chosen(proj_out, blocks, 1), bf16) for g in gated])
    out_sums_2 = moves.share_middle(out_sums)
    out_share = moves.share_end(out_sums_2)
    own_columns = tensor * share_width
    input_share = lax.dynamic_slice_in_dim(block_input, own_columns, share_width, 2).astype(f32)
    block_output = (input_share + out_share.reshape(input_share.shape)).astype(bf16)

    grad_step_pre, grad_direct, partial_grad, grad_decay, scan_sums = scan_backward(
        projected,
        values,
        step,
        grad_ssm,
        masks,
        proj_step,
        scan_vec,
        by_group(decay_rate * LOG2E),
        by_group(decay_rate, after(*out_sums).astype(f32)),
        hot,
        starts,
    )
    grad_decay_log = grad_decay.T * decay_rate
    step_low = projected[:, :, :rank].reshape(tokens, rank).astype(bf16)
    grad_step_proj = t_dot(step_low, grad_step_pre.reshape(tokens, inner))
    partial_grad = total(partial_grad, after(*out_sums_2))
    grad_x, conv_sums, grad_selected = convolve_back(
        partial_grad,
        grad_direct,
        x_part,
        conv_vec + after(block_output, early).astype(f32),
        masks,
        select_low,
        jnp.pad(select_state, ((0, 0), (0, LANE - select_state.shape[1]))),
        moves.place,
        len(normed),
        taps,
    )
    grad_select = t_dot(values.reshape(tokens, inner), grad_selected.reshape(tokens, -1))[:, :selected]

    small = jnp.concatenate(
        [
            grad_select,
            conv_sums[:taps].T,
            grad_decay_log,
            conv_sums[taps][:, None],
            scan_sums[:2].T,
        ],
        axis=1,
    ).astype(bf16)
    small = jnp.pad(small, ((0, 0), (0, 2 * LANE - small.shape[1])))
    late_local = jnp.concatenate(
        [
            weight_grad(normed, grad_x).reshape(shards, depth, inner),
            grad_step_proj.astype(bf16).reshape(shards, -1, inner),
            small.reshape(shards, -1, inner),
        ],
        axis=1,
    )
    begin = after(late_local)

    def normed_part(blocks):
        blocks = jnp.stack([jnp.asarray(b, jnp.int32) + begin for b in blocks])
        return products(grad_x, grad_z, proj_x, proj_z, blocks, share_width)

    grad_normed = moves.share_end(moves.share_middle(moves.share_begin(normed_part))).reshape(seqs, piece, share_width)
    inv_rms = inv_rms[:, :1].reshape(seqs, piece, 1)
    unit_share = input_share * inv_rms
    weighted = grad_normed * lax.dynamic_slice_in_dim(gain, own_columns, share_width, 0)
    row_dots = moves.row_total(jnp.sum(unit_share * weighted, axis=-1))[:, :, None]
    grad_share = lax.dynamic_slice_in_dim(output_grad, own_columns, share_width, 2).astype(f32)
    input_grad = grad_share + inv_rms * (weighted - unit_share * (row_dots / model_width))

    late = line_scatter(late_local, "shards")+ after(grad_normed, early_pair).astype(f32)
    grad_in_x = late[:depth]
    gain_part = jnp.sum(in_x.astype(f32) * grad_in_x, axis=1) + jnp.sum(in_z.astype(f32) * grad_in_z, axis=1)
    grad_gain = moves.vector_total(gain_part) / norm_gain.astype(f32)

    def columns_of(pair):
        pair = pair.astype(f32).reshape(pair.shape[:-1] + (shards, part))
        return jnp.moveaxis(pair, 0, -2).reshape(pair.shape[1], -1)

    late = moves.both(late.astype(bf16))
    grad_in = interleaved(late, early_pair, depth, part)
    grad_step_proj = columns_of(late[:, depth : depth + step_proj.shape[0]])
    small = late[:, depth + step_proj.shape[0] :].reshape(contexts * part, 2 * LANE).astype(f32)
    grad_out_proj = [out_pair[:, i * part : (i + 1) * part] for i in range(model_width // inner)]
    grad_out_proj = jnp.concatenate(grad_out_proj, axis=-1).reshape(contexts * part, model_width).astype(f32)
    at = selected + taps + states
    return (
        block_output,
        input_grad,
        grad_gain,
        grad_in,
        small[:, selected : selected + taps],
        small[:, at],
        small[:, :selected],
        grad_step_proj,
        small[:, at + 1],
        small[:, selected + taps : at],
        small[:, at + 2],
        grad_out_proj,
    )


def solution(mesh):
    placed = (
        P("shards", "context", None),
        P("shards", "context", None),
        P("shards", None),
        P("shards"),
        P("shards", None, "tensor"),
        P(("tensor", "shards"), None),
        P(("tensor", "shards")),
        P(("tensor", "shards"), None),
        P("shards", "tensor"),
        P(("tensor", "shards")),
        P(("tensor", "shards"), None),
        P(("tensor", "shards")),
        P(("tensor", "shards"), None),
    )
    return jax.shard_map(
        on_device,
        mesh=mesh,
        in_specs=placed,
        out_specs=(
            P("shards", "context", "tensor"),
            P("shards", "context", "tensor"),
            P("shards"),
            P("shards", None, "tensor"),
            P(("tensor", "shards"), None),
            P(("tensor", "shards")),
            P(("tensor", "shards"), None),
            P("shards", "tensor"),
            P(("tensor", "shards")),
            P(("tensor", "shards"), None),
            P(("tensor", "shards")),
            P(("tensor", "shards"), None),
        ),
        check_vma=False,
    )
```

time: 664 us -> 587 us (0.88)
  Pallas kernels: 110 us -> 208 us
  matrix products: 96.7 us -> 32.7 us
  local copies, waits for them, and re-layouts: 129 us -> 71.5 us
  other arithmetic: 116 us -> 60.5 us
  between operations: 3.33 us -> 14.1 us
  starting transfers between devices: 68.3 us -> 59.5 us
    pallas_call x2 -> x21, Pallas kernels: 110 us -> 208 us  [the longest x1 69.5 us: scan_backward(): pl.pallas_call(functools.partial(backward_kernel, S, G), grid=(T // LANE,...]
    dot_general x12 -> x0, matrix products: 36.4 us -> none  [dot_t(): lax.dot_general(a, b, (((1,), (1,)), ((), ())), preferred_element_type=f32)]
    reduce_sum x5 -> x1, other arithmetic: 30.7 us -> 0.18 us  [on_device(): jnp.sum(in_z.astype(f32) * grad_in_z, axis=1)]
    dot_general x10 -> x4, matrix products: 31.1 us -> 4.98 us  [dot(): return jnp.dot(a, b, preferred_element_type=f32).astype(out)]
    convert_element_type x12 -> x7, other arithmetic: 23.6 us -> 6.84 us  [the longest x2 2.72 us: share_end(): first = first + self.across(give.astype(bf16)).astype(f32)]
    dynamic_update_slice x8 -> x0, local copies, waits for them, and re-layouts: 16.5 us -> none  [the longest x3 6.09 us: pieces_soon(): out = lax.dynamic_update_slice_in_dim(out, block, start, 0)]
    unnamed x274 -> x145, local copies, waits for them, and re-layouts: 30.9 us -> 15.8 us
    add x6 -> x10, other arithmetic: 6.19 us -> 14.3 us  [the longest x3 6.72 us: share_begin(): k.astype(f32) + self.near(g).astype(f32)]
  transfers between devices with their start and end apart: 51 -> 44, of which waited for: 19 -> 18; matrix products, arithmetic and copies ran while one was open for 37% -> 19% of each run, Pallas kernels for 12% -> 27%
where the time goes in v2:
time: 587 us; the launch traced here: 580 us
  Pallas kernels  208 us (35%)
  waiting for transfers between devices  133 us (23%)
  local copies, waits for them, and re-layouts  71.5 us (12%)
  other arithmetic  60.5 us (10%)
  starting transfers between devices  59.5 us (10%)
  matrix products  32.7 us (6%)
  between operations  14.1 us (2%)
    pallas_call x1, Pallas kernels, scan_backward(): pl.pallas_call(functools.partial(backward_kernel, S, G), grid=(T // LANE,...  69.5 us
    ppermute x13, waiting for transfers between devices, across(): return lax.ppermute(array, 'context', [(0, 1), (1, 0)])  61.4 us
    ppermute x10, waiting for transfers between devices, far(): return lax.ppermute(array, 'tensor', [(0, 2), (2, 0), (1, 3), (3, 1)])  34.9 us
    ppermute x3, waiting for transfers between devices, line_gather(): lax.ppermute(left, axis, [(i, i - 1) for i in range(1, count - step + 1)])  34.2 us
    pallas_call x1, Pallas kernels, scan_forward(): pl.pallas_call(functools.partial(forward_kernel, S, G), grid=(T // LANE,)...  33.7 us
    dot_general x14, matrix products, t_dot(): lax.dot_general(a, b, (((0,), (0,)), ((), ())), preferred_element_type=f32)  27.7 us
    pallas_call x1, Pallas kernels, gates(): pl.pallas_call(kernel, grid_spec=pltpu.PrefetchScalarGridSpec(num_scalar_...  19.2 us
    pallas_call x2, Pallas kernels, products(): pl.pallas_call(kernel, grid_spec=pltpu.PrefetchScalarGridSpec(num_scalar_...  18.9 us
  transfers between devices with their start and end apart: 44, of which 18 were waited for; matrix products, arithmetic and copies ran while one was open for 19% of the time, Pallas kernels for 27%

profile of v2, /device:TPU:0, one launch (start us, length us, event | category | flops | bytes accessed | tf_op | source)
XLA Modules:
  0.0 579.7 jit_solution(16468552073045633071)
XLA Ops:
  0.7 3.2 constant_dynamic-slice_fusion.21.refs_0_
  3.9 3.0 collective-permute-start.6
  10.7 6.8 %fusion.66 = (bf16[512,1,1024]{2,1,0:T(2,128)(2,1)}, bf16[512,1,1024]{2,1,0:T(2,128)(2,1)}) fusion(bf16[512,2,1024]{2,1,0:T(2,128)(2,1)} %param.17), kind=kLoop, calls=%fused_computation.245 | loop fusion | bytes 4194304 | tf_op jit(solution)/shard_map/slice | solution.py:925
  22.0 4.6 collective-permute-start
  26.6 11.9 %collective-permute-done.3.refs_4_ = bf16[624,512]{1,0:T(8,128)(2,1)} collective-permute-done((bf16[624,512]{1,0:T(8,128)(2,1)S(1)}, bf16[624,512]{1,0:T(8,128)(2,1)}, u32[]{:S(2)}, u32[]{:S(2)}) %collective-permute-start.3) | collective-permute-done | bytes 639008 | tf_op jit(solution)/shard_map/ppermute | solution.py:694
  47.3 8.4 %collective-permute-done.4.refs_5_ = bf16[624,512]{1,0:T(8,128)(2,1)} collective-permute-done((bf16[624,512]{1,0:T(8,128)(2,1)}, bf16[624,512]{1,0:T(8,128)(2,1)}, u32[]{:S(2)}, u32[]{:S(2)}) %collective-permute-start.4) | collective-permute-done | bytes 639008 | tf_op jit(solution)/shard_map/ppermute | solution.py:694
  57.9 13.9 %collective-permute-done.5.refs_6_ = bf16[624,512]{1,0:T(8,128)(2,1)S(1)} collective-permute-done((bf16[624,512]{1,0:T(8,128)(2,1)}, bf16[624,512]{1,0:T(8,128)(2,1)S(1)}, u32[]{:S(2)}, u32[]{:S(2)}) %collective-permute-start.5) | collective-permute-done | bytes 639008 | tf_op jit(solution)/shard_map/ppermute | solution.py:694
  72.8 4.2 shard_map.221
  78.3 2.5 broadcast_in_dim.43
  80.8 6.9 %all-to-all-start = ((bf16[4,1024,512]{2,1,0:T(8,128)(2,1)}), bf16[4,1024,512]{2,1,0:T(8,128)(2,1)}, u32[]{:S(2)}, u32[]{:S(2)}) async-start(bf16[4,1024,512]{2,1,0:T(8,128)(2,1)} %broadcast_in_dim.43), calls=%async_computation | async-start | bytes 8388608 | tf_op jit(solution)/shard_map/all_to_all | solution.py:701
  92.7 5.6 stack.92
  104.0 5.5 shard_map.222
  111.6 3.2 constant_dynamic-slice_fusion.9
  115.4 7.5 %shard_map.223.refs_1_ = bf16[1024,2048]{1,0:T(8,128)(2,1)} custom-call(s32[1]{0:T(128)} %bitcast.12.place_ref, bf16[512,2048]{1,0:T(8,128)(2,1)} %copy-done.14, bf16[512,2048]{1,0:T(8,128)(2,1)} %collective-permute-done.7.second_ref, f32[1,2048]{1,0:T(1,128)} %bitcast.236), custom_call_target="tpu_custom_call" | custom-call | flops 460000000 | bytes 1440000 | tf_op jit(solution)/shard_map/pallas_call | solution.py:79
  122.9 15.2 %shard_map.228 = (bf16[2,1024,512]{2,1,0:T(8,128)(2,1)}, bf16[2,1024,512]{2,1,0:T(8,128)(2,1)}, f32[2,8,160,128]{3,2,1,0:T(8,128)}) custom-call(s32[1]{0:T(128)} %bitcast.place_ref, bf16[1024,2048]{1,0:T(8,128)(2,1)} %get-tuple-element.43.refs_0_, bf16[1024,2048]{1,0:T(8,128)(2,1)} %shard_map.223.refs_1_, bf16[2048,512]{1,0:T(8,128)(2,1)} %bitcast.179, ...), custom_call_target="tpu_custom_call" | custom-call | flops 1035000000 | bytes 3240000 | tf_op jit(solution)/shard_map/pallas_call | solution.py:270
  145.4 2.9 collective-permute-done.11
  148.4 17.7 %collective-permute-done.13 = bf16[640,128]{1,0:T(8,128)(2,1)S(1)} collective-permute-done((bf16[640,128]{1,0:T(8,128)(2,1)S(1)}, bf16[640,128]{1,0:T(8,128)(2,1)S(1)}, u32[]{:S(2)}, u32[]{:S(2)}) %collective-permute-start.13) | collective-permute-done | bytes 163872 | tf_op jit(solution)/shard_map/ppermute | solution.py:716
  175.3 33.7 %shard_map.229 = (f32[2,1024,512]{2,1,0:T(8,128)}, f32[2,1024,512]{2,1,0:T(8,128)}, f32[8,128,128]{2,1,0:T(8,128)}) custom-call(f32[2,8,160,128]{3,2,1,0:T(8,128)} %bitcast.200, bf16[2,1024,512]{2,1,0:T(8,128)(2,1)} %get-tuple-element.47.u_ref, f32[2,1024,128]{2,1,0:T(8,128)} %pad_convert_fusion.refs_4_.masks_ref, bf16[128,512]{1,0:T(8,128)(2,1)} %bitcast.247, ...), custom_call_target="tpu_custom_call" | custom-call | flops 3449999872 | bytes 10800000 | tf_op jit(solution)/shard_map/pallas_call | solution.py:624
  209.0 7.1 %shard_map.225.refs_3_ = bf16[1024,2048]{1,0:T(8,128)(2,1)} custom-call(s32[1]{0:T(128)} %bitcast.12.place_ref, bf16[512,2048]{1,0:T(8,128)(2,1)} %collective-permute-done.8.first_ref, bf16[512,2048]{1,0:T(8,128)(2,1)} %collective-permute-done.9.second_ref), custom_call_target="tpu_custom_call" | custom-call | flops 460000000 | bytes 1440000 | tf_op jit(solution)/shard_map/pallas_call | solution.py:79
  219.4 3.0 slice.333
  222.5 19.2 %shard_map.230 = (bf16[1024,512]{1,0:T(8,128)(2,1)}, bf16[1024,512]{1,0:T(8,128)(2,1)}, bf16[1024,512]{1,0:T(8,128)(2,1)}, bf16[1024,512]{1,0:T(8,128)(2,1)}, f32[2,1024,512]{2,1,0:T(8,128)}) custom-call(s32[1]{0:T(128)} %bitcast.place_ref, bf16[1024,2048]{1,0:T(8,128)(2,1)} %get-tuple-element.43.refs_0_, bf16[1024,2048]{1,0:T(8,128)(2,1)} %shard_map.223.refs_1_, ...), custom_call_target="tpu_custom_call" | custom-call | flops 1610000000 | bytes 5040000 | tf_op jit(solution)/shard_map/pallas_call | solution.py:313
  253.2 2.5 add_convert_fusion.1
  264.4 3.2 fusion.64
  275.0 5.2 all-to-all-start.1
  287.4 8.8 %collective-permute-done.18 = bf16[2,512,512]{2,1,0:T(8,128)(2,1)} collective-permute-done((bf16[2,512,512]{2,1,0:T(8,128)(2,1)}, bf16[2,512,512]{2,1,0:T(8,128)(2,1)}, u32[]{:S(2)}, u32[]{:S(2)}) %collective-permute-start.18) | collective-permute-done | bytes 1048608 | tf_op jit(solution)/shard_map/ppermute | solution.py:722
  296.2 2.6 fusion.63
  300.9 69.5 %shard_map.232 = (bf16[2,1024,512]{2,1,0:T(8,128)(2,1)}, f32[2,1024,512]{2,1,0:T(8,128)}, f32[2,8,160,128]{3,2,1,0:T(8,128)}, f32[16,512]{1,0:T(8,128)}, f32[8,512]{1,0:T(8,128)}) custom-call(f32[2,8,160,128]{3,2,1,0:T(8,128)} %bitcast.202, bf16[2,1024,512]{2,1,0:T(8,128)(2,1)} %get-tuple-element.47.u_ref, f32[2,1024,512]{2,1,0:T(8,128)} %get-tuple-element.53.step_ref, ...), custom_call_target="tpu_custom_call" | custom-call | flops 9774999552 | bytes 30600000 | tf_op jit(solution)/shard_map/pallas_call | solution.py:649
  372.0 3.3 slice_add_fusion.1.refs_2_
  375.3 2.6 convert_add_fusion.5
  383.9 3.0 convolution_convert_fusion.2
  390.9 13.9 %collective-permute-done.23 = bf16[640,128]{1,0:T(8,128)(2,1)S(1)} collective-permute-done((bf16[640,128]{1,0:T(8,128)(2,1)S(1)}, bf16[640,128]{1,0:T(8,128)(2,1)S(1)}, u32[]{:S(2)}, u32[]{:S(2)}) %collective-permute-start.23) | collective-permute-done | bytes 163872 | tf_op jit(solution)/shard_map/ppermute | solution.py:722
  406.8 4.1 collective-permute-done.24
  411.3 2.6 fusion.6.refs_0_
  415.2 4.4 convert_reduce_fusion.refs_1_
  421.4 16.3 %shard_map.235 = (bf16[1024,512]{1,0:T(8,128)(2,1)}, bf16[1024,512]{1,0:T(8,128)(2,1)}, f32[8,512]{1,0:T(8,128)}, bf16[2,1024,256]{2,1,0:T(8,128)(2,1)}) custom-call(s32[1]{0:T(128)} %bitcast.place_ref, f32[2,8,160,128]{3,2,1,0:T(8,128)} %bitcast.199, f32[2,1024,512]{2,1,0:T(8,128)} %get-tuple-element.57.d_ref, ...), custom_call_target="tpu_custom_call" | custom-call | flops 1150000000 | bytes 3600000 | tf_op jit(solution)/shard_map/pallas_call | solution.py:385
  438.5 5.8 fusion.72
  446.3 5.9 %add_convert_fusion = bf16[2048,512]{1,0:T(8,128)(2,1)S(1)} fusion(f32[2048,512]{1,0:T(8,128)} %fusion.72, bf16[1024,2048]{1,0:T(8,128)(2,1)} %shard_map.223.refs_1_, bf16[1024,512]{1,0:T(8,128)(2,1)S(1)} %copy-done.19), kind=kOutput, calls=%fused_computation.4 | convolution fusion | flops 2149580800 | bytes 11534336 | tf_op jit(solution)/shard_map/dot_general | solution.py:847
  457.5 9.5 %shard_map.238 = (bf16[1024,1024]{1,0:T(8,128)(2,1)}, bf16[1024,1024]{1,0:T(8,128)(2,1)}) custom-call(s32[2]{0:T(128)} %get-tuple-element.140.blocks_ref, bf16[1024,512]{1,0:T(8,128)(2,1)} %get-tuple-element.61.refs_0_, bf16[1024,512]{1,0:T(8,128)(2,1)} %get-tuple-element.62.refs_1_, bf16[1024,512]{1,0:T(8,128)(2,1)} %get-tuple-element.59.refs_2_, ...), custom_call_target="tpu_custom_call" | custom-call | flops 575000000 | bytes 1800000 | tf_op jit(solution)/shard_map/pallas_call | solution.py:157
  468.5 5.3 all-to-all-start.2
  475.6 9.4 %shard_map.237 = (bf16[1024,1024]{1,0:T(8,128)(2,1)}, bf16[1024,1024]{1,0:T(8,128)(2,1)}) custom-call(s32[2]{0:T(128)} %get-tuple-element.139.blocks_ref, bf16[1024,512]{1,0:T(8,128)(2,1)} %get-tuple-element.61.refs_0_, bf16[1024,512]{1,0:T(8,128)(2,1)} %get-tuple-element.62.refs_1_, bf16[1024,512]{1,0:T(8,128)(2,1)} %get-tuple-element.59.refs_2_, ...), custom_call_target="tpu_custom_call" | custom-call | flops 575000000 | bytes 1800000 | tf_op jit(solution)/shard_map/pallas_call | solution.py:157
  485.1 3.3 convert_add_fusion
  494.5 5.5 collective-permute-done.36
  500.3 21.4 %collective-permute-done.32 = bf16[512,1024]{1,0:T(8,128)(2,1)S(1)} collective-permute-done((bf16[512,1024]{1,0:T(8,128)(2,1)S(1)}, bf16[512,1024]{1,0:T(8,128)(2,1)S(1)}, u32[]{:S(2)}, u32[]{:S(2)}) %collective-permute-start.32) | collective-permute-done | bytes 1048608 | tf_op jit(solution)/shard_map/ppermute | solution.py:716
  526.7 8.7 %collective-permute-done.33 = bf16[512,512]{1,0:T(8,128)(2,1)S(1)} collective-permute-done((bf16[512,512]{1,0:T(8,128)(2,1)S(1)}, bf16[512,512]{1,0:T(8,128)(2,1)S(1)}, u32[]{:S(2)}, u32[]{:S(2)}) %collective-permute-start.33) | collective-permute-done | bytes 524320 | tf_op jit(solution)/shard_map/ppermute | solution.py:722
  537.3 2.6 fusion.2
  553.2 3.5 fusion.5
  557.3 8.9 %collective-permute-done.40 = bf16[608,512]{1,0:T(8,128)(2,1)S(1)} collective-permute-done((bf16[608,512]{1,0:T(8,128)(2,1)S(1)}, bf16[608,512]{1,0:T(8,128)(2,1)S(1)}, u32[]{:S(2)}, u32[]{:S(2)}) %collective-permute-start.40) | collective-permute-done | bytes 622624 | tf_op jit(solution)/shard_map/ppermute | solution.py:716
  573.0 6.5 %shard_map.240 = f32[512,2,1024]{2,1,0:T(2,128)} custom-call(bf16[2,608,512]{2,1,0:T(8,128)(2,1)} %pad_maximum_fusion.5.a_ref, bf16[2,1024,512]{2,1,0:T(8,128)(2,1)} %pad_maximum_fusion.refs_1_.b_ref), custom_call_target="tpu_custom_call" | custom-call | flops 575000000 | bytes 1800000 | tf_op jit(solution)/shard_map/pallas_call | solution.py:183
  (376 shorter events, 141.3 us)
Async XLA Ops:
  3.9 74.2 %collective-permute-start.6 = (bf16[512,2048]{1,0:T(8,128)(2,1)}, bf16[512,2048]{1,0:T(8,128)(2,1)S(1)}, u32[]{:S(2)}, u32[]{:S(2)}) collective-permute-start(bf16[512,2048]{1,0:T(8,128)(2,1)} %constant_dynamic-slice_fusion.21.refs_0_), channel_id=1, source_target_pairs={{0,4},{4,0},{1,5},{5,1},{2,6},{6,2},{3,7},{7,3},{8,12},{12,8},{9,1... | collective-permute-start | bytes 6291464 | tf_op jit(solution)/shard_map/ppermute | solution.py:716
  20.7 26.6 %copy-start.21 = (bf16[624,512]{1,0:T(8,128)(2,1)}, bf16[624,512]{1,0:T(8,128)(2,1)S(1)}, u32[]{:S(2)}) copy-start(bf16[624,512]{1,0:T(8,128)(2,1)S(1)} %fusion.30.refs_3_) | copy-start | bytes 1916932
  20.7 17.8 %collective-permute-start.3 = (bf16[624,512]{1,0:T(8,128)(2,1)S(1)}, bf16[624,512]{1,0:T(8,128)(2,1)}, u32[]{:S(2)}, u32[]{:S(2)}) collective-permute-start(bf16[624,512]{1,0:T(8,128)(2,1)S(1)} %fusion.30.refs_3_), channel_id=1, source_target_pairs={{8,0},{16,8},{24,16},{9,1},{17,9},{25,17},{10,2},{18,10},{26,18},{... | collective-permute-start | bytes 1916936 | tf_op jit(solution)/shard_map/ppermute | solution.py:694
  22.0 17.8 %collective-permute-start = (bf16[624,512]{1,0:T(8,128)(2,1)S(1)}, bf16[624,512]{1,0:T(8,128)(2,1)S(1)}, u32[]{:S(2)}, u32[]{:S(2)}) collective-permute-start(bf16[624,512]{1,0:T(8,128)(2,1)S(1)} %fusion.30.refs_3_), channel_id=1, source_target_pairs={{0,8},{8,16},{16,24},{1,9},{9,17},{17,25},{2,10},{10,18},{18,26},{... | collective-permute-start | bytes 1916936 | tf_op jit(solution)/shard_map/ppermute | solution.py:693
  38.5 17.1 %collective-permute-start.4 = (bf16[624,512]{1,0:T(8,128)(2,1)}, bf16[624,512]{1,0:T(8,128)(2,1)}, u32[]{:S(2)}, u32[]{:S(2)}) collective-permute-start(bf16[624,512]{1,0:T(8,128)(2,1)} %collective-permute-done.3.refs_4_), channel_id=1, source_target_pairs={{8,0},{16,8},{9,1},{17,9},{10,2},{18,10},{11,3},{19,11},{12,4},{20... | collective-permute-start | bytes 1916936 | tf_op jit(solution)/shard_map/ppermute | solution.py:694
  39.8 17.1 %collective-permute-start.1 = (bf16[624,512]{1,0:T(8,128)(2,1)S(1)}, bf16[624,512]{1,0:T(8,128)(2,1)}, u32[]{:S(2)}, u32[]{:S(2)}) collective-permute-start(bf16[624,512]{1,0:T(8,128)(2,1)S(1)} %collective-permute-done.refs_2_.refs_0_), channel_id=1, source_target_pairs={{8,16},{16,24},{9,17},{17,25},{10,18},{18,26},{11,19},{19,27},{12,... | collective-permute-start | bytes 1916936 | tf_op jit(solution)/shard_map/ppermute | solution.py:693
  47.2 24.6 %copy-start.34 = (bf16[512,1,128]{2,0,1:T(8,128)(2,1)}, bf16[512,1,128]{2,0,1:T(8,128)(2,1)S(1)}, u32[]{:S(2)}) copy-start(bf16[512,1,128]{2,0,1:T(8,128)(2,1)S(1)} %copy.338) | copy-start | bytes 393220
  47.2 24.5 %copy-start.36 = (bf16[512,1,128]{2,0,1:T(8,128)(2,1)}, bf16[512,1,128]{2,0,1:T(8,128)(2,1)S(1)}, u32[]{:S(2)}) copy-start(bf16[512,1,128]{2,0,1:T(8,128)(2,1)S(1)} %copy.339) | copy-start | bytes 393220
  47.3 24.5 %copy-start.38 = (bf16[512,1,128]{2,0,1:T(8,128)(2,1)}, bf16[512,1,128]{2,0,1:T(8,128)(2,1)S(1)}, u32[]{:S(2)}) copy-start(bf16[512,1,128]{2,0,1:T(8,128)(2,1)S(1)} %copy.337) | copy-start | bytes 393220
  55.6 16.1 %collective-permute-start.5 = (bf16[624,512]{1,0:T(8,128)(2,1)}, bf16[624,512]{1,0:T(8,128)(2,1)S(1)}, u32[]{:S(2)}, u32[]{:S(2)}) collective-permute-start(bf16[624,512]{1,0:T(8,128)(2,1)} %collective-permute-done.4.refs_5_), channel_id=1, source_target_pairs={{8,0},{9,1},{10,2},{11,3},{12,4},{13,5},{14,6},{15,7}} | collective-permute-start | bytes 1916936 | tf_op jit(solution)/shard_map/ppermute | solution.py:694
  56.9 14.8 %collective-permute-start.2 = (bf16[624,512]{1,0:T(8,128)(2,1)}, bf16[624,512]{1,0:T(8,128)(2,1)S(1)}, u32[]{:S(2)}, u32[]{:S(2)}) collective-permute-start(bf16[624,512]{1,0:T(8,128)(2,1)} %collective-permute-done.1.refs_1_), channel_id=1, source_target_pairs={{16,24},{17,25},{18,26},{19,27},{20,28},{21,29},{22,30},{23,31}} | collective-permute-start | bytes 1916936 | tf_op jit(solution)/shard_map/ppermute | solution.py:693
  78.2 37.2 %collective-permute-start.7 = (bf16[512,2048]{1,0:T(8,128)(2,1)S(1)}, bf16[512,2048]{1,0:T(8,128)(2,1)}, u32[]{:S(2)}, u32[]{:S(2)}) collective-permute-start(bf16[512,2048]{1,0:T(8,128)(2,1)S(1)} %collective-permute-done.6.first_ref.refs_0_), channel_id=1, source_target_pairs={{0,1},{1,0},{2,3},{3,2},{4,5},{5,4},{6,7},{7,6},{8,9},{9,8},{10,11... | collective-permute-start | bytes 6291464 | tf_op jit(solution)/shard_map/ppermute | solution.py:719
  80.8 135.3 %all-to-all-start = ((bf16[4,1024,512]{2,1,0:T(8,128)(2,1)}), bf16[4,1024,512]{2,1,0:T(8,128)(2,1)}, u32[]{:S(2)}, u32[]{:S(2)}) async-start(bf16[4,1024,512]{2,1,0:T(8,128)(2,1)} %broadcast_in_dim.43), calls=%async_computation | async-start | bytes 8388608 | tf_op jit(solution)/shard_map/all_to_all | solution.py:701
  114.8 54.3 %collective-permute-start.8 = (bf16[512,2048]{1,0:T(8,128)(2,1)}, bf16[512,2048]{1,0:T(8,128)(2,1)}, u32[]{:S(2)}, u32[]{:S(2)}) collective-permute-start(bf16[512,2048]{1,0:T(8,128)(2,1)} %constant_dynamic-slice_fusion.9), channel_id=1, source_target_pairs={{0,4},{4,0},{1,5},{5,1},{2,6},{6,2},{3,7},{7,3},{8,12},{12,8},{9,1... | collective-permute-start | bytes 6291464 | tf_op jit(solution)/shard_map/ppermute | solution.py:716
  139.2 1.7 collective-permute-start.10
  142.1 6.3 %collective-permute-start.11 = (bf16[640,128]{1,0:T(8,128)(2,1)S(1)}, bf16[640,128]{1,0:T(8,128)(2,1)S(1)}, u32[]{:S(2)}, u32[]{:S(2)}) collective-permute-start(bf16[640,128]{1,0:T(8,128)(2,1)S(1)} %get-tuple-element.122), channel_id=1, source_target_pairs={{0,2},{2,0},{1,3},{3,1},{4,6},{6,4},{5,7},{7,5},{8,10},{10,8},{9,1... | collective-permute-start | bytes 491528 | tf_op jit(solution)/shard_map/ppermute | solution.py:722
  143.6 22.5 %collective-permute-start.13 = (bf16[640,128]{1,0:T(8,128)(2,1)S(1)}, bf16[640,128]{1,0:T(8,128)(2,1)S(1)}, u32[]{:S(2)}, u32[]{:S(2)}) collective-permute-start(bf16[640,128]{1,0:T(8,128)(2,1)S(1)} %get-tuple-element.123), channel_id=1, source_target_pairs={{0,4},{4,0},{1,5},{5,1},{2,6},{6,2},{3,7},{7,3},{8,12},{12,8},{9,1... | collective-permute-start | bytes 491528 | tf_op jit(solution)/shard_map/ppermute | solution.py:716
  166.2 5.4 collective-permute-start.12
  166.8 5.3 collective-permute-start.14
  169.1 39.8 %collective-permute-start.9 = (bf16[512,2048]{1,0:T(8,128)(2,1)}, bf16[512,2048]{1,0:T(8,128)(2,1)}, u32[]{:S(2)}, u32[]{:S(2)}) collective-permute-start(bf16[512,2048]{1,0:T(8,128)(2,1)} %collective-permute-done.8.first_ref), channel_id=1, source_target_pairs={{0,1},{1,0},{2,3},{3,2},{4,5},{5,4},{6,7},{7,6},{8,9},{9,8},{10,11... | collective-permute-start | bytes 6291464 | tf_op jit(solution)/shard_map/ppermute | solution.py:719
  172.2 1.8 collective-permute-start.15
  249.2 15.2 %collective-permute-start.17 = (bf16[1024,1024]{1,0:T(8,128)(2,1)S(1)}, bf16[1024,1024]{1,0:T(8,128)(2,1)S(1)}, u32[]{:S(2)}, u32[]{:S(2)}) collective-permute-start(bf16[1024,1024]{1,0:T(8,128)(2,1)S(1)} %convolution_convert_fusion), channel_id=1, source_target_pairs={{0,1},{1,0},{2,3},{3,2},{4,5},{5,4},{6,7},{7,6},{8,9},{9,8},{10,11... | collective-permute-start | bytes 6291464 | tf_op jit(solution)/shard_map/ppermute | solution.py:719
  249.7 18.0 %collective-permute-start.16 = (bf16[1024,1024]{1,0:T(8,128)(2,1)S(1)}, bf16[1024,1024]{1,0:T(8,128)(2,1)S(1)}, u32[]{:S(2)}, u32[]{:S(2)}) collective-permute-start(bf16[1024,1024]{1,0:T(8,128)(2,1)S(1)} %convolution_convert_fusion.1), channel_id=1, source_target_pairs={{0,1},{1,0},{2,3},{3,2},{4,5},{5,4},{6,7},{7,6},{8,9},{9,8},{10,11... | collective-permute-start | bytes 6291464 | tf_op jit(solution)/shard_map/ppermute | solution.py:719
  270.3 25.9 %collective-permute-start.18 = (bf16[2,512,512]{2,1,0:T(8,128)(2,1)}, bf16[2,512,512]{2,1,0:T(8,128)(2,1)}, u32[]{:S(2)}, u32[]{:S(2)}) collective-permute-start(bf16[2,512,512]{2,1,0:T(8,128)(2,1)} %pad_maximum_fusion.10), channel_id=1, source_target_pairs={{0,2},{2,0},{1,3},{3,1},{4,6},{6,4},{5,7},{7,5},{8,10},{10,8},{9,1... | collective-permute-start | bytes 3145736 | tf_op jit(solution)/shard_map/ppermute | solution.py:722
  275.0 140.2 %all-to-all-start.1 = ((bf16[4,1024,512]{2,1,0:T(8,128)(2,1)}), bf16[4,1024,512]{2,1,0:T(8,128)(2,1)}, u32[]{:S(2)}, u32[]{:S(2)}) async-start(bf16[4,1024,512]{2,1,0:T(8,128)(2,1)} %constant_dynamic-update-slice_fusion.1), calls=%async_computation.1 | async-start | bytes 8388608 | tf_op jit(solution)/shard_map/all_to_all | solution.py:705
  283.2 88.8 %collective-permute-start.20 = (bf16[512,1024]{1,0:T(8,128)(2,1)S(1)}, bf16[512,1024]{1,0:T(8,128)(2,1)S(1)}, u32[]{:S(2)}, u32[]{:S(2)}) collective-permute-start(bf16[512,1024]{1,0:T(8,128)(2,1)S(1)} %slice.354), channel_id=1, source_target_pairs={{0,4},{4,0},{1,5},{5,1},{2,6},{6,2},{3,7},{7,3},{8,12},{12,8},{9,1... | collective-permute-start | bytes 3145736 | tf_op jit(solution)/shard_map/ppermute | solution.py:716
  298.7 76.6 %collective-permute-start.19 = (bf16[512,512]{1,0:T(8,128)(2,1)S(1)}, bf16[512,512]{1,0:T(8,128)(2,1)S(1)}, u32[]{:S(2)}, u32[]{:S(2)}) collective-permute-start(bf16[512,512]{1,0:T(8,128)(2,1)S(1)} %get-tuple-element.76), channel_id=1, source_target_pairs={{0,4},{4,0},{1,5},{5,1},{2,6},{6,2},{3,7},{7,3},{8,12},{12,8},{9,1... | collective-permute-start | bytes 1572872 | tf_op jit(solution)/shard_map/ppermute | solution.py:716
  381.2 7.4 %collective-permute-start.22 = (bf16[1280,128]{1,0:T(8,128)(2,1)}, bf16[1280,128]{1,0:T(8,128)(2,1)}, u32[]{:S(2)}, u32[]{:S(2)}) collective-permute-start(bf16[1280,128]{1,0:T(8,128)(2,1)} %dynamic-slice_convert_fusion), channel_id=1, source_target_pairs={{0,1},{1,0},{2,3},{3,2},{4,5},{5,4},{6,7},{7,6},{8,9},{9,8},{10,11... | collective-permute-start | bytes 983048 | tf_op jit(solution)/shard_map/ppermute | solution.py:719
  387.0 19.7 %collective-permute-start.21 = (bf16[512,512]{1,0:T(8,128)(2,1)S(1)}, bf16[512,512]{1,0:T(8,128)(2,1)S(1)}, u32[]{:S(2)}, u32[]{:S(2)}) collective-permute-start(bf16[512,512]{1,0:T(8,128)(2,1)S(1)} %slice.569), channel_id=1, source_target_pairs={{0,2},{2,0},{1,3},{3,1},{4,6},{6,4},{5,7},{7,5},{8,10},{10,8},{9,1... | collective-permute-start | bytes 1572872 | tf_op jit(solution)/shard_map/ppermute | solution.py:722
  389.6 15.2 %collective-permute-start.23 = (bf16[640,128]{1,0:T(8,128)(2,1)S(1)}, bf16[640,128]{1,0:T(8,128)(2,1)S(1)}, u32[]{:S(2)}, u32[]{:S(2)}) collective-permute-start(bf16[640,128]{1,0:T(8,128)(2,1)S(1)} %get-tuple-element.116), channel_id=1, source_target_pairs={{0,2},{2,0},{1,3},{3,1},{4,6},{6,4},{5,7},{7,5},{8,10},{10,8},{9,1... | collective-permute-start | bytes 491528 | tf_op jit(solution)/shard_map/ppermute | solution.py:722
  390.2 14.7 %collective-permute-start.25 = (bf16[640,128]{1,0:T(8,128)(2,1)S(1)}, bf16[640,128]{1,0:T(8,128)(2,1)S(1)}, u32[]{:S(2)}, u32[]{:S(2)}) collective-permute-start(bf16[640,128]{1,0:T(8,128)(2,1)S(1)} %get-tuple-element.117), channel_id=1, source_target_pairs={{0,4},{4,0},{1,5},{5,1},{2,6},{6,2},{3,7},{7,3},{8,12},{12,8},{9,1... | collective-permute-start | bytes 491528 | tf_op jit(solution)/shard_map/ppermute | solution.py:716
  405.0 5.9 %collective-permute-start.24 = (bf16[640,128]{1,0:T(8,128)(2,1)S(1)}, bf16[640,128]{1,0:T(8,128)(2,1)S(1)}, u32[]{:S(2)}, u32[]{:S(2)}) collective-permute-start(bf16[640,128]{1,0:T(8,128)(2,1)S(1)} %get-tuple-element.114), channel_id=1, source_target_pairs={{0,4},{4,0},{1,5},{5,1},{2,6},{6,2},{3,7},{7,3},{8,12},{12,8},{9,1... | collective-permute-start | bytes 491528 | tf_op jit(solution)/shard_map/ppermute | solution.py:716
  405.0 5.9 %collective-permute-start.26 = (bf16[640,128]{1,0:T(8,128)(2,1)S(1)}, bf16[640,128]{1,0:T(8,128)(2,1)S(1)}, u32[]{:S(2)}, u32[]{:S(2)}) collective-permute-start(bf16[640,128]{1,0:T(8,128)(2,1)S(1)} %get-tuple-element.115), channel_id=1, source_target_pairs={{0,2},{2,0},{1,3},{3,1},{4,6},{6,4},{5,7},{7,5},{8,10},{10,8},{9,1... | collective-permute-start | bytes 491528 | tf_op jit(solution)/shard_map/ppermute | solution.py:722
  411.1 2.8 collective-permute-start.27
  467.0 18.1 %collective-permute-start.29 = (bf16[1024,1024]{1,0:T(8,128)(2,1)}, bf16[1024,1024]{1,0:T(8,128)(2,1)}, u32[]{:S(2)}, u32[]{:S(2)}) collective-permute-start(bf16[1024,1024]{1,0:T(8,128)(2,1)} %get-tuple-element.71), channel_id=1, source_target_pairs={{0,1},{1,0},{2,3},{3,2},{4,5},{5,4},{6,7},{7,6},{8,9},{9,8},{10,11... | collective-permute-start | bytes 6291464 | tf_op jit(solution)/shard_map/ppermute | solution.py:719
  467.5 21.4 %collective-permute-start.28 = (bf16[1024,1024]{1,0:T(8,128)(2,1)}, bf16[1024,1024]{1,0:T(8,128)(2,1)}, u32[]{:S(2)}, u32[]{:S(2)}) collective-permute-start(bf16[1024,1024]{1,0:T(8,128)(2,1)} %get-tuple-element.69), channel_id=1, source_target_pairs={{0,1},{1,0},{2,3},{3,2},{4,5},{5,4},{6,7},{7,6},{8,9},{9,8},{10,11... | collective-permute-start | bytes 6291464 | tf_op jit(solution)/shard_map/ppermute | solution.py:719
  468.5 75.0 %all-to-all-start.2 = ((bf16[4,608,512]{2,1,0:T(8,128)(2,1)}), bf16[4,608,512]{2,1,0:T(8,128)(2,1)}, u32[]{:S(2)}, u32[]{:S(2)}) async-start(bf16[4,608,512]{2,1,0:T(8,128)(2,1)} %pad_maximum_fusion.1.refs_0_), calls=%async_computation.2 | async-start | bytes 4980736 | tf_op jit(solution)/shard_map/all_to_all | solution.py:705
  473.9 26.1 %collective-permute-start.36 = (bf16[1024,512]{1,0:T(8,128)(2,1)S(1)}, bf16[1024,512]{1,0:T(8,128)(2,1)S(1)}, u32[]{:S(2)}, u32[]{:S(2)}) collective-permute-start(bf16[1024,512]{1,0:T(8,128)(2,1)S(1)} %convert_element_type.379), channel_id=1, source_target_pairs={{0,4},{4,0},{1,5},{5,1},{2,6},{6,2},{3,7},{7,3},{8,12},{12,8},{9,1... | collective-permute-start | bytes 3145736 | tf_op jit(solution)/shard_map/ppermute | solution.py:716
  488.5 33.2 %collective-permute-start.32 = (bf16[512,1024]{1,0:T(8,128)(2,1)S(1)}, bf16[512,1024]{1,0:T(8,128)(2,1)S(1)}, u32[]{:S(2)}, u32[]{:S(2)}) collective-permute-start(bf16[512,1024]{1,0:T(8,128)(2,1)S(1)} %slice.379), channel_id=1, source_target_pairs={{0,4},{4,0},{1,5},{5,1},{2,6},{6,2},{3,7},{7,3},{8,12},{12,8},{9,1... | collective-permute-start | bytes 3145736 | tf_op jit(solution)/shard_map/ppermute | solution.py:716
  492.7 30.9 %collective-permute-start.30 = (bf16[2,512,512]{2,1,0:T(8,128)(2,1)S(1)}, bf16[2,512,512]{2,1,0:T(8,128)(2,1)S(1)}, u32[]{:S(2)}, u32[]{:S(2)}) collective-permute-start(bf16[2,512,512]{2,1,0:T(8,128)(2,1)S(1)} %pad_maximum_fusion.11), channel_id=1, source_target_pairs={{0,2},{2,0},{1,3},{3,1},{4,6},{6,4},{5,7},{7,5},{8,10},{10,8},{9,1... | collective-permute-start | bytes 3145736 | tf_op jit(solution)/shard_map/ppermute | solution.py:722
  522.1 13.3 %collective-permute-start.33 = (bf16[512,512]{1,0:T(8,128)(2,1)S(1)}, bf16[512,512]{1,0:T(8,128)(2,1)S(1)}, u32[]{:S(2)}, u32[]{:S(2)}) collective-permute-start(bf16[512,512]{1,0:T(8,128)(2,1)S(1)} %slice.567), channel_id=1, source_target_pairs={{0,2},{2,0},{1,3},{3,1},{4,6},{6,4},{5,7},{7,5},{8,10},{10,8},{9,1... | collective-permute-start | bytes 1572872 | tf_op jit(solution)/shard_map/ppermute | solution.py:722
  523.8 13.1 %collective-permute-start.31 = (bf16[512,512]{1,0:T(8,128)(2,1)S(1)}, bf16[512,512]{1,0:T(8,128)(2,1)S(1)}, u32[]{:S(2)}, u32[]{:S(2)}) collective-permute-start(bf16[512,512]{1,0:T(8,128)(2,1)S(1)} %fusion.14), channel_id=1, source_target_pairs={{0,4},{4,0},{1,5},{5,1},{2,6},{6,2},{3,7},{7,3},{8,12},{12,8},{9,1... | collective-permute-start | bytes 1572872 | tf_op jit(solution)/shard_map/ppermute | solution.py:716
  540.0 2.8 collective-permute-start.34
  542.8 8.0 %collective-permute-start.35 = (f32[2,512]{1,0:T(2,128)S(1)}, f32[2,512]{1,0:T(2,128)S(1)}, u32[]{:S(2)}, u32[]{:S(2)}) collective-permute-start(f32[2,512]{1,0:T(2,128)S(1)} %add.377), channel_id=1, source_target_pairs={{0,2},{2,0},{1,3},{3,1},{4,6},{6,4},{5,7},{7,5},{8,10},{10,8},{9,1... | collective-permute-start | bytes 12296 | tf_op jit(solution)/shard_map/ppermute | solution.py:722
  547.0 3.7 collective-permute-start.37
  550.4 15.9 %collective-permute-start.40 = (bf16[608,512]{1,0:T(8,128)(2,1)S(1)}, bf16[608,512]{1,0:T(8,128)(2,1)S(1)}, u32[]{:S(2)}, u32[]{:S(2)}) collective-permute-start(bf16[608,512]{1,0:T(8,128)(2,1)S(1)} %get-tuple-element.72), channel_id=1, source_target_pairs={{0,4},{4,0},{1,5},{5,1},{2,6},{6,2},{3,7},{7,3},{8,12},{12,8},{9,1... | collective-permute-start | bytes 1867784 | tf_op jit(solution)/shard_map/ppermute | solution.py:716
  550.8 1.2 collective-permute-start.38
  551.9 4.8 collective-permute-start.39
  (56 other events, 266.2 us)

commit v3 on v2

--- a/solution.py
+++ b/solution.py
@@ -112,14 +112,14 @@
     )(rows, gain.reshape(1, width))
 
 
-def unpacked(window, counts, place):
+def unpacked(window, counts, place, *before):
     slots = len(window)
     count = (slots + 1) // 2
     width = window[0].shape[1]
     starts = [sum(counts[:i]) for i in range(len(counts))]
 
     def kernel(place_ref, *refs):
-        ins, outs = refs[:slots], refs[slots:]
+        ins, outs = refs[:slots], refs[slots + len(before) :]
         wanted = pl.program_id(0) + count - 1 - place_ref[0]
         for slot, ref in enumerate(ins):
 
@@ -133,13 +133,13 @@
         grid_spec=pltpu.PrefetchScalarGridSpec(
             num_scalar_prefetch=1,
             grid=(count,),
-            in_specs=[whole(*window[0].shape) for _ in window],
+            in_specs=[whole(*window[0].shape) for _ in window] + [pl.BlockSpec(memory_space=pl.ANY) for _ in before],
             out_specs=[pl.BlockSpec((1, rows, width), lambda j, place: (j, 0, 0)) for rows in counts],
         ),
         out_shape=[jax.ShapeDtypeStruct((count, rows, width), bf16) for rows in counts],
         cost_estimate=cost(3),
         compiler_params=PARAMS,
-    )(place, *window)
+    )(place, *window, *before)
 
 
 def products(lefts, more_lefts, right, more_right, blocks, width):
@@ -829,12 +829,6 @@
         return lax.all_gather(array, "context")
 
 
-def document_ids(lengths, positions):
-    bounds = jnp.cumsum(lengths, axis=-1)[:, :2]
-    passed = positions[None, :, None] >= bounds[:, None, :]
-    return jnp.sum(passed.astype(jnp.int32), axis=-1)
-
-
 def dot(a, b, out=f32):
     return jnp.dot(a, b, preferred_element_type=f32).astype(out)
 
@@ -890,6 +884,16 @@
     rows_flat = block_input.reshape(seqs * piece, model_width)
     row_block, row_slice = moves.pieces(rows_flat, 0)
     in_x = my_columns(input_proj[:, 0], after(row_slice))
+    bounds = jnp.cumsum(doc_lengths, axis=-1)[:, :2, None, None]
+    position, lane = (lax.broadcasted_iota(jnp.int32, (1, length, LANE), axis) for axis in (1, 2))
+    other = jnp.where(lane < taps, position - lane, position + lane - taps)
+
+    def document(at):
+        return (at >= bounds[:, 0]).astype(jnp.int32) + (at >= bounds[:, 1]).astype(jnp.int32)
+
+    masks = (document(position) == document(other)) & (other >= 0) & (other < length)
+    masks = masks.astype(f32)
+
     vectors = jnp.concatenate(
         [
             mine(select_proj),
@@ -905,11 +909,12 @@
     flat = [in_x, my_columns(step_proj, 0), vectors.reshape(-1, inner), norm_gain.reshape(-1, inner)]
     flat = [jnp.pad(f, ((0, -f.shape[0] % 16), (0, 0))) for f in flat]
     window = line_gather(jnp.concatenate(flat, axis=0), "shards")
-    proj_x, proj_step, vectors, gain = unpacked(window, [f.shape[0] for f in flat], shard[None])
+    proj_x, proj_step, vectors, gain = unpacked(window, [f.shape[0] for f in flat], shard[None], masks)
+    gain = gain[:, : norm_gain.shape[0] // inner].reshape(model_width).astype(f32)
+    normed, inv_rms = moves.normed(rows_flat, row_block, gain)
     proj_x = proj_x.reshape(model_width, inner)
     proj_step = proj_step[:, : step_proj.shape[0]].reshape(rank, inner)
     vectors = vectors[:, : 2 * LANE * part // inner].reshape(inner, 2 * LANE)
-    gain = gain[:, : norm_gain.shape[0] // inner].reshape(model_width).astype(f32)
     proj_select = vectors[:, :selected]
     rest = vectors[:, selected:].astype(f32)
     decay_rate = -jnp.exp(rest[:, taps : taps + states])
@@ -918,9 +923,7 @@
     scan_vec = jnp.concatenate([rest[:, at + 1 : at + 3].T, jnp.zeros((6, inner), f32)], axis=0)
     select_low, select_state = proj_select[:, :rank], proj_select[:, rank:]
 
-    normed, inv_rms = moves.normed(rows_flat, row_block, gain)
     grad_flat = output_grad.reshape(seqs * piece, model_width)
-    grad_block = moves.pieces(grad_flat, after(row_block))[0]
 
     in_z = my_columns(input_proj[:, 1], after(window[len(window) // 2 - 1]))
     out_own = mine(output_proj)
@@ -929,12 +932,6 @@
     others = lax.dynamic_slice_in_dim(others, after(proj_x) * 16, others.shape[0] - 16, 0)
     others = line_gather_at_once(others, "shards")
 
-    document = document_ids(doc_lengths, jnp.arange(length, dtype=jnp.int32))
-    masks = [jnp.pad(document, ((0, 0), (by, 0)), constant_values=-1)[:, :length] for by in range(taps)]
-    masks += [jnp.pad(document, ((0, 0), (0, by)), constant_values=-1)[:, by:] for by in range(taps)]
-    masks = jnp.stack([m == document for m in masks], axis=-1).astype(f32)
-    masks = jnp.pad(masks, ((0, 0), (0, 0), (0, LANE - 2 * taps)))
-
     x_part, values, projected = convolve(
         normed, proj_x, conv_vec, masks, select_low, select_state.T, moves.place, taps
     )
@@ -943,6 +940,7 @@
         return moves.total(packed.reshape(-1, LANE), begin).reshape(packed.shape)
 
     projected = total(projected, 0)
+    grad_block = moves.pieces(grad_flat, after(row_block))[0]
 
     hot = hot_rows()
 
@@ -954,24 +952,16 @@
     )
 
     proj_z = others[:, :depth].reshape(model_width, inner)
-    proj_out = jnp.concatenate(
-        [others[:, depth + i * part : depth + (i + 1) * part] for i in range(model_width // inner)], axis=-1
-    ).reshape(inner, model_width)
+    proj_out = [others[:, depth + i * part : depth + (i + 1) * part] for i in range(model_width // inner)]
+    proj_out = jnp.concatenate(proj_out, axis=-1).reshape(inner, model_width)
     grad_all = moves.pieces_done(grad_flat, grad_block)
     gated, grad_z, grad_ssm = gates(normed, grad_all, proj_z, proj_out, ssm_out, moves.place)
 
     def weight_grad(lefts, rights):
         return sum(t_dot(a, b) for a, b in zip(lefts, rights)).astype(bf16)
 
-    early = [weight_grad(normed, grad_z).reshape(shards, depth, inner)]
-    for i in range(model_width // inner):
-        columns = [g[:, i * inner : (i + 1) * inner] for g in grad_all]
-        early.append(weight_grad(gated, columns).reshape(shards, part, inner))
-    early = line_scatter(jnp.concatenate(early, axis=1), "shards")
-    grad_in_z = early[:depth]
-    early_pair = moves.both(early.astype(bf16))
-    in_z_pair, out_pair = early_pair[:, :depth], early_pair[:, depth:]
-
+    early = lax.all_to_all(weight_grad(normed, grad_z).reshape(shards, depth, inner), "shards", 0, 0)
+    middle = lax.all_to_all(weight_grad(gated, grad_all).reshape(shards, part, model_width), "shards", 0, 0)
     def chosen(weights, blocks, axis, begin=0):
         return jnp.concatenate(
             [lax.dynamic_slice_in_dim(weights, (b + begin) * share_width, share_width, axis) for b in blocks], axis
@@ -1000,12 +990,16 @@
     grad_decay_log = grad_decay.T * decay_rate
     step_low = projected[:, :, :rank].reshape(tokens, rank).astype(bf16)
     grad_step_proj = t_dot(step_low, grad_step_pre.reshape(tokens, inner))
-    partial_grad = total(partial_grad, after(*out_sums_2))
+    pulled = after(early, partial_grad, *out_sums_2)
+    grad_in_z = jnp.sum(early.astype(f32), axis=0) + pulled.astype(f32)
+    z_pair = moves.both(grad_in_z.astype(bf16))
+    partial_grad = total(partial_grad, pulled)
+
     grad_x, conv_sums, grad_selected = convolve_back(
         partial_grad,
         grad_direct,
         x_part,
-        conv_vec + after(block_output, early).astype(f32),
+        conv_vec + after(block_output, partial_grad).astype(f32),
         masks,
         select_low,
         jnp.pad(select_state, ((0, 0), (0, LANE - select_state.shape[1]))),
@@ -1025,6 +1019,9 @@
         ],
         axis=1,
     ).astype(bf16)
+    sent = after(middle, grad_x[0])
+    small = small + sent.astype(bf16)
+    out_pair = moves.both((jnp.sum(middle.astype(f32), axis=0) + sent.astype(f32)).astype(bf16))
     small = jnp.pad(small, ((0, 0), (0, 2 * LANE - small.shape[1])))
     late_local = jnp.concatenate(
         [
@@ -1034,7 +1031,7 @@
         ],
         axis=1,
     )
-    begin = after(late_local)
+    begin = after(late_local, z_pair)
 
     def normed_part(blocks):
         blocks = jnp.stack([jnp.asarray(b, jnp.int32) + begin for b in blocks])
@@ -1048,7 +1045,7 @@
     grad_share = lax.dynamic_slice_in_dim(output_grad, own_columns, share_width, 2).astype(f32)
     input_grad = grad_share + inv_rms * (weighted - unit_share * (row_dots / model_width))
 
-    late = line_scatter(late_local, "shards")+ after(grad_normed, early_pair).astype(f32)
+    late = line_scatter(late_local, "shards") + after(grad_normed, z_pair, out_pair).astype(f32)
     grad_in_x = late[:depth]
     gain_part = jnp.sum(in_x.astype(f32) * grad_in_x, axis=1) + jnp.sum(in_z.astype(f32) * grad_in_z, axis=1)
     grad_gain = moves.vector_total(gain_part) / norm_gain.astype(f32)
@@ -1058,11 +1055,10 @@
         return jnp.moveaxis(pair, 0, -2).reshape(pair.shape[1], -1)
 
     late = moves.both(late.astype(bf16))
-    grad_in = interleaved(late, early_pair, depth, part)
+    grad_in = interleaved(late, z_pair, depth, part)
     grad_step_proj = columns_of(late[:, depth : depth + step_proj.shape[0]])
     small = late[:, depth + step_proj.shape[0] :].reshape(contexts * part, 2 * LANE).astype(f32)
-    grad_out_proj = [out_pair[:, i * part : (i + 1) * part] for i in range(model_width // inner)]
-    grad_out_proj = jnp.concatenate(grad_out_proj, axis=-1).reshape(contexts * part, model_width).astype(f32)
+    grad_out_proj = out_pair.reshape(contexts * part, model_width).astype(f32)
     at = selected + taps + states
     return (
         block_output,

time: 587 us -> 571 us (0.973)
  waiting for transfers between devices: 133 us -> 118 us
  local copies, waits for them, and re-layouts: 71.5 us -> 56.9 us
  matrix products: 32.7 us -> 39.2 us
    ppermute x10, waiting for transfers between devices: 34.9 us -> 13 us  [far(): return lax.ppermute(array, 'tensor', [(0, 2), (2, 0), (1, 3), (3, 1)])]
    all_to_all x0 -> x2, starting transfers between devices: none -> 10.9 us  [the longest x1 5.62 us: on_device(): lax.all_to_all(weight_grad(normed, grad_z).reshape(shards, depth, inner),...]
    another operation x8 -> x0, local copies, waits for them, and re-layouts: 10.3 us -> none  [on_device(): masks = jnp.stack([m == document for m in masks], axis=-1).astype(f32)]
    ppermute x13 -> x14, waiting for transfers between devices: 61.4 us -> 69.3 us  [across(): return lax.ppermute(array, 'context', [(0, 1), (1, 0)])]
    unnamed x145 -> x151, local copies, waits for them, and re-layouts: 15.8 us -> 12.6 us
    dot_general x14 -> x8, matrix products: 27.7 us -> 30.2 us  [t_dot(): lax.dot_general(a, b, (((0,), (0,)), ((), ())), preferred_element_type=f32)]
    ppermute x13 -> x14, starting transfers between devices: 16.3 us -> 15.2 us  [across(): return lax.ppermute(array, 'context', [(0, 1), (1, 0)])]
  transfers between devices with their start and end apart: 44 -> 46, of which waited for: 18 -> 21; matrix products, arithmetic and copies ran while one was open for 19% -> 20% of each run, Pallas kernels for 27% -> 31%
where the time goes in v3:
time: 571 us; the launch traced here: 563 us
  Pallas kernels  208 us (36%)
  waiting for transfers between devices  118 us (21%)
  starting transfers between devices  64.1 us (11%)
  other arithmetic  60.4 us (11%)
  local copies, waits for them, and re-layouts  56.9 us (10%)
  matrix products  39.2 us (7%)
  between operations  16.1 us (3%)
    pallas_call x1, Pallas kernels, scan_backward(): pl.pallas_call(functools.partial(backward_kernel, S, G), grid=(T // LANE,...  69.6 us
    ppermute x14, waiting for transfers between devices, across(): return lax.ppermute(array, 'context', [(0, 1), (1, 0)])  69.3 us
    pallas_call x1, Pallas kernels, scan_forward(): pl.pallas_call(functools.partial(forward_kernel, S, G), grid=(T // LANE,)...  33.6 us
    ppermute x3, waiting for transfers between devices, line_gather(): lax.ppermute(left, axis, [(i, i - 1) for i in range(1, count - step + 1)])  32 us
    dot_general x8, matrix products, t_dot(): lax.dot_general(a, b, (((0,), (0,)), ((), ())), preferred_element_type=f32)  30.2 us
    pallas_call x1, Pallas kernels, gates(): pl.pallas_call(kernel, grid_spec=pltpu.PrefetchScalarGridSpec(num_scalar_...  19 us
    pallas_call x2, Pallas kernels, products(): pl.pallas_call(kernel, grid_spec=pltpu.PrefetchScalarGridSpec(num_scalar_...  18.9 us
    pallas_call x1, Pallas kernels, convolve_back(): pl.pallas_call(kernel, grid_spec=pltpu.PrefetchScalarGridSpec(num_scalar_...  16.2 us
  transfers between devices with their start and end apart: 46, of which 21 were waited for; matrix products, arithmetic and copies ran while one was open for 20% of the time, Pallas kernels for 31%

profile of v3, /device:TPU:0, one launch (start us, length us, event | category | flops | bytes accessed | tf_op | source)
XLA Modules:
  0.0 562.6 jit_solution(13777802797670375499)
XLA Ops:
  0.7 3.2 constant_dynamic-slice_fusion.21.refs_0_
  3.9 3.0 collective-permute-start.6
  10.2 6.8 %fusion.48 = (bf16[512,1,1024]{2,1,0:T(2,128)(2,1)}, bf16[512,1,1024]{2,1,0:T(2,128)(2,1)}) fusion(bf16[512,2,1024]{2,1,0:T(2,128)(2,1)} %param.17), kind=kLoop, calls=%fused_computation.213 | loop fusion | bytes 4194304 | tf_op jit(solution)/shard_map/slice | solution.py:928
  21.9 4.6 collective-permute-start
  26.9 11.4 %collective-permute-done.3.refs_4_ = bf16[624,512]{1,0:T(8,128)(2,1)} collective-permute-done((bf16[624,512]{1,0:T(8,128)(2,1)S(1)}, bf16[624,512]{1,0:T(8,128)(2,1)}, u32[]{:S(2)}, u32[]{:S(2)}) %collective-permute-start.3) | collective-permute-done | bytes 639008 | tf_op jit(solution)/shard_map/ppermute | solution.py:694
  48.7 6.8 %collective-permute-done.4.refs_5_ = bf16[624,512]{1,0:T(8,128)(2,1)} collective-permute-done((bf16[624,512]{1,0:T(8,128)(2,1)}, bf16[624,512]{1,0:T(8,128)(2,1)}, u32[]{:S(2)}, u32[]{:S(2)}) %collective-permute-start.4) | collective-permute-done | bytes 639008 | tf_op jit(solution)/shard_map/ppermute | solution.py:694
  57.8 13.8 %collective-permute-done.5.refs_6_ = bf16[624,512]{1,0:T(8,128)(2,1)S(1)} collective-permute-done((bf16[624,512]{1,0:T(8,128)(2,1)}, bf16[624,512]{1,0:T(8,128)(2,1)S(1)}, u32[]{:S(2)}, u32[]{:S(2)}) %collective-permute-start.5) | collective-permute-done | bytes 639008 | tf_op jit(solution)/shard_map/ppermute | solution.py:694
  72.7 4.2 shard_map.221
  80.4 7.0 %all-to-all-start = ((bf16[4,1024,512]{2,1,0:T(8,128)(2,1)}), bf16[4,1024,512]{2,1,0:T(8,128)(2,1)}, u32[]{:S(2)}, u32[]{:S(2)}) async-start(bf16[4,1024,512]{2,1,0:T(8,128)(2,1)} %broadcast_in_dim.45), calls=%async_computation | async-start | bytes 8388608 | tf_op jit(solution)/shard_map/all_to_all | solution.py:701
  90.6 5.5 shard_map.222
  98.1 3.2 constant_dynamic-slice_fusion.9
  101.9 7.5 %shard_map.223.refs_1_ = bf16[1024,2048]{1,0:T(8,128)(2,1)} custom-call(s32[1]{0:T(128)} %bitcast.13.place_ref, bf16[512,2048]{1,0:T(8,128)(2,1)} %copy-done.17, bf16[512,2048]{1,0:T(8,128)(2,1)} %collective-permute-done.7.second_ref, f32[1,2048]{1,0:T(1,128)} %bitcast.219), custom_call_target="tpu_custom_call" | custom-call | flops 460000000 | bytes 1440000 | tf_op jit(solution)/shard_map/pallas_call | solution.py:79
  109.3 15.2 %shard_map.228 = (bf16[2,1024,512]{2,1,0:T(8,128)(2,1)}, bf16[2,1024,512]{2,1,0:T(8,128)(2,1)}, f32[2,8,160,128]{3,2,1,0:T(8,128)}) custom-call(s32[1]{0:T(128)} %bitcast.place_ref, bf16[1024,2048]{1,0:T(8,128)(2,1)} %get-tuple-element.43.refs_0_, bf16[1024,2048]{1,0:T(8,128)(2,1)} %shard_map.223.refs_1_, bf16[2048,512]{1,0:T(8,128)(2,1)} %bitcast.167, ...), custom_call_target="tpu_custom_call" | custom-call | flops 1035000000 | bytes 3240000 | tf_op jit(solution)/shard_map/pallas_call | solution.py:270
  131.9 2.9 collective-permute-done.11
  134.8 15.8 %collective-permute-done.13 = bf16[640,128]{1,0:T(8,128)(2,1)S(1)} collective-permute-done((bf16[640,128]{1,0:T(8,128)(2,1)S(1)}, bf16[640,128]{1,0:T(8,128)(2,1)S(1)}, u32[]{:S(2)}, u32[]{:S(2)}) %collective-permute-start.13) | collective-permute-done | bytes 163872 | tf_op jit(solution)/shard_map/ppermute | solution.py:716
  160.6 33.6 %shard_map.229 = (f32[2,1024,512]{2,1,0:T(8,128)}, f32[2,1024,512]{2,1,0:T(8,128)}, f32[8,128,128]{2,1,0:T(8,128)}) custom-call(f32[2,8,160,128]{3,2,1,0:T(8,128)} %bitcast.190, bf16[2,1024,512]{2,1,0:T(8,128)(2,1)} %get-tuple-element.47.u_ref, f32[2,1024,128]{2,1,0:T(8,128)} %and_convert_fusion.refs_7_.refs_4_.masks_ref, bf16[128,512]{1,0:T(8,128)(2,1)} %bitcast.229, ...), custom_call_target="tpu_custom_call" | custom-call | flops 3449999872 | bytes 10800000 | tf_op jit(solution)/shard_map/pallas_call | solution.py:624
  194.3 7.1 %shard_map.225.refs_3_ = bf16[1024,2048]{1,0:T(8,128)(2,1)} custom-call(s32[1]{0:T(128)} %bitcast.13.place_ref, bf16[512,2048]{1,0:T(8,128)(2,1)} %collective-permute-done.8.first_ref, bf16[512,2048]{1,0:T(8,128)(2,1)} %collective-permute-done.9.second_ref), custom_call_target="tpu_custom_call" | custom-call | flops 460000000 | bytes 1440000 | tf_op jit(solution)/shard_map/pallas_call | solution.py:79
  204.7 3.0 slice.262
  207.8 19.0 %shard_map.230 = (bf16[1024,512]{1,0:T(8,128)(2,1)}, bf16[1024,512]{1,0:T(8,128)(2,1)}, bf16[1024,512]{1,0:T(8,128)(2,1)}, bf16[1024,512]{1,0:T(8,128)(2,1)}, f32[2,1024,512]{2,1,0:T(8,128)}) custom-call(s32[1]{0:T(128)} %bitcast.place_ref, bf16[1024,2048]{1,0:T(8,128)(2,1)} %get-tuple-element.43.refs_0_, bf16[1024,2048]{1,0:T(8,128)(2,1)} %shard_map.223.refs_1_, ...), custom_call_target="tpu_custom_call" | custom-call | flops 1610000000 | bytes 5040000 | tf_op jit(solution)/shard_map/pallas_call | solution.py:313
  230.7 2.6 convolution_convert_fusion
  236.4 3.7 add_convert_fusion.2
  240.1 5.6 all-to-all-start.1
  245.8 2.6 fusion.11
  253.1 3.7 add_convert_fusion
  256.7 4.6 fusion.46
  264.6 4.5 convert_add_fusion.3.refs_0_
  276.1 69.6 %shard_map.232 = (bf16[2,1024,512]{2,1,0:T(8,128)(2,1)}, f32[2,1024,512]{2,1,0:T(8,128)}, f32[2,8,160,128]{3,2,1,0:T(8,128)}, f32[16,512]{1,0:T(8,128)}, f32[8,512]{1,0:T(8,128)}) custom-call(f32[2,8,160,128]{3,2,1,0:T(8,128)} %bitcast.191, bf16[2,1024,512]{2,1,0:T(8,128)(2,1)} %get-tuple-element.47.u_ref, f32[2,1024,512]{2,1,0:T(8,128)} %get-tuple-element.53.step_ref, ...), custom_call_target="tpu_custom_call" | custom-call | flops 9774999552 | bytes 30600000 | tf_op jit(solution)/shard_map/pallas_call | solution.py:649
  347.5 2.9 convolution_convert_fusion.2
  350.4 2.7 fusion.45
  358.3 5.3 all-to-all-start.2
  367.0 3.2 convert_add_fusion.5
  378.9 4.1 collective-permute-done.23
  383.0 9.5 %collective-permute-done.25 = bf16[640,128]{1,0:T(8,128)(2,1)S(1)} collective-permute-done((bf16[640,128]{1,0:T(8,128)(2,1)S(1)}, bf16[640,128]{1,0:T(8,128)(2,1)S(1)}, u32[]{:S(2)}, u32[]{:S(2)}) %collective-permute-start.25) | collective-permute-done | bytes 163872 | tf_op jit(solution)/shard_map/ppermute | solution.py:716
  403.5 16.2 %shard_map.235 = (bf16[1024,512]{1,0:T(8,128)(2,1)}, bf16[1024,512]{1,0:T(8,128)(2,1)}, f32[8,512]{1,0:T(8,128)}, bf16[2,1024,256]{2,1,0:T(8,128)(2,1)}) custom-call(s32[1]{0:T(128)} %bitcast.place_ref, f32[2,8,160,128]{3,2,1,0:T(8,128)} %bitcast.183, f32[2,1024,512]{2,1,0:T(8,128)} %get-tuple-element.59.d_ref, ...), custom_call_target="tpu_custom_call" | custom-call | flops 1150000000 | bytes 3600000 | tf_op jit(solution)/shard_map/pallas_call | solution.py:385
  420.5 6.9 %fusion.54 = f32[2048,512]{1,0:T(8,128)} fusion(bf16[1024,2048]{1,0:T(8,128)(2,1)} %get-tuple-element.43.refs_0_, bf16[1024,512]{1,0:T(8,128)(2,1)} %get-tuple-element.61.refs_1_.refs_0_), kind=kOutput, calls=%fused_computation.219 | convolution fusion | flops 2147483648 | bytes 9437184 | tf_op jit(solution)/shard_map/dot_general | solution.py:841
  433.4 5.9 %add_convert_fusion.1 = bf16[2048,512]{1,0:T(8,128)(2,1)S(1)} fusion(f32[2048,512]{1,0:T(8,128)} %fusion.54, bf16[1024,2048]{1,0:T(8,128)(2,1)} %shard_map.223.refs_1_, bf16[1024,512]{1,0:T(8,128)(2,1)S(1)} %copy-done.21), kind=kOutput, calls=%fused_computation.6 | convolution fusion | flops 2149580800 | bytes 11534336 | tf_op jit(solution)/shard_map/dot_general | solution.py:841
  444.6 9.5 %shard_map.239 = (bf16[1024,1024]{1,0:T(8,128)(2,1)}, bf16[1024,1024]{1,0:T(8,128)(2,1)}) custom-call(s32[2]{0:T(128)} %get-tuple-element.138.blocks_ref, bf16[1024,512]{1,0:T(8,128)(2,1)} %get-tuple-element.61.refs_1_.refs_0_, bf16[1024,512]{1,0:T(8,128)(2,1)} %get-tuple-element.62.refs_1_, bf16[1024,512]{1,0:T(8,128)(2,1)} %get-tuple-element.57.refs_2_, ...), custom_call_target="tpu_custom_call" | custom-call | flops 575000000 | bytes 1800000 | tf_op jit(solution)/shard_map/pallas_call | solution.py:157
  455.6 5.3 all-to-all-start.3
  461.0 9.4 %shard_map.238 = (bf16[1024,1024]{1,0:T(8,128)(2,1)}, bf16[1024,1024]{1,0:T(8,128)(2,1)}) custom-call(s32[2]{0:T(128)} %get-tuple-element.137.blocks_ref, bf16[1024,512]{1,0:T(8,128)(2,1)} %get-tuple-element.61.refs_1_.refs_0_, bf16[1024,512]{1,0:T(8,128)(2,1)} %get-tuple-element.62.refs_1_, bf16[1024,512]{1,0:T(8,128)(2,1)} %get-tuple-element.57.refs_2_, ...), custom_call_target="tpu_custom_call" | custom-call | flops 575000000 | bytes 1800000 | tf_op jit(solution)/shard_map/pallas_call | solution.py:157
  470.4 2.7 convert_add_fusion
  481.1 18.2 %collective-permute-done.33 = bf16[512,1024]{1,0:T(8,128)(2,1)S(1)} collective-permute-done((bf16[512,1024]{1,0:T(8,128)(2,1)S(1)}, bf16[512,1024]{1,0:T(8,128)(2,1)S(1)}, u32[]{:S(2)}, u32[]{:S(2)}) %collective-permute-start.33) | collective-permute-done | bytes 1048608 | tf_op jit(solution)/shard_map/ppermute | solution.py:716
  504.9 5.6 collective-permute-done.37
  510.6 3.0 collective-permute-done.34
  513.8 6.8 %collective-permute-done.32 = bf16[512,512]{1,0:T(8,128)(2,1)S(1)} collective-permute-done((bf16[512,512]{1,0:T(8,128)(2,1)S(1)}, bf16[512,512]{1,0:T(8,128)(2,1)S(1)}, u32[]{:S(2)}, u32[]{:S(2)}) %collective-permute-start.32) | collective-permute-done | bytes 524320 | tf_op jit(solution)/shard_map/ppermute | solution.py:716
  521.1 2.6 fusion.2
  536.5 3.5 fusion.5
  540.6 8.5 %collective-permute-done.41 = bf16[608,512]{1,0:T(8,128)(2,1)S(1)} collective-permute-done((bf16[608,512]{1,0:T(8,128)(2,1)S(1)}, bf16[608,512]{1,0:T(8,128)(2,1)S(1)}, u32[]{:S(2)}, u32[]{:S(2)}) %collective-permute-start.41) | collective-permute-done | bytes 622624 | tf_op jit(solution)/shard_map/ppermute | solution.py:716
  555.9 6.5 %shard_map.241 = f32[512,2,1024]{2,1,0:T(2,128)} custom-call(bf16[2,608,512]{2,1,0:T(8,128)(2,1)} %pad_maximum_fusion.4.a_ref, bf16[2,512,512]{2,1,0:T(8,128)(2,1)} %pad_maximum_fusion.10.refs_1_.b_ref), custom_call_target="tpu_custom_call" | custom-call | flops 575000000 | bytes 1800000 | tf_op jit(solution)/shard_map/pallas_call | solution.py:183
  (377 shorter events, 137.7 us)
Async XLA Ops:
  3.9 53.8 %collective-permute-start.6 = (bf16[512,2048]{1,0:T(8,128)(2,1)}, bf16[512,2048]{1,0:T(8,128)(2,1)S(1)}, u32[]{:S(2)}, u32[]{:S(2)}) collective-permute-start(bf16[512,2048]{1,0:T(8,128)(2,1)} %constant_dynamic-slice_fusion.21.refs_0_), channel_id=1, source_target_pairs={{0,4},{4,0},{1,5},{5,1},{2,6},{6,2},{3,7},{7,3},{8,12},{12,8},{9,1... | collective-permute-start | bytes 6291464 | tf_op jit(solution)/shard_map/ppermute | solution.py:716
  20.5 28.0 %copy-start.25 = (bf16[624,512]{1,0:T(8,128)(2,1)}, bf16[624,512]{1,0:T(8,128)(2,1)S(1)}, u32[]{:S(2)}) copy-start(bf16[624,512]{1,0:T(8,128)(2,1)S(1)} %fusion.13.refs_3_) | copy-start | bytes 1916932
  20.5 17.8 %collective-permute-start.3 = (bf16[624,512]{1,0:T(8,128)(2,1)S(1)}, bf16[624,512]{1,0:T(8,128)(2,1)}, u32[]{:S(2)}, u32[]{:S(2)}) collective-permute-start(bf16[624,512]{1,0:T(8,128)(2,1)S(1)} %fusion.13.refs_3_), channel_id=1, source_target_pairs={{8,0},{16,8},{24,16},{9,1},{17,9},{25,17},{10,2},{18,10},{26,18},{... | collective-permute-start | bytes 1916936 | tf_op jit(solution)/shard_map/ppermute | solution.py:694
  21.9 17.8 %collective-permute-start = (bf16[624,512]{1,0:T(8,128)(2,1)S(1)}, bf16[624,512]{1,0:T(8,128)(2,1)S(1)}, u32[]{:S(2)}, u32[]{:S(2)}) collective-permute-start(bf16[624,512]{1,0:T(8,128)(2,1)S(1)} %fusion.13.refs_3_), channel_id=1, source_target_pairs={{0,8},{8,16},{16,24},{1,9},{9,17},{17,25},{2,10},{10,18},{18,26},{... | collective-permute-start | bytes 1916936 | tf_op jit(solution)/shard_map/ppermute | solution.py:693
  38.4 17.1 %collective-permute-start.4 = (bf16[624,512]{1,0:T(8,128)(2,1)}, bf16[624,512]{1,0:T(8,128)(2,1)}, u32[]{:S(2)}, u32[]{:S(2)}) collective-permute-start(bf16[624,512]{1,0:T(8,128)(2,1)} %collective-permute-done.3.refs_4_), channel_id=1, source_target_pairs={{8,0},{16,8},{9,1},{17,9},{10,2},{18,10},{11,3},{19,11},{12,4},{20... | collective-permute-start | bytes 1916936 | tf_op jit(solution)/shard_map/ppermute | solution.py:694
  39.7 17.1 %collective-permute-start.1 = (bf16[624,512]{1,0:T(8,128)(2,1)S(1)}, bf16[624,512]{1,0:T(8,128)(2,1)}, u32[]{:S(2)}, u32[]{:S(2)}) collective-permute-start(bf16[624,512]{1,0:T(8,128)(2,1)S(1)} %collective-permute-done.refs_2_.refs_0_), channel_id=1, source_target_pairs={{8,16},{16,24},{9,17},{17,25},{10,18},{18,26},{11,19},{19,27},{12,... | collective-permute-start | bytes 1916936 | tf_op jit(solution)/shard_map/ppermute | solution.py:693
  55.5 16.1 %collective-permute-start.5 = (bf16[624,512]{1,0:T(8,128)(2,1)}, bf16[624,512]{1,0:T(8,128)(2,1)S(1)}, u32[]{:S(2)}, u32[]{:S(2)}) collective-permute-start(bf16[624,512]{1,0:T(8,128)(2,1)} %collective-permute-done.4.refs_5_), channel_id=1, source_target_pairs={{8,0},{9,1},{10,2},{11,3},{12,4},{13,5},{14,6},{15,7}} | collective-permute-start | bytes 1916936 | tf_op jit(solution)/shard_map/ppermute | solution.py:694
  56.8 14.8 %collective-permute-start.2 = (bf16[624,512]{1,0:T(8,128)(2,1)}, bf16[624,512]{1,0:T(8,128)(2,1)S(1)}, u32[]{:S(2)}, u32[]{:S(2)}) collective-permute-start(bf16[624,512]{1,0:T(8,128)(2,1)} %collective-permute-done.1.refs_1_), channel_id=1, source_target_pairs={{16,24},{17,25},{18,26},{19,27},{20,28},{21,29},{22,30},{23,31}} | collective-permute-start | bytes 1916936 | tf_op jit(solution)/shard_map/ppermute | solution.py:693
  57.7 44.2 %collective-permute-start.7 = (bf16[512,2048]{1,0:T(8,128)(2,1)S(1)}, bf16[512,2048]{1,0:T(8,128)(2,1)}, u32[]{:S(2)}, u32[]{:S(2)}) collective-permute-start(bf16[512,2048]{1,0:T(8,128)(2,1)S(1)} %collective-permute-done.6.first_ref.refs_0_), channel_id=1, source_target_pairs={{0,1},{1,0},{2,3},{3,2},{4,5},{5,4},{6,7},{7,6},{8,9},{9,8},{10,11... | collective-permute-start | bytes 6291464 | tf_op jit(solution)/shard_map/ppermute | solution.py:719
  80.4 121.0 %all-to-all-start = ((bf16[4,1024,512]{2,1,0:T(8,128)(2,1)}), bf16[4,1024,512]{2,1,0:T(8,128)(2,1)}, u32[]{:S(2)}, u32[]{:S(2)}) async-start(bf16[4,1024,512]{2,1,0:T(8,128)(2,1)} %broadcast_in_dim.45), calls=%async_computation | async-start | bytes 8388608 | tf_op jit(solution)/shard_map/all_to_all | solution.py:701
  101.4 52.3 %collective-permute-start.8 = (bf16[512,2048]{1,0:T(8,128)(2,1)}, bf16[512,2048]{1,0:T(8,128)(2,1)}, u32[]{:S(2)}, u32[]{:S(2)}) collective-permute-start(bf16[512,2048]{1,0:T(8,128)(2,1)} %constant_dynamic-slice_fusion.9), channel_id=1, source_target_pairs={{0,4},{4,0},{1,5},{5,1},{2,6},{6,2},{3,7},{7,3},{8,12},{12,8},{9,1... | collective-permute-start | bytes 6291464 | tf_op jit(solution)/shard_map/ppermute | solution.py:716
  125.6 1.7 collective-permute-start.10
  128.5 6.3 %collective-permute-start.11 = (bf16[640,128]{1,0:T(8,128)(2,1)S(1)}, bf16[640,128]{1,0:T(8,128)(2,1)S(1)}, u32[]{:S(2)}, u32[]{:S(2)}) collective-permute-start(bf16[640,128]{1,0:T(8,128)(2,1)S(1)} %get-tuple-element.124), channel_id=1, source_target_pairs={{0,2},{2,0},{1,3},{3,1},{4,6},{6,4},{5,7},{7,5},{8,10},{10,8},{9,1... | collective-permute-start | bytes 491528 | tf_op jit(solution)/shard_map/ppermute | solution.py:722
  130.1 20.5 %collective-permute-start.13 = (bf16[640,128]{1,0:T(8,128)(2,1)S(1)}, bf16[640,128]{1,0:T(8,128)(2,1)S(1)}, u32[]{:S(2)}, u32[]{:S(2)}) collective-permute-start(bf16[640,128]{1,0:T(8,128)(2,1)S(1)} %get-tuple-element.125), channel_id=1, source_target_pairs={{0,4},{4,0},{1,5},{5,1},{2,6},{6,2},{3,7},{7,3},{8,12},{12,8},{9,1... | collective-permute-start | bytes 491528 | tf_op jit(solution)/shard_map/ppermute | solution.py:716
  150.7 5.4 collective-permute-start.12
  151.3 5.3 collective-permute-start.14
  153.6 40.7 %collective-permute-start.9 = (bf16[512,2048]{1,0:T(8,128)(2,1)}, bf16[512,2048]{1,0:T(8,128)(2,1)}, u32[]{:S(2)}, u32[]{:S(2)}) collective-permute-start(bf16[512,2048]{1,0:T(8,128)(2,1)} %collective-permute-done.8.first_ref), channel_id=1, source_target_pairs={{0,1},{1,0},{2,3},{3,2},{4,5},{5,4},{6,7},{7,6},{8,9},{9,8},{10,11... | collective-permute-start | bytes 6291464 | tf_op jit(solution)/shard_map/ppermute | solution.py:719
  156.7 2.5 collective-permute-start.15
  233.3 23.5 %collective-permute-start.17 = (bf16[1024,1024]{1,0:T(8,128)(2,1)}, bf16[1024,1024]{1,0:T(8,128)(2,1)}, u32[]{:S(2)}, u32[]{:S(2)}) collective-permute-start(bf16[1024,1024]{1,0:T(8,128)(2,1)} %convolution_convert_fusion), channel_id=1, source_target_pairs={{0,1},{1,0},{2,3},{3,2},{4,5},{5,4},{6,7},{7,6},{8,9},{9,8},{10,11... | collective-permute-start | bytes 6291464 | tf_op jit(solution)/shard_map/ppermute | solution.py:719
  233.8 30.8 %collective-permute-start.16 = (bf16[1024,1024]{1,0:T(8,128)(2,1)}, bf16[1024,1024]{1,0:T(8,128)(2,1)}, u32[]{:S(2)}, u32[]{:S(2)}) collective-permute-start(bf16[1024,1024]{1,0:T(8,128)(2,1)} %convolution_convert_fusion.1), channel_id=1, source_target_pairs={{0,1},{1,0},{2,3},{3,2},{4,5},{5,4},{6,7},{7,6},{8,9},{9,8},{10,11... | collective-permute-start | bytes 6291464 | tf_op jit(solution)/shard_map/ppermute | solution.py:719
  240.1 116.8 %all-to-all-start.1 = ((bf16[4,512,512]{2,1,0:T(8,128)(2,1)}), bf16[4,512,512]{2,1,0:T(8,128)(2,1)S(1)}, u32[]{:S(2)}, u32[]{:S(2)}) async-start(bf16[4,512,512]{2,1,0:T(8,128)(2,1)} %bitcast.192), calls=%async_computation.1 | async-start | bytes 4194304 | tf_op jit(solution)/shard_map/all_to_all | solution.py:963
  262.5 90.6 %collective-permute-start.20 = (bf16[512,1024]{1,0:T(8,128)(2,1)}, bf16[512,1024]{1,0:T(8,128)(2,1)}, u32[]{:S(2)}, u32[]{:S(2)}) collective-permute-start(bf16[512,1024]{1,0:T(8,128)(2,1)} %slice.283), channel_id=1, source_target_pairs={{0,4},{4,0},{1,5},{5,1},{2,6},{6,2},{3,7},{7,3},{8,12},{12,8},{9,1... | collective-permute-start | bytes 3145736 | tf_op jit(solution)/shard_map/ppermute | solution.py:716
  274.6 75.9 %collective-permute-start.18 = (bf16[2,512,512]{2,1,0:T(8,128)(2,1)}, bf16[2,512,512]{2,1,0:T(8,128)(2,1)}, u32[]{:S(2)}, u32[]{:S(2)}) collective-permute-start(bf16[2,512,512]{2,1,0:T(8,128)(2,1)} %pad_maximum_fusion.9), channel_id=1, source_target_pairs={{0,2},{2,0},{1,3},{3,1},{4,6},{6,4},{5,7},{7,5},{8,10},{10,8},{9,1... | collective-permute-start | bytes 3145736 | tf_op jit(solution)/shard_map/ppermute | solution.py:722
  276.1 71.5 %copy-start.29 = (bf16[2,8,128,128]{3,2,1,0:T(8,128)(2,1)S(1)}, bf16[2,8,128,128]{3,2,1,0:T(8,128)(2,1)}, u32[]{:S(2)}) copy-start(bf16[2,8,128,128]{3,2,1,0:T(8,128)(2,1)} %slice.422) | copy-start | bytes 1572868
  353.2 13.8 %collective-permute-start.19 = (bf16[512,512]{1,0:T(8,128)(2,1)}, bf16[512,512]{1,0:T(8,128)(2,1)}, u32[]{:S(2)}, u32[]{:S(2)}) collective-permute-start(bf16[512,512]{1,0:T(8,128)(2,1)} %get-tuple-element.78), channel_id=1, source_target_pairs={{0,4},{4,0},{1,5},{5,1},{2,6},{6,2},{3,7},{7,3},{8,12},{12,8},{9,1... | collective-permute-start | bytes 1572872 | tf_op jit(solution)/shard_map/ppermute | solution.py:716
  356.4 19.0 %collective-permute-start.21 = (bf16[512,512]{1,0:T(8,128)(2,1)}, bf16[512,512]{1,0:T(8,128)(2,1)}, u32[]{:S(2)}, u32[]{:S(2)}) collective-permute-start(bf16[512,512]{1,0:T(8,128)(2,1)} %slice.423), channel_id=1, source_target_pairs={{0,2},{2,0},{1,3},{3,1},{4,6},{6,4},{5,7},{7,5},{8,10},{10,8},{9,1... | collective-permute-start | bytes 1572872 | tf_op jit(solution)/shard_map/ppermute | solution.py:722
  358.3 69.1 %all-to-all-start.2 = ((bf16[4,128,2048]{2,1,0:T(8,128)(2,1)}), bf16[4,128,2048]{2,1,0:T(8,128)(2,1)S(1)}, u32[]{:S(2)}, u32[]{:S(2)}) async-start(bf16[4,128,2048]{2,1,0:T(8,128)(2,1)} %bitcast.185), calls=%async_computation.2 | async-start | bytes 4194304 | tf_op jit(solution)/shard_map/all_to_all | solution.py:964
  373.3 3.3 collective-permute-start.22
  374.7 24.1 %collective-permute-start.28 = (bf16[512,512]{1,0:T(8,128)(2,1)S(1)}, bf16[512,512]{1,0:T(8,128)(2,1)S(1)}, u32[]{:S(2)}, u32[]{:S(2)}) collective-permute-start(bf16[512,512]{1,0:T(8,128)(2,1)S(1)} %get-tuple-element.105), channel_id=1, source_target_pairs={{0,4},{4,0},{1,5},{5,1},{2,6},{6,2},{3,7},{7,3},{8,12},{12,8},{9,1... | collective-permute-start | bytes 1572872 | tf_op jit(solution)/shard_map/ppermute | solution.py:716
  376.7 6.3 %collective-permute-start.23 = (bf16[640,128]{1,0:T(8,128)(2,1)S(1)}, bf16[640,128]{1,0:T(8,128)(2,1)S(1)}, u32[]{:S(2)}, u32[]{:S(2)}) collective-permute-start(bf16[640,128]{1,0:T(8,128)(2,1)S(1)} %get-tuple-element.118), channel_id=1, source_target_pairs={{0,2},{2,0},{1,3},{3,1},{4,6},{6,4},{5,7},{7,5},{8,10},{10,8},{9,1... | collective-permute-start | bytes 491528 | tf_op jit(solution)/shard_map/ppermute | solution.py:722
  378.3 14.2 %collective-permute-start.25 = (bf16[640,128]{1,0:T(8,128)(2,1)S(1)}, bf16[640,128]{1,0:T(8,128)(2,1)S(1)}, u32[]{:S(2)}, u32[]{:S(2)}) collective-permute-start(bf16[640,128]{1,0:T(8,128)(2,1)S(1)} %get-tuple-element.119), channel_id=1, source_target_pairs={{0,4},{4,0},{1,5},{5,1},{2,6},{6,2},{3,7},{7,3},{8,12},{12,8},{9,1... | collective-permute-start | bytes 491528 | tf_op jit(solution)/shard_map/ppermute | solution.py:716
  392.6 5.7 %collective-permute-start.24 = (bf16[640,128]{1,0:T(8,128)(2,1)S(1)}, bf16[640,128]{1,0:T(8,128)(2,1)S(1)}, u32[]{:S(2)}, u32[]{:S(2)}) collective-permute-start(bf16[640,128]{1,0:T(8,128)(2,1)S(1)} %get-tuple-element.116), channel_id=1, source_target_pairs={{0,4},{4,0},{1,5},{5,1},{2,6},{6,2},{3,7},{7,3},{8,12},{12,8},{9,1... | collective-permute-start | bytes 491528 | tf_op jit(solution)/shard_map/ppermute | solution.py:716
  393.2 5.4 collective-permute-start.26
  398.7 1.7 collective-permute-start.27
  454.1 16.2 %collective-permute-start.30 = (bf16[1024,1024]{1,0:T(8,128)(2,1)}, bf16[1024,1024]{1,0:T(8,128)(2,1)S(1)}, u32[]{:S(2)}, u32[]{:S(2)}) collective-permute-start(bf16[1024,1024]{1,0:T(8,128)(2,1)} %get-tuple-element.71), channel_id=1, source_target_pairs={{0,1},{1,0},{2,3},{3,2},{4,5},{5,4},{6,7},{7,6},{8,9},{9,8},{10,11... | collective-permute-start | bytes 6291464 | tf_op jit(solution)/shard_map/ppermute | solution.py:719
  454.3 20.1 %collective-permute-start.29 = (bf16[1024,1024]{1,0:T(8,128)(2,1)}, bf16[1024,1024]{1,0:T(8,128)(2,1)}, u32[]{:S(2)}, u32[]{:S(2)}) collective-permute-start(bf16[1024,1024]{1,0:T(8,128)(2,1)} %get-tuple-element.69), channel_id=1, source_target_pairs={{0,1},{1,0},{2,3},{3,2},{4,5},{5,4},{6,7},{7,6},{8,9},{9,8},{10,11... | collective-permute-start | bytes 6291464 | tf_op jit(solution)/shard_map/ppermute | solution.py:719
  455.6 72.0 %all-to-all-start.3 = ((bf16[4,608,512]{2,1,0:T(8,128)(2,1)}), bf16[4,608,512]{2,1,0:T(8,128)(2,1)}, u32[]{:S(2)}, u32[]{:S(2)}) async-start(bf16[4,608,512]{2,1,0:T(8,128)(2,1)} %pad_maximum_fusion.refs_0_), calls=%async_computation.3 | async-start | bytes 4980736 | tf_op jit(solution)/shard_map/all_to_all | solution.py:705
  473.2 26.1 %collective-permute-start.33 = (bf16[512,1024]{1,0:T(8,128)(2,1)S(1)}, bf16[512,1024]{1,0:T(8,128)(2,1)S(1)}, u32[]{:S(2)}, u32[]{:S(2)}) collective-permute-start(bf16[512,1024]{1,0:T(8,128)(2,1)S(1)} %slice.300), channel_id=1, source_target_pairs={{0,4},{4,0},{1,5},{5,1},{2,6},{6,2},{3,7},{7,3},{8,12},{12,8},{9,1... | collective-permute-start | bytes 3145736 | tf_op jit(solution)/shard_map/ppermute | solution.py:716
  477.4 26.1 %collective-permute-start.31 = (bf16[2,512,512]{2,1,0:T(8,128)(2,1)S(1)}, bf16[2,512,512]{2,1,0:T(8,128)(2,1)S(1)}, u32[]{:S(2)}, u32[]{:S(2)}) collective-permute-start(bf16[2,512,512]{2,1,0:T(8,128)(2,1)S(1)} %pad_maximum_fusion.11), channel_id=1, source_target_pairs={{0,2},{2,0},{1,3},{3,1},{4,6},{6,4},{5,7},{7,5},{8,10},{10,8},{9,1... | collective-permute-start | bytes 3145736 | tf_op jit(solution)/shard_map/ppermute | solution.py:722
  480.1 30.4 %collective-permute-start.37 = (bf16[128,2048]{1,0:T(8,128)(2,1)S(1)}, bf16[128,2048]{1,0:T(8,128)(2,1)S(1)}, u32[]{:S(2)}, u32[]{:S(2)}) collective-permute-start(bf16[128,2048]{1,0:T(8,128)(2,1)S(1)} %add_convert_fusion.3), channel_id=1, source_target_pairs={{0,4},{4,0},{1,5},{5,1},{2,6},{6,2},{3,7},{7,3},{8,12},{12,8},{9,1... | collective-permute-start | bytes 1572872 | tf_op jit(solution)/shard_map/ppermute | solution.py:716
  499.7 13.9 %collective-permute-start.34 = (bf16[512,512]{1,0:T(8,128)(2,1)S(1)}, bf16[512,512]{1,0:T(8,128)(2,1)S(1)}, u32[]{:S(2)}, u32[]{:S(2)}) collective-permute-start(bf16[512,512]{1,0:T(8,128)(2,1)S(1)} %slice.421), channel_id=1, source_target_pairs={{0,2},{2,0},{1,3},{3,1},{4,6},{6,4},{5,7},{7,5},{8,10},{10,8},{9,1... | collective-permute-start | bytes 1572872 | tf_op jit(solution)/shard_map/ppermute | solution.py:722
  503.7 16.9 %collective-permute-start.32 = (bf16[512,512]{1,0:T(8,128)(2,1)S(1)}, bf16[512,512]{1,0:T(8,128)(2,1)S(1)}, u32[]{:S(2)}, u32[]{:S(2)}) collective-permute-start(bf16[512,512]{1,0:T(8,128)(2,1)S(1)} %fusion.9), channel_id=1, source_target_pairs={{0,4},{4,0},{1,5},{5,1},{2,6},{6,2},{3,7},{7,3},{8,12},{12,8},{9,1... | collective-permute-start | bytes 1572872 | tf_op jit(solution)/shard_map/ppermute | solution.py:716
  523.7 2.3 collective-permute-start.35
  526.0 8.8 %collective-permute-start.36 = (f32[2,512]{1,0:T(2,128)S(1)}, f32[2,512]{1,0:T(2,128)S(1)}, u32[]{:S(2)}, u32[]{:S(2)}) collective-permute-start(f32[2,512]{1,0:T(2,128)S(1)} %add.416), channel_id=1, source_target_pairs={{0,2},{2,0},{1,3},{3,1},{4,6},{6,4},{5,7},{7,5},{8,10},{10,8},{9,1... | collective-permute-start | bytes 12296 | tf_op jit(solution)/shard_map/ppermute | solution.py:722
  531.1 3.7 collective-permute-start.38
  533.3 15.9 %collective-permute-start.41 = (bf16[608,512]{1,0:T(8,128)(2,1)S(1)}, bf16[608,512]{1,0:T(8,128)(2,1)S(1)}, u32[]{:S(2)}, u32[]{:S(2)}) collective-permute-start(bf16[608,512]{1,0:T(8,128)(2,1)S(1)} %get-tuple-element.74), channel_id=1, source_target_pairs={{0,4},{4,0},{1,5},{5,1},{2,6},{6,2},{3,7},{7,3},{8,12},{12,8},{9,1... | collective-permute-start | bytes 1867784 | tf_op jit(solution)/shard_map/ppermute | solution.py:716
  534.9 1.2 collective-permute-start.39
  536.0 4.0 collective-permute-start.40
  (63 other events, 326.1 us)

commit v4 on v3

--- a/solution.py
+++ b/solution.py
@@ -42,23 +42,16 @@
     return pl.BlockSpec(shape, lambda *_: (0,) * len(shape))
 
 
-def rms(rows, gain):
-    wide = rows.astype(f32)
-    inv_rms = lax.rsqrt(jnp.mean(wide * wide, axis=-1, keepdims=True) + EPS)
-    return (wide * inv_rms * gain).astype(bf16)
-
-
-def joined_halves(first, second, place, gain=None):
+def joined_halves(first, second, place):
     half, width = first.shape
     size = min(half, 128)
     count = half // size
 
-    def kernel(place_ref, first_ref, second_ref, *rest):
-        out_ref = rest[-1]
+    def kernel(place_ref, first_ref, second_ref, out_ref):
         this = (pl.program_id(0) // count) == place_ref[0]
 
         def put(ref):
-            out_ref[...] = ref[...] if gain is None else rms(ref[...], rest[0][...])
+            out_ref[...] = ref[...]
 
         @pl.when(this)
         def _():
@@ -75,41 +68,71 @@
 
         return pl.BlockSpec((size, width), index)
 
-    extra = [] if gain is None else [gain.reshape(1, width)]
     return pl.pallas_call(
         kernel,
         grid_spec=pltpu.PrefetchScalarGridSpec(
             num_scalar_prefetch=1,
             grid=(2 * count,),
-            in_specs=[spec(0), spec(1)] + [whole(1, width) for _ in extra],
+            in_specs=[spec(0), spec(1)],
             out_specs=pl.BlockSpec((size, width), lambda i, place: (i, 0)),
         ),
         out_shape=jax.ShapeDtypeStruct((2 * half, width), bf16),
         cost_estimate=cost(4),
         compiler_params=PARAMS,
-    )(place, first, second, *extra)
-
-
-def normalised_rows(rows, gain):
-    count, width = rows.shape
+    )(place, first, second)
+
+
+def normalised_rows(blocks, place, gain):
+    count, width = blocks[0].shape
     size = min(count, 256)
-
-    def kernel(in_ref, gain_ref, out_ref, inv_ref):
-        wide = in_ref[...].astype(f32)
-        inv_rms = lax.rsqrt(jnp.mean(wide * wide, axis=-1, keepdims=True) + EPS)
-        out_ref[...] = (wide * inv_rms * gain_ref[...]).astype(bf16)
-        inv_ref[...] = jnp.broadcast_to(inv_rms, inv_ref.shape)
-
-    by_rows = lambda w: pl.BlockSpec((size, w), lambda i: (i, 0))
+    per = count // size
+    half = per // 2
+    n = 1 if len(blocks) == 1 else 2
+
+    def kernel(place_ref, *refs):
+        ins, (gain_ref, out_ref, inv_ref) = refs[: len(blocks)], refs[len(blocks) :]
+        i = pl.program_id(0)
+
+        def inverse(ref):
+            wide = ref[...].astype(f32)
+            inv_rms = lax.rsqrt(jnp.mean(wide * wide, axis=-1, keepdims=True) + EPS)
+            out_ref[0] = (wide * inv_rms * gain_ref[...]).astype(bf16)
+            return inv_rms
+
+        @pl.when(i < per)
+        def _():
+            inv_ref[...] = jnp.broadcast_to(inverse(ins[0]), inv_ref.shape)
+
+        for which, ref in enumerate(ins[1:]):
+            start = per + (place_ref[0] ^ which) * half
+
+            @pl.when((i >= start) & (i < start + half))
+            def _(ref=ref):
+                inverse(ref)
+
+    def spec(which):
+        def index(i, place):
+            if which == 0:
+                return (jnp.minimum(i, per - 1), 0)
+            return (jnp.clip(i - per - (place[0] ^ (which - 1)) * half, 0, half - 1), 0)
+
+        return pl.BlockSpec((size, width), index)
+
     return pl.pallas_call(
         kernel,
-        grid=(count // size,),
-        in_specs=[by_rows(width), whole(1, width)],
-        out_specs=[by_rows(width), by_rows(LANE)],
-        out_shape=[jax.ShapeDtypeStruct(rows.shape, bf16), jax.ShapeDtypeStruct((count, LANE), f32)],
-        cost_estimate=cost(4),
+        grid_spec=pltpu.PrefetchScalarGridSpec(
+            num_scalar_prefetch=1,
+            grid=(n * per,),
+            in_specs=[spec(i) for i in range(len(blocks))] + [whole(1, width)],
+            out_specs=[
+                pl.BlockSpec((1, size, width), lambda i, place: (i // per, lax.rem(i, per), 0)),
+                pl.BlockSpec((size, LANE), lambda i, place: (jnp.minimum(i, per - 1), 0)),
+            ],
+        ),
+        out_shape=[jax.ShapeDtypeStruct((n, count, width), bf16), jax.ShapeDtypeStruct((count, LANE), f32)],
+        cost_estimate=cost(8),
         compiler_params=PARAMS,
-    )(rows, gain.reshape(1, width))
+    )(place, *blocks, gain.reshape(1, width))
 
 
 def unpacked(window, counts, place, *before):
@@ -143,29 +166,28 @@
 
 
 def products(lefts, more_lefts, right, more_right, blocks, width):
-    n = len(lefts)
-    count, inner = lefts[0].shape
+    n, count, inner = lefts.shape
     size = min(count, 512)
 
     def kernel(blocks_ref, *refs):
         a, b, (w, v), outs = refs[:n], refs[n : 2 * n], refs[2 * n : 2 * n + 2], refs[2 * n + 2 :]
         for i in range(n):
-            outs[i][...] = (mm_t(a[i][...], w[...]) + mm_t(b[i][...], v[...])).astype(bf16)
-
-    rows = pl.BlockSpec((size, inner), lambda j, i, blocks: (i, 0))
+            outs[i][...] = (mm_t(a[i][0], w[...]) + mm_t(b[i][0], v[...])).astype(bf16)
+
+    rows = [pl.BlockSpec((1, size, inner), lambda j, i, blocks, which=which: (which, i, 0)) for which in range(n)]
     weights = pl.BlockSpec((width, inner), lambda j, i, blocks: (blocks[j], 0))
     return pl.pallas_call(
         kernel,
         grid_spec=pltpu.PrefetchScalarGridSpec(
             num_scalar_prefetch=1,
             grid=(blocks.shape[0], count // size),
-            in_specs=[rows] * (2 * n) + [weights] * 2,
+            in_specs=rows * 2 + [weights] * 2,
             out_specs=[pl.BlockSpec((size, width), lambda j, i, blocks: (i, j))] * n,
         ),
         out_shape=[jax.ShapeDtypeStruct((count, width * blocks.shape[0]), bf16)] * n,
         cost_estimate=cost(5),
         compiler_params=PARAMS,
-    )(blocks, *lefts, *more_lefts, right, more_right)
+    )(blocks, *[lefts] * n, *[more_lefts] * n, right, more_right)
 
 
 def interleaved(first, second, depth, part):
@@ -210,6 +232,13 @@
 
         return pl.BlockSpec((self.size, width), index)
 
+    def stacked(self, width):
+        def index(s, i, place):
+            turn = self.at(i) // self.per
+            return (turn ^ place[0] if self.pieces > 1 else turn, s * self.per + lax.rem(self.at(i), self.per), 0)
+
+        return pl.BlockSpec((1, self.size, width), index)
+
     def is_turn(self, which, place_ref):
         return (self.at(pl.program_id(1)) // self.per) == (place_ref[0] ^ which)
 
@@ -232,14 +261,10 @@
     seqs, length = masks.shape[:2]
     width, inner = proj_x.shape
     size = min(256, length)
-    rows = Rows(seqs, length, len(normed), size)
+    rows = Rows(seqs, length, normed.shape[0], size)
     packed = select_low.shape[1] + select_state.shape[0]
 
-    def kernel(place_ref, *refs):
-        ins, (w_ref, vec_ref, masks_ref, low_ref, state_ref, x_ref, u_ref, p_ref, xs) = (
-            refs[: len(normed)],
-            refs[len(normed) :],
-        )
+    def kernel(place_ref, in_ref, w_ref, vec_ref, masks_ref, low_ref, state_ref, x_ref, u_ref, p_ref, xs):
         fresh = pl.program_id(1) == 0
 
         @pl.when(fresh)
@@ -250,14 +275,9 @@
         def _():
             xs[0:8] = xs[size : size + 8]
 
-        for which, ref in enumerate(ins):
-
-            @pl.when(rows.is_turn(which, place_ref))
-            def _(ref=ref):
-                x = mm(ref[...], w_ref[...]).astype(bf16)
-                x_ref[0] = x
-                xs[8 : 8 + size] = x.astype(f32)
-
+        x = mm(in_ref[0], w_ref[...]).astype(bf16)
+        x_ref[0] = x
+        xs[8 : 8 + size] = x.astype(f32)
         pre = convolved(xs, masks_ref, vec_ref, size, taps)
         u = (pre / (1.0 + jnp.exp(-pre))).astype(bf16)
         u_ref[0] = u
@@ -272,7 +292,7 @@
         grid_spec=pltpu.PrefetchScalarGridSpec(
             num_scalar_prefetch=1,
             grid=rows.grid,
-            in_specs=[rows.spec(i, width) for i in range(len(normed))]
+            in_specs=[rows.stacked(width)]
             + [whole(width, inner), whole(8, inner), rows.block(LANE), whole(*select_low.shape), whole(*select_state.shape)],
             out_specs=[rows.block(inner), rows.block(inner), rows.packed(packed)],
             scratch_shapes=[pltpu.VMEM((size + 8, inner), f32)],
@@ -284,46 +304,46 @@
         ],
         cost_estimate=cost(9),
         compiler_params=PARAMS,
-    )(place, *normed, proj_x, vec, masks, select_low, select_state)
+    )(place, normed, proj_x, vec, masks, select_low, select_state)
 
 
 def gates(normed, grads, proj_z, proj_out, ssm_out, place):
     seqs, length, inner = ssm_out.shape
     width = proj_z.shape[0]
     size = min(256, length)
-    rows = Rows(seqs, length, len(normed), size)
-    n = len(normed)
-
-    def kernel(place_ref, *refs):
-        a_refs, g_refs, (z_ref, o_ref, s_ref), outs = refs[:n], refs[n : 2 * n], refs[2 * n : 2 * n + 3], refs[2 * n + 3 :]
+    n = len(grads)
+    rows = Rows(seqs, length, n, size)
+
+    def kernel(place_ref, a_ref, *refs):
+        g_refs, (z_ref, o_ref, s_ref, gated_ref, grad_z_ref, grad_ref) = refs[:n], refs[n:]
         for which in range(n):
 
             @pl.when(rows.is_turn(which, place_ref))
             def _(which=which):
-                z = mm(a_refs[which][...], z_ref[...]).astype(bf16).astype(f32)
+                z = mm(a_ref[0], z_ref[...]).astype(bf16).astype(f32)
                 grad = mm_t(g_refs[which][...], o_ref[...])
                 ssm = s_ref[0]
                 sigmoid = 1.0 / (1.0 + jnp.exp(-z))
                 gate = z * sigmoid
-                outs[which][...] = (ssm * gate).astype(bf16)
-                outs[n + which][...] = (grad * ssm * sigmoid * (1.0 + z * (1.0 - sigmoid))).astype(bf16)
-                outs[2 * n][0] = grad * gate
+                gated_ref[0] = (ssm * gate).astype(bf16)
+                grad_z_ref[0] = (grad * ssm * sigmoid * (1.0 + z * (1.0 - sigmoid))).astype(bf16)
+                grad_ref[0] = grad * gate
 
     total = seqs * length // n
-    outs = pl.pallas_call(
+    return pl.pallas_call(
         kernel,
         grid_spec=pltpu.PrefetchScalarGridSpec(
             num_scalar_prefetch=1,
             grid=rows.grid,
-            in_specs=[rows.spec(i, width) for i in range(n)] * 2
+            in_specs=[rows.stacked(width)]
+            + [rows.spec(i, width) for i in range(n)]
             + [whole(width, inner), whole(inner, width), rows.block(inner)],
-            out_specs=[rows.spec(i, inner) for i in range(n)] * 2 + [rows.block(inner)],
+            out_specs=[rows.stacked(inner)] * 2 + [rows.block(inner)],
         ),
-        out_shape=[jax.ShapeDtypeStruct((total, inner), bf16)] * (2 * n) + [jax.ShapeDtypeStruct((seqs, length, inner), f32)],
+        out_shape=[jax.ShapeDtypeStruct((n, total, inner), bf16)] * 2 + [jax.ShapeDtypeStruct((seqs, length, inner), f32)],
         cost_estimate=cost(14),
         compiler_params=PARAMS,
-    )(place, *normed, *grads, proj_z, proj_out, ssm_out)
-    return outs[:n], outs[n : 2 * n], outs[2 * n]
+    )(place, normed, *grads, proj_z, proj_out, ssm_out)
 
 
 def convolve_back(packed, direct, x_part, vec, masks, select_low, select_state, place, n, taps):
@@ -333,7 +353,7 @@
     states = (packed.shape[2] - LANE) // 2
 
     def kernel(place_ref, p_ref, d_ref, x_ref, edge_ref, vec_ref, masks_ref, low_ref, state_ref, *rest):
-        outs, (sum_ref, tok_ref, xs, ds) = rest[:n], rest[n:]
+        out_ref, sum_ref, tok_ref, xs, ds = rest
         fresh = pl.program_id(1) == 0
 
         @pl.when(jnp.logical_and(fresh, pl.program_id(0) == 0))
@@ -375,14 +395,10 @@
             total = total + ds[by : by + size] * masks_ref[0, :, taps + by : taps + by + 1] * vec_ref[tap : tap + 1]
             joint = grad * xs[8 - by : 8 - by + size] * masks_ref[0, :, by : by + 1]
             sum_ref[tap : tap + 1] += jnp.sum(joint, axis=0, keepdims=True)
-        for which in range(n):
-
-            @pl.when(rows.is_turn(which, place_ref))
-            def _(which=which):
-                outs[which][...] = total.astype(bf16)
+        out_ref[0] = total.astype(bf16)
 
     edge = pl.BlockSpec((1, 16, inner), lambda s, i, place: (s, jnp.maximum(rows.at(i) * (size // 16) - 1, 0), 0))
-    outs = pl.pallas_call(
+    return pl.pallas_call(
         kernel,
         grid_spec=pltpu.PrefetchScalarGridSpec(
             num_scalar_prefetch=1,
@@ -397,15 +413,14 @@
                 whole(inner, LANE),
                 whole(inner, LANE),
             ],
-            out_specs=[rows.spec(i, inner) for i in range(n)] + [whole(8, inner), rows.block(2 * LANE)],
+            out_specs=[rows.stacked(inner), whole(8, inner), rows.block(2 * LANE)],
             scratch_shapes=[pltpu.VMEM((size + 8, inner), f32)] * 2,
         ),
-        out_shape=[jax.ShapeDtypeStruct((seqs * length // n, inner), bf16)] * n
+        out_shape=[jax.ShapeDtypeStruct((n, seqs * length // n, inner), bf16)]
         + [jax.ShapeDtypeStruct((8, inner), f32), jax.ShapeDtypeStruct((seqs, length, 2 * LANE), bf16)],
         cost_estimate=cost(10),
         compiler_params=PARAMS,
     )(place, packed, direct, x_part, x_part, vec, masks, select_low, select_state)
-    return outs[:n], outs[n], outs[n + 1]
 
 
 def log_one_plus(v):
@@ -730,8 +745,7 @@
         return [array, joined_halves(block, self.near(block), self.core[None])]
 
     def normed(self, array, block, gain):
-        own, inv_rms = normalised_rows(array, gain)
-        return [own, joined_halves(block, self.near(block), self.core[None], gain)], inv_rms
+        return normalised_rows([array, block, self.near(block)], self.core[None], gain)
 
     def total(self, array, begin):
         half = array.shape[0] // 2
@@ -796,8 +810,8 @@
         return [self.in_order([block], self.seqs).reshape(block.shape)]
 
     def normed(self, array, block, gain):
-        inv_rms = normalised_rows(array, gain)[1]
-        return [normalised_rows(self.pieces_done(array, block)[0], gain)[0]], inv_rms
+        inv_rms = normalised_rows([array], self.place, gain)[1]
+        return normalised_rows(self.pieces_done(array, block), self.place, gain)[0], inv_rms
 
     def in_order(self, arrays, seqs):
         array = arrays[0].reshape(lax.axis_size("context"), seqs, -1, arrays[0].shape[-1])
@@ -958,6 +972,8 @@
     gated, grad_z, grad_ssm = gates(normed, grad_all, proj_z, proj_out, ssm_out, moves.place)
 
     def weight_grad(lefts, rights):
+        if not isinstance(rights, list):
+            lefts, rights = ([a.reshape(-1, a.shape[-1])] for a in (lefts, rights))
         return sum(t_dot(a, b) for a, b in zip(lefts, rights)).astype(bf16)
 
     early = lax.all_to_all(weight_grad(normed, grad_z).reshape(shards, depth, inner), "shards", 0, 0)
@@ -967,7 +983,7 @@
             [lax.dynamic_slice_in_dim(weights, (b + begin) * share_width, share_width, axis) for b in blocks], axis
         )
 
-    out_sums = moves.share_begin(lambda blocks: [dot(g, chosen(proj_out, blocks, 1), bf16) for g in gated])
+    out_sums = moves.share_begin(lambda blocks: [dot(gated[i], chosen(proj_out, blocks, 1), bf16) for i in range(gated.shape[0])])
     out_sums_2 = moves.share_middle(out_sums)
     out_share = moves.share_end(out_sums_2)
     own_columns = tensor * share_width
@@ -1004,7 +1020,7 @@
         select_low,
         jnp.pad(select_state, ((0, 0), (0, LANE - select_state.shape[1]))),
         moves.place,
-        len(normed),
+        normed.shape[0],
         taps,
     )
     grad_select = t_dot(values.reshape(tokens, inner), grad_selected.reshape(tokens, -1))[:, :selected]

time: 571 us -> 565 us (0.989)
  other arithmetic: 60.4 us -> 51.5 us
  matrix products: 39.2 us -> 46.1 us
    ppermute x3, waiting for transfers between devices: 0.01 us -> 11.5 us  [line_gather(): lax.ppermute(right, axis, [(i, i + 1) for i in range(step - 1, count - 1)])]
    dot_general x4, matrix products: 8.99 us -> 16.8 us  [dot(): return jnp.dot(a, b, preferred_element_type=f32).astype(out)]
    pallas_call x2 -> x1, Pallas kernels: 14.6 us -> 7.12 us  [joined_halves(): pl.pallas_call(kernel, grid_spec=pltpu.PrefetchScalarGridSpec(num_scalar_...]
    ppermute x3, waiting for transfers between devices: 32 us -> 25.6 us  [line_gather(): lax.ppermute(left, axis, [(i, i - 1) for i in range(1, count - step + 1)])]
    unnamed x151 -> x137, local copies, waits for them, and re-layouts: 12.6 us -> 11.4 us
    dot_general x8 -> x6, matrix products: 30.2 us -> 29.2 us  [t_dot(): lax.dot_general(a, b, (((0,), (0,)), ((), ())), preferred_element_type=f32)]
  transfers between devices with their start and end apart: 46 -> 46, of which waited for: 21 -> 22; matrix products, arithmetic and copies ran while one was open for 20% -> 22% of each run, Pallas kernels for 31% -> 30%
where the time goes in v4:
time: 565 us; the launch traced here: 557 us
  Pallas kernels  204 us (36%)
  waiting for transfers between devices  121 us (21%)
  starting transfers between devices  60.7 us (11%)
  local copies, waits for them, and re-layouts  58 us (10%)
  other arithmetic  51.5 us (9%)
  matrix products  46.1 us (8%)
  between operations  16.3 us (3%)
    pallas_call x1, Pallas kernels, scan_backward(): pl.pallas_call(functools.partial(backward_kernel, S, G), grid=(T // LANE,...  69.6 us
    ppermute x14, waiting for transfers between devices, across(): return lax.ppermute(array, 'context', [(0, 1), (1, 0)])  66.9 us
    pallas_call x1, Pallas kernels, scan_forward(): pl.pallas_call(functools.partial(forward_kernel, S, G), grid=(T // LANE,)...  33.7 us
    dot_general x6, matrix products, t_dot(): lax.dot_general(a, b, (((0,), (0,)), ((), ())), preferred_element_type=f32)  29.2 us
    ppermute x3, waiting for transfers between devices, line_gather(): lax.ppermute(left, axis, [(i, i - 1) for i in range(1, count - step + 1)])  25.6 us
    pallas_call x2, Pallas kernels, products(): pl.pallas_call(kernel, grid_spec=pltpu.PrefetchScalarGridSpec(num_scalar_...  18.9 us
    pallas_call x1, Pallas kernels, gates(): pl.pallas_call(kernel, grid_spec=pltpu.PrefetchScalarGridSpec(num_scalar_...  18.3 us
    dot_general x4, matrix products, dot(): return jnp.dot(a, b, preferred_element_type=f32).astype(out)  16.8 us
  transfers between devices with their start and end apart: 46, of which 22 were waited for; matrix products, arithmetic and copies ran while one was open for 22% of the time, Pallas kernels for 30%

profile of v4, /device:TPU:0, one launch (start us, length us, event | category | flops | bytes accessed | tf_op | source)
XLA Modules:
  0.0 557.0 jit_solution(15021420878518075728)
XLA Ops:
  0.7 3.2 constant_dynamic-slice_fusion.21.refs_0_
  3.9 2.9 collective-permute-start
  10.0 6.8 %fusion.58 = (bf16[512,1,1024]{2,1,0:T(2,128)(2,1)}, bf16[512,1,1024]{2,1,0:T(2,128)(2,1)}) fusion(bf16[512,2,1024]{2,1,0:T(2,128)(2,1)} %param.17), kind=kLoop, calls=%fused_computation.224 | loop fusion | bytes 4194304 | tf_op jit(solution)/shard_map/slice | solution.py:942
  20.4 3.5 collective-permute-start.2
  25.7 11.5 %collective-permute-done.2.refs_2_.refs_0_ = bf16[624,512]{1,0:T(8,128)(2,1)S(1)} collective-permute-done((bf16[624,512]{1,0:T(8,128)(2,1)S(1)}, bf16[624,512]{1,0:T(8,128)(2,1)S(1)}, u32[]{:S(2)}, u32[]{:S(2)}) %collective-permute-start.2) | collective-permute-done | bytes 639008 | tf_op jit(solution)/shard_map/ppermute | solution.py:708
  38.7 2.7 collective-permute-done.5.refs_4_
  51.0 8.3 %collective-permute-done.6.refs_5_ = bf16[624,512]{1,0:T(8,128)(2,1)} collective-permute-done((bf16[624,512]{1,0:T(8,128)(2,1)}, bf16[624,512]{1,0:T(8,128)(2,1)}, u32[]{:S(2)}, u32[]{:S(2)}) %collective-permute-start.6) | collective-permute-done | bytes 639008 | tf_op jit(solution)/shard_map/ppermute | solution.py:709
  60.9 14.6 %collective-permute-done.7.refs_6_ = bf16[624,512]{1,0:T(8,128)(2,1)S(1)} collective-permute-done((bf16[624,512]{1,0:T(8,128)(2,1)}, bf16[624,512]{1,0:T(8,128)(2,1)S(1)}, u32[]{:S(2)}, u32[]{:S(2)}) %collective-permute-start.7) | collective-permute-done | bytes 639008 | tf_op jit(solution)/shard_map/ppermute | solution.py:709
  76.3 4.2 shard_map.221
  84.1 5.5 all-to-all-start
  94.8 3.2 constant_dynamic-slice_fusion.9
  98.5 11.0 %shard_map.222 = (bf16[2,1024,2048]{2,1,0:T(8,128)(2,1)}, f32[1024,128]{1,0:T(8,128)}) custom-call(s32[1]{0:T(128)} %bitcast.1.place_ref, bf16[1024,2048]{1,0:T(8,128)(2,1)} %bitcast.191, bf16[512,2048]{1,0:T(8,128)(2,1)} %copy-done.18, bf16[512,2048]{1,0:T(8,128)(2,1)} %collective-permute-done.1.refs_2_, f32[1,2048]{1,0:T(1,128)} %bitcast.232), custom_call_target="tpu_custom_call" | custom-call | flops 920000000 | bytes 2880000 | tf_op jit(solution)/shard_map/pallas_call | solution.py:121
  109.5 13.3 %shard_map.227 = (bf16[2,1024,512]{2,1,0:T(8,128)(2,1)}, bf16[2,1024,512]{2,1,0:T(8,128)(2,1)}, f32[2,8,160,128]{3,2,1,0:T(8,128)}) custom-call(s32[1]{0:T(128)} %bitcast.place_ref, bf16[2,1024,2048]{2,1,0:T(8,128)(2,1)} %get-tuple-element.40.in_ref.a_ref, bf16[2048,512]{1,0:T(8,128)(2,1)} %bitcast.182, f32[8,512]{1,0:T(8,128)} %maximum_maximum_fusion.vec_ref, ...), custom_call_target="tpu_custom_call" | custom-call | flops 1035000000 | bytes 3240000 | tf_op jit(solution)/shard_map/pallas_call | solution.py:290
  130.0 3.2 collective-permute-done.11
  133.2 14.1 %collective-permute-done.13 = bf16[640,128]{1,0:T(8,128)(2,1)S(1)} collective-permute-done((bf16[640,128]{1,0:T(8,128)(2,1)S(1)}, bf16[640,128]{1,0:T(8,128)(2,1)S(1)}, u32[]{:S(2)}, u32[]{:S(2)}) %collective-permute-start.13) | collective-permute-done | bytes 163872 | tf_op jit(solution)/shard_map/ppermute | solution.py:731
  157.3 33.7 %shard_map.228 = (f32[2,1024,512]{2,1,0:T(8,128)}, f32[2,1024,512]{2,1,0:T(8,128)}, f32[8,128,128]{2,1,0:T(8,128)}) custom-call(f32[2,8,160,128]{3,2,1,0:T(8,128)} %bitcast.204, bf16[2,1024,512]{2,1,0:T(8,128)(2,1)} %get-tuple-element.44.u_ref, f32[2,1024,128]{2,1,0:T(8,128)} %and_convert_fusion.refs_7_.masks_ref, bf16[128,512]{1,0:T(8,128)(2,1)} %bitcast.242, ...), custom_call_target="tpu_custom_call" | custom-call | flops 3449999872 | bytes 10800000 | tf_op jit(solution)/shard_map/pallas_call | solution.py:639
  191.0 7.1 %shard_map.224.refs_1_ = bf16[1024,2048]{1,0:T(8,128)(2,1)} custom-call(s32[1]{0:T(128)} %bitcast.1.place_ref, bf16[512,2048]{1,0:T(8,128)(2,1)} %collective-permute-done.8.first_ref, bf16[512,2048]{1,0:T(8,128)(2,1)} %collective-permute-done.9.second_ref), custom_call_target="tpu_custom_call" | custom-call | flops 460000000 | bytes 1440000 | tf_op jit(solution)/shard_map/pallas_call | solution.py:71
  201.5 3.0 slice.276
  204.6 18.3 %shard_map.229 = (bf16[2,1024,512]{2,1,0:T(8,128)(2,1)}, bf16[2,1024,512]{2,1,0:T(8,128)(2,1)}, f32[2,1024,512]{2,1,0:T(8,128)}) custom-call(s32[1]{0:T(128)} %bitcast.place_ref, bf16[2,1024,2048]{2,1,0:T(8,128)(2,1)} %get-tuple-element.40.in_ref.a_ref, bf16[1024,2048]{1,0:T(8,128)(2,1)} %bitcast.179, bf16[1024,2048]{1,0:T(8,128)(2,1)} %shard_map.224.refs_1_, ...), custom_call_target="tpu_custom_call" | custom-call | flops 1610000000 | bytes 5040000 | tf_op jit(solution)/shard_map/pallas_call | solution.py:333
  223.2 4.0 convolution_convert_fusion
  227.2 2.6 convolution_convert_fusion.1
  230.3 5.9 %bitcast_convert_fusion.1 = bf16[2048,512]{1,0:T(8,128)(2,1)} fusion(bf16[2,1024,2048]{2,1,0:T(8,128)(2,1)S(1)} %bitcast.186, bf16[2,1024,512]{2,1,0:T(8,128)(2,1)S(1)} %copy-done.5), kind=kOutput, calls=%fused_computation.2 | convolution fusion | flops 4296015872 | bytes 12582912 | tf_op jit(solution)/shard_map/dot_general | solution.py:855
  236.2 5.1 all-to-all-start.1
  241.3 5.0 fusion.14
  246.3 3.7 add_convert_fusion
  250.0 5.4 fusion.63
  255.4 4.9 convert_add_fusion.3.refs_0_
  270.7 69.6 %shard_map.231 = (bf16[2,1024,512]{2,1,0:T(8,128)(2,1)}, f32[2,1024,512]{2,1,0:T(8,128)}, f32[2,8,160,128]{3,2,1,0:T(8,128)}, f32[16,512]{1,0:T(8,128)}, f32[8,512]{1,0:T(8,128)}) custom-call(f32[2,8,160,128]{3,2,1,0:T(8,128)} %bitcast.205, bf16[2,1024,512]{2,1,0:T(8,128)(2,1)} %get-tuple-element.44.u_ref, f32[2,1024,512]{2,1,0:T(8,128)} %get-tuple-element.49.step_ref, ...), custom_call_target="tpu_custom_call" | custom-call | flops 9774999552 | bytes 30600000 | tf_op jit(solution)/shard_map/pallas_call | solution.py:664
  342.2 2.9 convolution_convert_fusion.2
  345.1 2.8 fusion.56
  353.6 5.3 all-to-all-start.2
  361.6 3.2 convert_add_fusion.5
  373.9 3.9 collective-permute-done.23
  377.8 9.3 %collective-permute-done.25 = bf16[640,128]{1,0:T(8,128)(2,1)S(1)} collective-permute-done((bf16[640,128]{1,0:T(8,128)(2,1)S(1)}, bf16[640,128]{1,0:T(8,128)(2,1)S(1)}, u32[]{:S(2)}, u32[]{:S(2)}) %collective-permute-start.25) | collective-permute-done | bytes 163872 | tf_op jit(solution)/shard_map/ppermute | solution.py:731
  398.4 15.9 %shard_map.234 = (bf16[2,1024,512]{2,1,0:T(8,128)(2,1)}, f32[8,512]{1,0:T(8,128)}, bf16[2,1024,256]{2,1,0:T(8,128)(2,1)}) custom-call(s32[1]{0:T(128)} %bitcast.place_ref, f32[2,8,160,128]{3,2,1,0:T(8,128)} %bitcast.197, f32[2,1024,512]{2,1,0:T(8,128)} %get-tuple-element.54.d_ref, bf16[2,1024,512]{2,1,0:T(8,128)(2,1)} %get-tuple-element.55.x_ref.edge_ref, ...), custom_call_target="tpu_custom_call" | custom-call | flops 1150000000 | bytes 3600000 | tf_op jit(solution)/shard_map/pallas_call | solution.py:401
  417.4 9.4 %bitcast_convert_fusion = bf16[2048,512]{1,0:T(8,128)(2,1)} fusion(bf16[2,1024,2048]{2,1,0:T(8,128)(2,1)} %get-tuple-element.40.in_ref.a_ref, bf16[2,1024,512]{2,1,0:T(8,128)(2,1)S(1)} %copy-done.3), kind=kOutput, calls=%fused_computation.1 | convolution fusion | flops 4296015872 | bytes 12582912 | tf_op jit(solution)/shard_map/dot_general | solution.py:855
  438.6 9.5 %shard_map.238 = (bf16[1024,1024]{1,0:T(8,128)(2,1)}, bf16[1024,1024]{1,0:T(8,128)(2,1)}) custom-call(s32[2]{0:T(128)} %get-tuple-element.132.blocks_ref, bf16[2,1024,512]{2,1,0:T(8,128)(2,1)} %get-tuple-element.56.refs_0_.refs_1_, bf16[2,1024,512]{2,1,0:T(8,128)(2,1)} %get-tuple-element.56.refs_0_.refs_1_, ...), custom_call_target="tpu_custom_call" | custom-call | flops 575000000 | bytes 1800000 | tf_op jit(solution)/shard_map/pallas_call | solution.py:179
  449.6 5.1 all-to-all-start.3
  454.7 9.4 %shard_map.237 = (bf16[1024,1024]{1,0:T(8,128)(2,1)}, bf16[1024,1024]{1,0:T(8,128)(2,1)}) custom-call(s32[2]{0:T(128)} %get-tuple-element.131.blocks_ref, bf16[2,1024,512]{2,1,0:T(8,128)(2,1)} %get-tuple-element.56.refs_0_.refs_1_, bf16[2,1024,512]{2,1,0:T(8,128)(2,1)} %get-tuple-element.56.refs_0_.refs_1_, ...), custom_call_target="tpu_custom_call" | custom-call | flops 575000000 | bytes 1800000 | tf_op jit(solution)/shard_map/pallas_call | solution.py:179
  464.1 2.7 convert_add_fusion
  474.9 18.2 %collective-permute-done.33 = bf16[512,1024]{1,0:T(8,128)(2,1)S(1)} collective-permute-done((bf16[512,1024]{1,0:T(8,128)(2,1)S(1)}, bf16[512,1024]{1,0:T(8,128)(2,1)S(1)}, u32[]{:S(2)}, u32[]{:S(2)}) %collective-permute-start.33) | collective-permute-done | bytes 1048608 | tf_op jit(solution)/shard_map/ppermute | solution.py:731
  498.7 5.6 %collective-permute-done.37 = bf16[128,2048]{1,0:T(8,128)(2,1)S(1)} collective-permute-done((bf16[128,2048]{1,0:T(8,128)(2,1)S(1)}, bf16[128,2048]{1,0:T(8,128)(2,1)S(1)}, u32[]{:S(2)}, u32[]{:S(2)}) %collective-permute-start.37) | collective-permute-done | bytes 524320 | tf_op jit(solution)/shard_map/ppermute | solution.py:731
  504.4 3.0 collective-permute-done.34
  507.6 6.8 %collective-permute-done.32 = bf16[512,512]{1,0:T(8,128)(2,1)S(1)} collective-permute-done((bf16[512,512]{1,0:T(8,128)(2,1)S(1)}, bf16[512,512]{1,0:T(8,128)(2,1)S(1)}, u32[]{:S(2)}, u32[]{:S(2)}) %collective-permute-start.32) | collective-permute-done | bytes 524320 | tf_op jit(solution)/shard_map/ppermute | solution.py:731
  514.8 2.6 fusion.2
  530.3 3.5 fusion.5
  534.4 8.9 %collective-permute-done.41 = bf16[608,512]{1,0:T(8,128)(2,1)S(1)} collective-permute-done((bf16[608,512]{1,0:T(8,128)(2,1)S(1)}, bf16[608,512]{1,0:T(8,128)(2,1)S(1)}, u32[]{:S(2)}, u32[]{:S(2)}) %collective-permute-start.41) | collective-permute-done | bytes 622624 | tf_op jit(solution)/shard_map/ppermute | solution.py:731
  550.0 6.5 %shard_map.240 = f32[512,2,1024]{2,1,0:T(2,128)} custom-call(bf16[2,608,512]{2,1,0:T(8,128)(2,1)} %pad_maximum_fusion.4.a_ref, bf16[2,512,512]{2,1,0:T(8,128)(2,1)} %pad_maximum_fusion.10.refs_1_.b_ref), custom_call_target="tpu_custom_call" | custom-call | flops 575000000 | bytes 1800000 | tf_op jit(solution)/shard_map/pallas_call | solution.py:205
  (360 shorter events, 130.0 us)
Async XLA Ops:
  3.9 56.9 %collective-permute-start = (bf16[512,2048]{1,0:T(8,128)(2,1)}, bf16[512,2048]{1,0:T(8,128)(2,1)S(1)}, u32[]{:S(2)}, u32[]{:S(2)}) collective-permute-start(bf16[512,2048]{1,0:T(8,128)(2,1)} %constant_dynamic-slice_fusion.21.refs_0_), channel_id=1, source_target_pairs={{0,4},{4,0},{1,5},{5,1},{2,6},{6,2},{3,7},{7,3},{8,12},{12,8},{9,1... | collective-permute-start | bytes 6291464 | tf_op jit(solution)/shard_map/ppermute | solution.py:731
  20.4 29.7 %copy-start.22 = (bf16[624,512]{1,0:T(8,128)(2,1)}, bf16[624,512]{1,0:T(8,128)(2,1)S(1)}, u32[]{:S(2)}) copy-start(bf16[624,512]{1,0:T(8,128)(2,1)S(1)} %fusion.24.refs_3_) | copy-start | bytes 1916932
  20.4 16.8 %collective-permute-start.2 = (bf16[624,512]{1,0:T(8,128)(2,1)S(1)}, bf16[624,512]{1,0:T(8,128)(2,1)S(1)}, u32[]{:S(2)}, u32[]{:S(2)}) collective-permute-start(bf16[624,512]{1,0:T(8,128)(2,1)S(1)} %fusion.24.refs_3_), channel_id=1, source_target_pairs={{0,8},{8,16},{16,24},{1,9},{9,17},{17,25},{2,10},{10,18},{18,26},{... | collective-permute-start | bytes 1916936 | tf_op jit(solution)/shard_map/ppermute | solution.py:708
  23.9 17.6 %collective-permute-start.5 = (bf16[624,512]{1,0:T(8,128)(2,1)S(1)}, bf16[624,512]{1,0:T(8,128)(2,1)}, u32[]{:S(2)}, u32[]{:S(2)}) collective-permute-start(bf16[624,512]{1,0:T(8,128)(2,1)S(1)} %fusion.24.refs_3_), channel_id=1, source_target_pairs={{8,0},{16,8},{24,16},{9,1},{17,9},{25,17},{10,2},{18,10},{26,18},{... | collective-permute-start | bytes 1916936 | tf_op jit(solution)/shard_map/ppermute | solution.py:709
  37.2 13.1 %collective-permute-start.3 = (bf16[624,512]{1,0:T(8,128)(2,1)S(1)}, bf16[624,512]{1,0:T(8,128)(2,1)}, u32[]{:S(2)}, u32[]{:S(2)}) collective-permute-start(bf16[624,512]{1,0:T(8,128)(2,1)S(1)} %collective-permute-done.2.refs_2_.refs_0_), channel_id=1, source_target_pairs={{8,16},{16,24},{9,17},{17,25},{10,18},{18,26},{11,19},{19,27},{12,... | collective-permute-start | bytes 1916936 | tf_op jit(solution)/shard_map/ppermute | solution.py:708
  41.5 17.8 %collective-permute-start.6 = (bf16[624,512]{1,0:T(8,128)(2,1)}, bf16[624,512]{1,0:T(8,128)(2,1)}, u32[]{:S(2)}, u32[]{:S(2)}) collective-permute-start(bf16[624,512]{1,0:T(8,128)(2,1)} %collective-permute-done.5.refs_4_), channel_id=1, source_target_pairs={{8,0},{16,8},{9,1},{17,9},{10,2},{18,10},{11,3},{19,11},{12,4},{20... | collective-permute-start | bytes 1916936 | tf_op jit(solution)/shard_map/ppermute | solution.py:709
  50.3 10.6 %collective-permute-start.4 = (bf16[624,512]{1,0:T(8,128)(2,1)}, bf16[624,512]{1,0:T(8,128)(2,1)S(1)}, u32[]{:S(2)}, u32[]{:S(2)}) collective-permute-start(bf16[624,512]{1,0:T(8,128)(2,1)} %collective-permute-done.3.refs_1_), channel_id=1, source_target_pairs={{16,24},{17,25},{18,26},{19,27},{20,28},{21,29},{22,30},{23,31}} | collective-permute-start | bytes 1916936 | tf_op jit(solution)/shard_map/ppermute | solution.py:708
  59.3 16.2 %collective-permute-start.7 = (bf16[624,512]{1,0:T(8,128)(2,1)}, bf16[624,512]{1,0:T(8,128)(2,1)S(1)}, u32[]{:S(2)}, u32[]{:S(2)}) collective-permute-start(bf16[624,512]{1,0:T(8,128)(2,1)} %collective-permute-done.6.refs_5_), channel_id=1, source_target_pairs={{8,0},{9,1},{10,2},{11,3},{12,4},{13,5},{14,6},{15,7}} | collective-permute-start | bytes 1916936 | tf_op jit(solution)/shard_map/ppermute | solution.py:709
  60.8 37.7 %collective-permute-start.1 = (bf16[512,2048]{1,0:T(8,128)(2,1)S(1)}, bf16[512,2048]{1,0:T(8,128)(2,1)}, u32[]{:S(2)}, u32[]{:S(2)}) collective-permute-start(bf16[512,2048]{1,0:T(8,128)(2,1)S(1)} %collective-permute-done.refs_1_.refs_0_), channel_id=1, source_target_pairs={{0,1},{1,0},{2,3},{3,2},{4,5},{5,4},{6,7},{7,6},{8,9},{9,8},{10,11... | collective-permute-start | bytes 6291464 | tf_op jit(solution)/shard_map/ppermute | solution.py:734
  84.1 114.1 %all-to-all-start = ((bf16[4,1024,512]{2,1,0:T(8,128)(2,1)}), bf16[4,1024,512]{2,1,0:T(8,128)(2,1)}, u32[]{:S(2)}, u32[]{:S(2)}) async-start(bf16[4,1024,512]{2,1,0:T(8,128)(2,1)} %broadcast_in_dim.45), calls=%async_computation | async-start | bytes 8388608 | tf_op jit(solution)/shard_map/all_to_all | solution.py:716
  98.0 52.3 %collective-permute-start.8 = (bf16[512,2048]{1,0:T(8,128)(2,1)}, bf16[512,2048]{1,0:T(8,128)(2,1)}, u32[]{:S(2)}, u32[]{:S(2)}) collective-permute-start(bf16[512,2048]{1,0:T(8,128)(2,1)} %constant_dynamic-slice_fusion.9), channel_id=1, source_target_pairs={{0,4},{4,0},{1,5},{5,1},{2,6},{6,2},{3,7},{7,3},{8,12},{12,8},{9,1... | collective-permute-start | bytes 6291464 | tf_op jit(solution)/shard_map/ppermute | solution.py:731
  124.0 1.7 collective-permute-start.10
  126.9 6.3 %collective-permute-start.11 = (bf16[640,128]{1,0:T(8,128)(2,1)S(1)}, bf16[640,128]{1,0:T(8,128)(2,1)S(1)}, u32[]{:S(2)}, u32[]{:S(2)}) collective-permute-start(bf16[640,128]{1,0:T(8,128)(2,1)S(1)} %get-tuple-element.116), channel_id=1, source_target_pairs={{0,2},{2,0},{1,3},{3,1},{4,6},{6,4},{5,7},{7,5},{8,10},{10,8},{9,1... | collective-permute-start | bytes 491528 | tf_op jit(solution)/shard_map/ppermute | solution.py:737
  128.5 18.8 %collective-permute-start.13 = (bf16[640,128]{1,0:T(8,128)(2,1)S(1)}, bf16[640,128]{1,0:T(8,128)(2,1)S(1)}, u32[]{:S(2)}, u32[]{:S(2)}) collective-permute-start(bf16[640,128]{1,0:T(8,128)(2,1)S(1)} %get-tuple-element.117), channel_id=1, source_target_pairs={{0,4},{4,0},{1,5},{5,1},{2,6},{6,2},{3,7},{7,3},{8,12},{12,8},{9,1... | collective-permute-start | bytes 491528 | tf_op jit(solution)/shard_map/ppermute | solution.py:731
  147.3 5.4 collective-permute-start.12
  147.9 5.3 collective-permute-start.14
  150.3 40.7 %collective-permute-start.9 = (bf16[512,2048]{1,0:T(8,128)(2,1)}, bf16[512,2048]{1,0:T(8,128)(2,1)}, u32[]{:S(2)}, u32[]{:S(2)}) collective-permute-start(bf16[512,2048]{1,0:T(8,128)(2,1)} %collective-permute-done.8.first_ref), channel_id=1, source_target_pairs={{0,1},{1,0},{2,3},{3,2},{4,5},{5,4},{6,7},{7,6},{8,9},{9,8},{10,11... | collective-permute-start | bytes 6291464 | tf_op jit(solution)/shard_map/ppermute | solution.py:734
  153.4 2.5 collective-permute-start.15
  229.8 20.3 %collective-permute-start.17 = (bf16[1024,1024]{1,0:T(8,128)(2,1)}, bf16[1024,1024]{1,0:T(8,128)(2,1)}, u32[]{:S(2)}, u32[]{:S(2)}) collective-permute-start(bf16[1024,1024]{1,0:T(8,128)(2,1)} %convolution_convert_fusion), channel_id=1, source_target_pairs={{0,1},{1,0},{2,3},{3,2},{4,5},{5,4},{6,7},{7,6},{8,9},{9,8},{10,11... | collective-permute-start | bytes 6291464 | tf_op jit(solution)/shard_map/ppermute | solution.py:734
  230.3 25.2 %collective-permute-start.16 = (bf16[1024,1024]{1,0:T(8,128)(2,1)}, bf16[1024,1024]{1,0:T(8,128)(2,1)}, u32[]{:S(2)}, u32[]{:S(2)}) collective-permute-start(bf16[1024,1024]{1,0:T(8,128)(2,1)} %convolution_convert_fusion.1), channel_id=1, source_target_pairs={{0,1},{1,0},{2,3},{3,2},{4,5},{5,4},{6,7},{7,6},{8,9},{9,8},{10,11... | collective-permute-start | bytes 6291464 | tf_op jit(solution)/shard_map/ppermute | solution.py:734
  236.2 116.1 %all-to-all-start.1 = ((bf16[4,512,512]{2,1,0:T(8,128)(2,1)}), bf16[4,512,512]{2,1,0:T(8,128)(2,1)S(1)}, u32[]{:S(2)}, u32[]{:S(2)}) async-start(bf16[4,512,512]{2,1,0:T(8,128)(2,1)} %bitcast.206), calls=%async_computation.1 | async-start | bytes 4194304 | tf_op jit(solution)/shard_map/all_to_all | solution.py:979
  268.0 77.1 %collective-permute-start.18 = (bf16[2,512,512]{2,1,0:T(8,128)(2,1)}, bf16[2,512,512]{2,1,0:T(8,128)(2,1)}, u32[]{:S(2)}, u32[]{:S(2)}) collective-permute-start(bf16[2,512,512]{2,1,0:T(8,128)(2,1)} %pad_maximum_fusion.9), channel_id=1, source_target_pairs={{0,2},{2,0},{1,3},{3,1},{4,6},{6,4},{5,7},{7,5},{8,10},{10,8},{9,1... | collective-permute-start | bytes 3145736 | tf_op jit(solution)/shard_map/ppermute | solution.py:737
  269.5 79.1 %collective-permute-start.20 = (bf16[512,1024]{1,0:T(8,128)(2,1)}, bf16[512,1024]{1,0:T(8,128)(2,1)}, u32[]{:S(2)}, u32[]{:S(2)}) collective-permute-start(bf16[512,1024]{1,0:T(8,128)(2,1)} %slice.297), channel_id=1, source_target_pairs={{0,4},{4,0},{1,5},{5,1},{2,6},{6,2},{3,7},{7,3},{8,12},{12,8},{9,1... | collective-permute-start | bytes 3145736 | tf_op jit(solution)/shard_map/ppermute | solution.py:731
  270.7 71.4 %copy-start.25 = (bf16[2,8,128,128]{3,2,1,0:T(8,128)(2,1)S(1)}, bf16[2,8,128,128]{3,2,1,0:T(8,128)(2,1)}, u32[]{:S(2)}) copy-start(bf16[2,8,128,128]{3,2,1,0:T(8,128)(2,1)} %slice.461) | copy-start | bytes 1572868
  347.8 13.8 %collective-permute-start.19 = (bf16[512,512]{1,0:T(8,128)(2,1)}, bf16[512,512]{1,0:T(8,128)(2,1)}, u32[]{:S(2)}, u32[]{:S(2)}) collective-permute-start(bf16[512,512]{1,0:T(8,128)(2,1)} %get-tuple-element.72), channel_id=1, source_target_pairs={{0,4},{4,0},{1,5},{5,1},{2,6},{6,2},{3,7},{7,3},{8,12},{12,8},{9,1... | collective-permute-start | bytes 1572872 | tf_op jit(solution)/shard_map/ppermute | solution.py:731
  351.8 18.5 %collective-permute-start.21 = (bf16[512,512]{1,0:T(8,128)(2,1)}, bf16[512,512]{1,0:T(8,128)(2,1)}, u32[]{:S(2)}, u32[]{:S(2)}) collective-permute-start(bf16[512,512]{1,0:T(8,128)(2,1)} %slice.462), channel_id=1, source_target_pairs={{0,2},{2,0},{1,3},{3,1},{4,6},{6,4},{5,7},{7,5},{8,10},{10,8},{9,1... | collective-permute-start | bytes 1572872 | tf_op jit(solution)/shard_map/ppermute | solution.py:737
  353.6 73.3 %all-to-all-start.2 = ((bf16[4,128,2048]{2,1,0:T(8,128)(2,1)}), bf16[4,128,2048]{2,1,0:T(8,128)(2,1)S(1)}, u32[]{:S(2)}, u32[]{:S(2)}) async-start(bf16[4,128,2048]{2,1,0:T(8,128)(2,1)} %bitcast.199), calls=%async_computation.2 | async-start | bytes 4194304 | tf_op jit(solution)/shard_map/all_to_all | solution.py:980
  367.9 3.5 collective-permute-start.22
  369.3 24.3 %collective-permute-start.28 = (bf16[512,512]{1,0:T(8,128)(2,1)S(1)}, bf16[512,512]{1,0:T(8,128)(2,1)S(1)}, u32[]{:S(2)}, u32[]{:S(2)}) collective-permute-start(bf16[512,512]{1,0:T(8,128)(2,1)S(1)} %get-tuple-element.97), channel_id=1, source_target_pairs={{0,4},{4,0},{1,5},{5,1},{2,6},{6,2},{3,7},{7,3},{8,12},{12,8},{9,1... | collective-permute-start | bytes 1572872 | tf_op jit(solution)/shard_map/ppermute | solution.py:731
  371.6 6.3 %collective-permute-start.23 = (bf16[640,128]{1,0:T(8,128)(2,1)S(1)}, bf16[640,128]{1,0:T(8,128)(2,1)S(1)}, u32[]{:S(2)}, u32[]{:S(2)}) collective-permute-start(bf16[640,128]{1,0:T(8,128)(2,1)S(1)} %get-tuple-element.110), channel_id=1, source_target_pairs={{0,2},{2,0},{1,3},{3,1},{4,6},{6,4},{5,7},{7,5},{8,10},{10,8},{9,1... | collective-permute-start | bytes 491528 | tf_op jit(solution)/shard_map/ppermute | solution.py:737
  372.9 14.2 %collective-permute-start.25 = (bf16[640,128]{1,0:T(8,128)(2,1)S(1)}, bf16[640,128]{1,0:T(8,128)(2,1)S(1)}, u32[]{:S(2)}, u32[]{:S(2)}) collective-permute-start(bf16[640,128]{1,0:T(8,128)(2,1)S(1)} %get-tuple-element.111), channel_id=1, source_target_pairs={{0,4},{4,0},{1,5},{5,1},{2,6},{6,2},{3,7},{7,3},{8,12},{12,8},{9,1... | collective-permute-start | bytes 491528 | tf_op jit(solution)/shard_map/ppermute | solution.py:731
  387.2 5.7 %collective-permute-start.24 = (bf16[640,128]{1,0:T(8,128)(2,1)S(1)}, bf16[640,128]{1,0:T(8,128)(2,1)S(1)}, u32[]{:S(2)}, u32[]{:S(2)}) collective-permute-start(bf16[640,128]{1,0:T(8,128)(2,1)S(1)} %get-tuple-element.108), channel_id=1, source_target_pairs={{0,4},{4,0},{1,5},{5,1},{2,6},{6,2},{3,7},{7,3},{8,12},{12,8},{9,1... | collective-permute-start | bytes 491528 | tf_op jit(solution)/shard_map/ppermute | solution.py:731
  388.1 5.4 collective-permute-start.26
  393.6 1.7 collective-permute-start.27
  448.1 16.0 %collective-permute-start.30 = (bf16[1024,1024]{1,0:T(8,128)(2,1)}, bf16[1024,1024]{1,0:T(8,128)(2,1)S(1)}, u32[]{:S(2)}, u32[]{:S(2)}) collective-permute-start(bf16[1024,1024]{1,0:T(8,128)(2,1)} %get-tuple-element.65), channel_id=1, source_target_pairs={{0,1},{1,0},{2,3},{3,2},{4,5},{5,4},{6,7},{7,6},{8,9},{9,8},{10,11... | collective-permute-start | bytes 6291464 | tf_op jit(solution)/shard_map/ppermute | solution.py:734
  448.2 19.9 %collective-permute-start.29 = (bf16[1024,1024]{1,0:T(8,128)(2,1)}, bf16[1024,1024]{1,0:T(8,128)(2,1)}, u32[]{:S(2)}, u32[]{:S(2)}) collective-permute-start(bf16[1024,1024]{1,0:T(8,128)(2,1)} %get-tuple-element.63), channel_id=1, source_target_pairs={{0,1},{1,0},{2,3},{3,2},{4,5},{5,4},{6,7},{7,6},{8,9},{9,8},{10,11... | collective-permute-start | bytes 6291464 | tf_op jit(solution)/shard_map/ppermute | solution.py:734
  449.6 71.8 %all-to-all-start.3 = ((bf16[4,608,512]{2,1,0:T(8,128)(2,1)}), bf16[4,608,512]{2,1,0:T(8,128)(2,1)}, u32[]{:S(2)}, u32[]{:S(2)}) async-start(bf16[4,608,512]{2,1,0:T(8,128)(2,1)} %pad_maximum_fusion.refs_0_), calls=%async_computation.3 | async-start | bytes 4980736 | tf_op jit(solution)/shard_map/all_to_all | solution.py:720
  466.9 26.1 %collective-permute-start.33 = (bf16[512,1024]{1,0:T(8,128)(2,1)S(1)}, bf16[512,1024]{1,0:T(8,128)(2,1)S(1)}, u32[]{:S(2)}, u32[]{:S(2)}) collective-permute-start(bf16[512,1024]{1,0:T(8,128)(2,1)S(1)} %slice.314), channel_id=1, source_target_pairs={{0,4},{4,0},{1,5},{5,1},{2,6},{6,2},{3,7},{7,3},{8,12},{12,8},{9,1... | collective-permute-start | bytes 3145736 | tf_op jit(solution)/shard_map/ppermute | solution.py:731
  471.1 26.1 %collective-permute-start.31 = (bf16[2,512,512]{2,1,0:T(8,128)(2,1)S(1)}, bf16[2,512,512]{2,1,0:T(8,128)(2,1)S(1)}, u32[]{:S(2)}, u32[]{:S(2)}) collective-permute-start(bf16[2,512,512]{2,1,0:T(8,128)(2,1)S(1)} %pad_maximum_fusion.11), channel_id=1, source_target_pairs={{0,2},{2,0},{1,3},{3,1},{4,6},{6,4},{5,7},{7,5},{8,10},{10,8},{9,1... | collective-permute-start | bytes 3145736 | tf_op jit(solution)/shard_map/ppermute | solution.py:737
  473.8 30.4 %collective-permute-start.37 = (bf16[128,2048]{1,0:T(8,128)(2,1)S(1)}, bf16[128,2048]{1,0:T(8,128)(2,1)S(1)}, u32[]{:S(2)}, u32[]{:S(2)}) collective-permute-start(bf16[128,2048]{1,0:T(8,128)(2,1)S(1)} %add_convert_fusion.1), channel_id=1, source_target_pairs={{0,4},{4,0},{1,5},{5,1},{2,6},{6,2},{3,7},{7,3},{8,12},{12,8},{9,1... | collective-permute-start | bytes 1572872 | tf_op jit(solution)/shard_map/ppermute | solution.py:731
  493.4 13.9 %collective-permute-start.34 = (bf16[512,512]{1,0:T(8,128)(2,1)S(1)}, bf16[512,512]{1,0:T(8,128)(2,1)S(1)}, u32[]{:S(2)}, u32[]{:S(2)}) collective-permute-start(bf16[512,512]{1,0:T(8,128)(2,1)S(1)} %slice.460), channel_id=1, source_target_pairs={{0,2},{2,0},{1,3},{3,1},{4,6},{6,4},{5,7},{7,5},{8,10},{10,8},{9,1... | collective-permute-start | bytes 1572872 | tf_op jit(solution)/shard_map/ppermute | solution.py:737
  497.4 16.9 %collective-permute-start.32 = (bf16[512,512]{1,0:T(8,128)(2,1)S(1)}, bf16[512,512]{1,0:T(8,128)(2,1)S(1)}, u32[]{:S(2)}, u32[]{:S(2)}) collective-permute-start(bf16[512,512]{1,0:T(8,128)(2,1)S(1)} %fusion.9), channel_id=1, source_target_pairs={{0,4},{4,0},{1,5},{5,1},{2,6},{6,2},{3,7},{7,3},{8,12},{12,8},{9,1... | collective-permute-start | bytes 1572872 | tf_op jit(solution)/shard_map/ppermute | solution.py:731
  517.4 2.4 collective-permute-start.35
  519.8 8.8 %collective-permute-start.36 = (f32[2,512]{1,0:T(2,128)S(1)}, f32[2,512]{1,0:T(2,128)S(1)}, u32[]{:S(2)}, u32[]{:S(2)}) collective-permute-start(f32[2,512]{1,0:T(2,128)S(1)} %add.408), channel_id=1, source_target_pairs={{0,2},{2,0},{1,3},{3,1},{4,6},{6,4},{5,7},{7,5},{8,10},{10,8},{9,1... | collective-permute-start | bytes 12296 | tf_op jit(solution)/shard_map/ppermute | solution.py:737
  524.9 3.7 collective-permute-start.38
  527.4 15.9 %collective-permute-start.41 = (bf16[608,512]{1,0:T(8,128)(2,1)S(1)}, bf16[608,512]{1,0:T(8,128)(2,1)S(1)}, u32[]{:S(2)}, u32[]{:S(2)}) collective-permute-start(bf16[608,512]{1,0:T(8,128)(2,1)S(1)} %get-tuple-element.68), channel_id=1, source_target_pairs={{0,4},{4,0},{1,5},{5,1},{2,6},{6,2},{3,7},{7,3},{8,12},{12,8},{9,1... | collective-permute-start | bytes 1867784 | tf_op jit(solution)/shard_map/ppermute | solution.py:731
  528.6 1.2 collective-permute-start.39
  529.8 4.0 collective-permute-start.40
  (56 other events, 326.1 us)

commit v5 on v4

--- a/solution.py
+++ b/solution.py
@@ -418,7 +418,7 @@
         ),
         out_shape=[jax.ShapeDtypeStruct((n, seqs * length // n, inner), bf16)]
         + [jax.ShapeDtypeStruct((8, inner), f32), jax.ShapeDtypeStruct((seqs, length, 2 * LANE), bf16)],
-        cost_estimate=cost(10),
+        cost_estimate=cost(160),
         compiler_params=PARAMS,
     )(place, packed, direct, x_part, x_part, vec, masks, select_low, select_state)
 
@@ -1035,7 +1035,7 @@
         ],
         axis=1,
     ).astype(bf16)
-    sent = after(middle, grad_x[0])
+    sent = after(middle, conv_sums)
     small = small + sent.astype(bf16)
     out_pair = moves.both((jnp.sum(middle.astype(f32), axis=0) + sent.astype(f32)).astype(bf16))
     small = jnp.pad(small, ((0, 0), (0, 2 * LANE - small.shape[1])))

time: 565 us -> 563 us (level)
  transfers between devices with their start and end apart: 46 -> 46, of which waited for: 22 -> 22; matrix products, arithmetic and copies ran while one was open for 22% -> 21% of each run, Pallas kernels for 30% -> 30%
where the time goes in v5:
time: 563 us; the launch traced here: 555 us
  Pallas kernels  204 us (36%)
  waiting for transfers between devices  121 us (21%)
  starting transfers between devices  60.7 us (11%)
  local copies, waits for them, and re-layouts  55.7 us (10%)
  other arithmetic  51.3 us (9%)
  matrix products  46.5 us (8%)
  between operations  16.3 us (3%)
    pallas_call x1, Pallas kernels, scan_backward(): pl.pallas_call(functools.partial(backward_kernel, S, G), grid=(T // LANE,...  69.6 us
    ppermute x14, waiting for transfers between devices, across(): return lax.ppermute(array, 'context', [(0, 1), (1, 0)])  66.8 us
    pallas_call x1, Pallas kernels, scan_forward(): pl.pallas_call(functools.partial(forward_kernel, S, G), grid=(T // LANE,)...  33.7 us
    dot_general x6, matrix products, t_dot(): lax.dot_general(a, b, (((0,), (0,)), ((), ())), preferred_element_type=f32)  29.7 us
    ppermute x3, waiting for transfers between devices, line_gather(): lax.ppermute(left, axis, [(i, i - 1) for i in range(1, count - step + 1)])  25.6 us
    pallas_call x2, Pallas kernels, products(): pl.pallas_call(kernel, grid_spec=pltpu.PrefetchScalarGridSpec(num_scalar_...  18.9 us
    pallas_call x1, Pallas kernels, gates(): pl.pallas_call(kernel, grid_spec=pltpu.PrefetchScalarGridSpec(num_scalar_...  18.4 us
    dot_general x4, matrix products, dot(): return jnp.dot(a, b, preferred_element_type=f32).astype(out)  16.8 us
  transfers between devices with their start and end apart: 46, of which 22 were waited for; matrix products, arithmetic and copies ran while one was open for 21% of the time, Pallas kernels for 30%

profile of v5, /device:TPU:0, one launch (start us, length us, event | category | flops | bytes accessed | tf_op | source)
XLA Modules:
  0.0 555.0 jit_solution(6445196350861300841)
XLA Ops:
  0.7 3.2 constant_dynamic-slice_fusion.21.refs_0_
  3.9 2.9 collective-permute-start
  10.0 6.8 %fusion.58 = (bf16[512,1,1024]{2,1,0:T(2,128)(2,1)}, bf16[512,1,1024]{2,1,0:T(2,128)(2,1)}) fusion(bf16[512,2,1024]{2,1,0:T(2,128)(2,1)} %param.17), kind=kLoop, calls=%fused_computation.223 | loop fusion | bytes 4194304 | tf_op jit(solution)/shard_map/slice | solution.py:942
  20.4 3.5 collective-permute-start.2
  25.7 11.5 %collective-permute-done.2.refs_2_.refs_0_ = bf16[624,512]{1,0:T(8,128)(2,1)S(1)} collective-permute-done((bf16[624,512]{1,0:T(8,128)(2,1)S(1)}, bf16[624,512]{1,0:T(8,128)(2,1)S(1)}, u32[]{:S(2)}, u32[]{:S(2)}) %collective-permute-start.2) | collective-permute-done | bytes 639008 | tf_op jit(solution)/shard_map/ppermute | solution.py:708
  38.7 2.7 collective-permute-done.5.refs_4_
  51.0 8.3 %collective-permute-done.6.refs_5_ = bf16[624,512]{1,0:T(8,128)(2,1)} collective-permute-done((bf16[624,512]{1,0:T(8,128)(2,1)}, bf16[624,512]{1,0:T(8,128)(2,1)}, u32[]{:S(2)}, u32[]{:S(2)}) %collective-permute-start.6) | collective-permute-done | bytes 639008 | tf_op jit(solution)/shard_map/ppermute | solution.py:709
  60.9 14.6 %collective-permute-done.7.refs_6_ = bf16[624,512]{1,0:T(8,128)(2,1)S(1)} collective-permute-done((bf16[624,512]{1,0:T(8,128)(2,1)}, bf16[624,512]{1,0:T(8,128)(2,1)S(1)}, u32[]{:S(2)}, u32[]{:S(2)}) %collective-permute-start.7) | collective-permute-done | bytes 639008 | tf_op jit(solution)/shard_map/ppermute | solution.py:709
  76.3 4.2 shard_map.221
  84.1 5.5 all-to-all-start
  94.8 3.2 constant_dynamic-slice_fusion.9
  98.5 11.0 %shard_map.222 = (bf16[2,1024,2048]{2,1,0:T(8,128)(2,1)}, f32[1024,128]{1,0:T(8,128)}) custom-call(s32[1]{0:T(128)} %bitcast.1.place_ref, bf16[1024,2048]{1,0:T(8,128)(2,1)} %bitcast.189, bf16[512,2048]{1,0:T(8,128)(2,1)} %copy-done.17, bf16[512,2048]{1,0:T(8,128)(2,1)} %collective-permute-done.1.refs_2_, f32[1,2048]{1,0:T(1,128)} %bitcast.230), custom_call_target="tpu_custom_call" | custom-call | flops 920000000 | bytes 2880000 | tf_op jit(solution)/shard_map/pallas_call | solution.py:121
  109.5 13.3 %shard_map.227 = (bf16[2,1024,512]{2,1,0:T(8,128)(2,1)}, bf16[2,1024,512]{2,1,0:T(8,128)(2,1)}, f32[2,8,160,128]{3,2,1,0:T(8,128)}) custom-call(s32[1]{0:T(128)} %bitcast.place_ref, bf16[2,1024,2048]{2,1,0:T(8,128)(2,1)} %get-tuple-element.40.in_ref.a_ref, bf16[2048,512]{1,0:T(8,128)(2,1)} %bitcast.180, f32[8,512]{1,0:T(8,128)} %maximum_maximum_fusion.vec_ref, ...), custom_call_target="tpu_custom_call" | custom-call | flops 1035000000 | bytes 3240000 | tf_op jit(solution)/shard_map/pallas_call | solution.py:290
  130.0 3.2 collective-permute-done.11
  133.2 14.1 %collective-permute-done.13 = bf16[640,128]{1,0:T(8,128)(2,1)S(1)} collective-permute-done((bf16[640,128]{1,0:T(8,128)(2,1)S(1)}, bf16[640,128]{1,0:T(8,128)(2,1)S(1)}, u32[]{:S(2)}, u32[]{:S(2)}) %collective-permute-start.13) | collective-permute-done | bytes 163872 | tf_op jit(solution)/shard_map/ppermute | solution.py:731
  157.3 33.7 %shard_map.228 = (f32[2,1024,512]{2,1,0:T(8,128)}, f32[2,1024,512]{2,1,0:T(8,128)}, f32[8,128,128]{2,1,0:T(8,128)}) custom-call(f32[2,8,160,128]{3,2,1,0:T(8,128)} %bitcast.202, bf16[2,1024,512]{2,1,0:T(8,128)(2,1)} %get-tuple-element.44.u_ref, f32[2,1024,128]{2,1,0:T(8,128)} %and_convert_fusion.refs_7_.masks_ref, bf16[128,512]{1,0:T(8,128)(2,1)} %bitcast.240, ...), custom_call_target="tpu_custom_call" | custom-call | flops 3449999872 | bytes 10800000 | tf_op jit(solution)/shard_map/pallas_call | solution.py:639
  191.0 7.1 %shard_map.224.refs_1_ = bf16[1024,2048]{1,0:T(8,128)(2,1)} custom-call(s32[1]{0:T(128)} %bitcast.1.place_ref, bf16[512,2048]{1,0:T(8,128)(2,1)} %collective-permute-done.8.first_ref, bf16[512,2048]{1,0:T(8,128)(2,1)} %collective-permute-done.9.second_ref), custom_call_target="tpu_custom_call" | custom-call | flops 460000000 | bytes 1440000 | tf_op jit(solution)/shard_map/pallas_call | solution.py:71
  201.5 3.0 slice.272
  204.6 18.4 %shard_map.229 = (bf16[2,1024,512]{2,1,0:T(8,128)(2,1)}, bf16[2,1024,512]{2,1,0:T(8,128)(2,1)}, f32[2,1024,512]{2,1,0:T(8,128)}) custom-call(s32[1]{0:T(128)} %bitcast.place_ref, bf16[2,1024,2048]{2,1,0:T(8,128)(2,1)} %get-tuple-element.40.in_ref.a_ref, bf16[1024,2048]{1,0:T(8,128)(2,1)} %bitcast.177, bf16[1024,2048]{1,0:T(8,128)(2,1)} %shard_map.224.refs_1_, ...), custom_call_target="tpu_custom_call" | custom-call | flops 1610000000 | bytes 5040000 | tf_op jit(solution)/shard_map/pallas_call | solution.py:333
  223.2 4.0 convolution_convert_fusion
  227.2 2.6 convolution_convert_fusion.1
  230.3 5.9 %bitcast_convert_fusion.1 = bf16[2048,512]{1,0:T(8,128)(2,1)} fusion(bf16[2,1024,2048]{2,1,0:T(8,128)(2,1)S(1)} %bitcast.184, bf16[2,1024,512]{2,1,0:T(8,128)(2,1)S(1)} %copy-done.4), kind=kOutput, calls=%fused_computation.2 | convolution fusion | flops 4296015872 | bytes 12582912 | tf_op jit(solution)/shard_map/dot_general | solution.py:855
  236.2 5.1 all-to-all-start.1
  241.3 5.0 fusion.14
  246.3 3.7 add_convert_fusion
  250.0 5.4 fusion.63
  255.4 4.9 convert_add_fusion.3.refs_0_
  270.7 69.6 %shard_map.231 = (bf16[2,1024,512]{2,1,0:T(8,128)(2,1)}, f32[2,1024,512]{2,1,0:T(8,128)}, f32[2,8,160,128]{3,2,1,0:T(8,128)}, f32[16,512]{1,0:T(8,128)}, f32[8,512]{1,0:T(8,128)}) custom-call(f32[2,8,160,128]{3,2,1,0:T(8,128)} %bitcast.203, bf16[2,1024,512]{2,1,0:T(8,128)(2,1)} %get-tuple-element.44.u_ref, f32[2,1024,512]{2,1,0:T(8,128)} %get-tuple-element.49.step_ref, ...), custom_call_target="tpu_custom_call" | custom-call | flops 9774999552 | bytes 30600000 | tf_op jit(solution)/shard_map/pallas_call | solution.py:664
  342.2 2.9 convolution_convert_fusion.2
  345.0 2.8 fusion.56
  353.6 5.3 all-to-all-start.2
  361.6 3.2 convert_add_fusion.5
  373.9 3.9 collective-permute-done.23
  377.8 9.3 %collective-permute-done.25 = bf16[640,128]{1,0:T(8,128)(2,1)S(1)} collective-permute-done((bf16[640,128]{1,0:T(8,128)(2,1)S(1)}, bf16[640,128]{1,0:T(8,128)(2,1)S(1)}, u32[]{:S(2)}, u32[]{:S(2)}) %collective-permute-start.25) | collective-permute-done | bytes 163872 | tf_op jit(solution)/shard_map/ppermute | solution.py:731
  398.4 15.9 %shard_map.234 = (bf16[2,1024,512]{2,1,0:T(8,128)(2,1)}, f32[8,512]{1,0:T(8,128)}, bf16[2,1024,256]{2,1,0:T(8,128)(2,1)}) custom-call(s32[1]{0:T(128)} %bitcast.place_ref, f32[2,8,160,128]{3,2,1,0:T(8,128)} %bitcast.198, f32[2,1024,512]{2,1,0:T(8,128)} %get-tuple-element.54.d_ref, bf16[2,1024,512]{2,1,0:T(8,128)(2,1)} %get-tuple-element.55.x_ref.edge_ref, ...), custom_call_target="tpu_custom_call" | custom-call | flops 18400000000 | bytes 57600000 | tf_op jit(solution)/shard_map/pallas_call | solution.py:401
  415.1 9.9 %bitcast_convert_fusion = bf16[2048,512]{1,0:T(8,128)(2,1)} fusion(bf16[2,1024,2048]{2,1,0:T(8,128)(2,1)} %get-tuple-element.40.in_ref.a_ref, bf16[2,1024,512]{2,1,0:T(8,128)(2,1)} %get-tuple-element.56.refs_0_.refs_1_), kind=kOutput, calls=%fused_computation.1 | convolution fusion | flops 4296015872 | bytes 12582912 | tf_op jit(solution)/shard_map/dot_general | solution.py:855
  436.7 9.6 %shard_map.238 = (bf16[1024,1024]{1,0:T(8,128)(2,1)}, bf16[1024,1024]{1,0:T(8,128)(2,1)}) custom-call(s32[2]{0:T(128)} %get-tuple-element.132.blocks_ref, bf16[2,1024,512]{2,1,0:T(8,128)(2,1)} %get-tuple-element.56.refs_0_.refs_1_, bf16[2,1024,512]{2,1,0:T(8,128)(2,1)} %get-tuple-element.56.refs_0_.refs_1_, ...), custom_call_target="tpu_custom_call" | custom-call | flops 575000000 | bytes 1800000 | tf_op jit(solution)/shard_map/pallas_call | solution.py:179
  447.7 5.1 all-to-all-start.3
  452.8 9.4 %shard_map.237 = (bf16[1024,1024]{1,0:T(8,128)(2,1)}, bf16[1024,1024]{1,0:T(8,128)(2,1)}) custom-call(s32[2]{0:T(128)} %get-tuple-element.131.blocks_ref, bf16[2,1024,512]{2,1,0:T(8,128)(2,1)} %get-tuple-element.56.refs_0_.refs_1_, bf16[2,1024,512]{2,1,0:T(8,128)(2,1)} %get-tuple-element.56.refs_0_.refs_1_, ...), custom_call_target="tpu_custom_call" | custom-call | flops 575000000 | bytes 1800000 | tf_op jit(solution)/shard_map/pallas_call | solution.py:179
  462.2 2.7 convert_add_fusion
  472.9 18.2 %collective-permute-done.33 = bf16[512,1024]{1,0:T(8,128)(2,1)S(1)} collective-permute-done((bf16[512,1024]{1,0:T(8,128)(2,1)S(1)}, bf16[512,1024]{1,0:T(8,128)(2,1)S(1)}, u32[]{:S(2)}, u32[]{:S(2)}) %collective-permute-start.33) | collective-permute-done | bytes 1048608 | tf_op jit(solution)/shard_map/ppermute | solution.py:731
  496.7 5.6 %collective-permute-done.37 = bf16[128,2048]{1,0:T(8,128)(2,1)S(1)} collective-permute-done((bf16[128,2048]{1,0:T(8,128)(2,1)S(1)}, bf16[128,2048]{1,0:T(8,128)(2,1)S(1)}, u32[]{:S(2)}, u32[]{:S(2)}) %collective-permute-start.37) | collective-permute-done | bytes 524320 | tf_op jit(solution)/shard_map/ppermute | solution.py:731
  502.4 3.0 collective-permute-done.34
  505.6 6.8 %collective-permute-done.32 = bf16[512,512]{1,0:T(8,128)(2,1)S(1)} collective-permute-done((bf16[512,512]{1,0:T(8,128)(2,1)S(1)}, bf16[512,512]{1,0:T(8,128)(2,1)S(1)}, u32[]{:S(2)}, u32[]{:S(2)}) %collective-permute-start.32) | collective-permute-done | bytes 524320 | tf_op jit(solution)/shard_map/ppermute | solution.py:731
  512.9 2.6 fusion.2
  528.4 3.5 fusion.5
  532.5 8.9 %collective-permute-done.41 = bf16[608,512]{1,0:T(8,128)(2,1)S(1)} collective-permute-done((bf16[608,512]{1,0:T(8,128)(2,1)S(1)}, bf16[608,512]{1,0:T(8,128)(2,1)S(1)}, u32[]{:S(2)}, u32[]{:S(2)}) %collective-permute-start.41) | collective-permute-done | bytes 622624 | tf_op jit(solution)/shard_map/ppermute | solution.py:731
  548.1 6.5 %shard_map.240 = f32[512,2,1024]{2,1,0:T(2,128)} custom-call(bf16[2,608,512]{2,1,0:T(8,128)(2,1)} %pad_maximum_fusion.4.a_ref, bf16[2,512,512]{2,1,0:T(8,128)(2,1)} %pad_maximum_fusion.10.refs_1_.b_ref), custom_call_target="tpu_custom_call" | custom-call | flops 575000000 | bytes 1800000 | tf_op jit(solution)/shard_map/pallas_call | solution.py:205
  (359 shorter events, 127.6 us)
Async XLA Ops:
  3.9 56.9 %collective-permute-start = (bf16[512,2048]{1,0:T(8,128)(2,1)}, bf16[512,2048]{1,0:T(8,128)(2,1)S(1)}, u32[]{:S(2)}, u32[]{:S(2)}) collective-permute-start(bf16[512,2048]{1,0:T(8,128)(2,1)} %constant_dynamic-slice_fusion.21.refs_0_), channel_id=1, source_target_pairs={{0,4},{4,0},{1,5},{5,1},{2,6},{6,2},{3,7},{7,3},{8,12},{12,8},{9,1... | collective-permute-start | bytes 6291464 | tf_op jit(solution)/shard_map/ppermute | solution.py:731
  20.4 29.7 %copy-start.21 = (bf16[624,512]{1,0:T(8,128)(2,1)}, bf16[624,512]{1,0:T(8,128)(2,1)S(1)}, u32[]{:S(2)}) copy-start(bf16[624,512]{1,0:T(8,128)(2,1)S(1)} %fusion.24.refs_3_) | copy-start | bytes 1916932
  20.4 16.8 %collective-permute-start.2 = (bf16[624,512]{1,0:T(8,128)(2,1)S(1)}, bf16[624,512]{1,0:T(8,128)(2,1)S(1)}, u32[]{:S(2)}, u32[]{:S(2)}) collective-permute-start(bf16[624,512]{1,0:T(8,128)(2,1)S(1)} %fusion.24.refs_3_), channel_id=1, source_target_pairs={{0,8},{8,16},{16,24},{1,9},{9,17},{17,25},{2,10},{10,18},{18,26},{... | collective-permute-start | bytes 1916936 | tf_op jit(solution)/shard_map/ppermute | solution.py:708
  23.9 17.6 %collective-permute-start.5 = (bf16[624,512]{1,0:T(8,128)(2,1)S(1)}, bf16[624,512]{1,0:T(8,128)(2,1)}, u32[]{:S(2)}, u32[]{:S(2)}) collective-permute-start(bf16[624,512]{1,0:T(8,128)(2,1)S(1)} %fusion.24.refs_3_), channel_id=1, source_target_pairs={{8,0},{16,8},{24,16},{9,1},{17,9},{25,17},{10,2},{18,10},{26,18},{... | collective-permute-start | bytes 1916936 | tf_op jit(solution)/shard_map/ppermute | solution.py:709
  37.2 13.1 %collective-permute-start.3 = (bf16[624,512]{1,0:T(8,128)(2,1)S(1)}, bf16[624,512]{1,0:T(8,128)(2,1)}, u32[]{:S(2)}, u32[]{:S(2)}) collective-permute-start(bf16[624,512]{1,0:T(8,128)(2,1)S(1)} %collective-permute-done.2.refs_2_.refs_0_), channel_id=1, source_target_pairs={{8,16},{16,24},{9,17},{17,25},{10,18},{18,26},{11,19},{19,27},{12,... | collective-permute-start | bytes 1916936 | tf_op jit(solution)/shard_map/ppermute | solution.py:708
  41.5 17.8 %collective-permute-start.6 = (bf16[624,512]{1,0:T(8,128)(2,1)}, bf16[624,512]{1,0:T(8,128)(2,1)}, u32[]{:S(2)}, u32[]{:S(2)}) collective-permute-start(bf16[624,512]{1,0:T(8,128)(2,1)} %collective-permute-done.5.refs_4_), channel_id=1, source_target_pairs={{8,0},{16,8},{9,1},{17,9},{10,2},{18,10},{11,3},{19,11},{12,4},{20... | collective-permute-start | bytes 1916936 | tf_op jit(solution)/shard_map/ppermute | solution.py:709
  50.3 10.6 %collective-permute-start.4 = (bf16[624,512]{1,0:T(8,128)(2,1)}, bf16[624,512]{1,0:T(8,128)(2,1)S(1)}, u32[]{:S(2)}, u32[]{:S(2)}) collective-permute-start(bf16[624,512]{1,0:T(8,128)(2,1)} %collective-permute-done.3.refs_1_), channel_id=1, source_target_pairs={{16,24},{17,25},{18,26},{19,27},{20,28},{21,29},{22,30},{23,31}} | collective-permute-start | bytes 1916936 | tf_op jit(solution)/shard_map/ppermute | solution.py:708
  59.3 16.2 %collective-permute-start.7 = (bf16[624,512]{1,0:T(8,128)(2,1)}, bf16[624,512]{1,0:T(8,128)(2,1)S(1)}, u32[]{:S(2)}, u32[]{:S(2)}) collective-permute-start(bf16[624,512]{1,0:T(8,128)(2,1)} %collective-permute-done.6.refs_5_), channel_id=1, source_target_pairs={{8,0},{9,1},{10,2},{11,3},{12,4},{13,5},{14,6},{15,7}} | collective-permute-start | bytes 1916936 | tf_op jit(solution)/shard_map/ppermute | solution.py:709
  60.8 37.7 %collective-permute-start.1 = (bf16[512,2048]{1,0:T(8,128)(2,1)S(1)}, bf16[512,2048]{1,0:T(8,128)(2,1)}, u32[]{:S(2)}, u32[]{:S(2)}) collective-permute-start(bf16[512,2048]{1,0:T(8,128)(2,1)S(1)} %collective-permute-done.refs_1_.refs_0_), channel_id=1, source_target_pairs={{0,1},{1,0},{2,3},{3,2},{4,5},{5,4},{6,7},{7,6},{8,9},{9,8},{10,11... | collective-permute-start | bytes 6291464 | tf_op jit(solution)/shard_map/ppermute | solution.py:734
  84.1 114.1 %all-to-all-start = ((bf16[4,1024,512]{2,1,0:T(8,128)(2,1)}), bf16[4,1024,512]{2,1,0:T(8,128)(2,1)}, u32[]{:S(2)}, u32[]{:S(2)}) async-start(bf16[4,1024,512]{2,1,0:T(8,128)(2,1)} %broadcast_in_dim.45), calls=%async_computation | async-start | bytes 8388608 | tf_op jit(solution)/shard_map/all_to_all | solution.py:716
  98.0 52.3 %collective-permute-start.8 = (bf16[512,2048]{1,0:T(8,128)(2,1)}, bf16[512,2048]{1,0:T(8,128)(2,1)}, u32[]{:S(2)}, u32[]{:S(2)}) collective-permute-start(bf16[512,2048]{1,0:T(8,128)(2,1)} %constant_dynamic-slice_fusion.9), channel_id=1, source_target_pairs={{0,4},{4,0},{1,5},{5,1},{2,6},{6,2},{3,7},{7,3},{8,12},{12,8},{9,1... | collective-permute-start | bytes 6291464 | tf_op jit(solution)/shard_map/ppermute | solution.py:731
  124.0 1.7 collective-permute-start.10
  126.9 6.3 %collective-permute-start.11 = (bf16[640,128]{1,0:T(8,128)(2,1)S(1)}, bf16[640,128]{1,0:T(8,128)(2,1)S(1)}, u32[]{:S(2)}, u32[]{:S(2)}) collective-permute-start(bf16[640,128]{1,0:T(8,128)(2,1)S(1)} %get-tuple-element.116), channel_id=1, source_target_pairs={{0,2},{2,0},{1,3},{3,1},{4,6},{6,4},{5,7},{7,5},{8,10},{10,8},{9,1... | collective-permute-start | bytes 491528 | tf_op jit(solution)/shard_map/ppermute | solution.py:737
  128.5 18.8 %collective-permute-start.13 = (bf16[640,128]{1,0:T(8,128)(2,1)S(1)}, bf16[640,128]{1,0:T(8,128)(2,1)S(1)}, u32[]{:S(2)}, u32[]{:S(2)}) collective-permute-start(bf16[640,128]{1,0:T(8,128)(2,1)S(1)} %get-tuple-element.117), channel_id=1, source_target_pairs={{0,4},{4,0},{1,5},{5,1},{2,6},{6,2},{3,7},{7,3},{8,12},{12,8},{9,1... | collective-permute-start | bytes 491528 | tf_op jit(solution)/shard_map/ppermute | solution.py:731
  147.3 5.4 collective-permute-start.12
  147.9 5.3 collective-permute-start.14
  150.3 40.7 %collective-permute-start.9 = (bf16[512,2048]{1,0:T(8,128)(2,1)}, bf16[512,2048]{1,0:T(8,128)(2,1)}, u32[]{:S(2)}, u32[]{:S(2)}) collective-permute-start(bf16[512,2048]{1,0:T(8,128)(2,1)} %collective-permute-done.8.first_ref), channel_id=1, source_target_pairs={{0,1},{1,0},{2,3},{3,2},{4,5},{5,4},{6,7},{7,6},{8,9},{9,8},{10,11... | collective-permute-start | bytes 6291464 | tf_op jit(solution)/shard_map/ppermute | solution.py:734
  153.4 2.5 collective-permute-start.15
  229.8 20.3 %collective-permute-start.17 = (bf16[1024,1024]{1,0:T(8,128)(2,1)}, bf16[1024,1024]{1,0:T(8,128)(2,1)}, u32[]{:S(2)}, u32[]{:S(2)}) collective-permute-start(bf16[1024,1024]{1,0:T(8,128)(2,1)} %convolution_convert_fusion), channel_id=1, source_target_pairs={{0,1},{1,0},{2,3},{3,2},{4,5},{5,4},{6,7},{7,6},{8,9},{9,8},{10,11... | collective-permute-start | bytes 6291464 | tf_op jit(solution)/shard_map/ppermute | solution.py:734
  230.3 25.2 %collective-permute-start.16 = (bf16[1024,1024]{1,0:T(8,128)(2,1)}, bf16[1024,1024]{1,0:T(8,128)(2,1)}, u32[]{:S(2)}, u32[]{:S(2)}) collective-permute-start(bf16[1024,1024]{1,0:T(8,128)(2,1)} %convolution_convert_fusion.1), channel_id=1, source_target_pairs={{0,1},{1,0},{2,3},{3,2},{4,5},{5,4},{6,7},{7,6},{8,9},{9,8},{10,11... | collective-permute-start | bytes 6291464 | tf_op jit(solution)/shard_map/ppermute | solution.py:734
  236.2 116.1 %all-to-all-start.1 = ((bf16[4,512,512]{2,1,0:T(8,128)(2,1)}), bf16[4,512,512]{2,1,0:T(8,128)(2,1)S(1)}, u32[]{:S(2)}, u32[]{:S(2)}) async-start(bf16[4,512,512]{2,1,0:T(8,128)(2,1)} %bitcast.204), calls=%async_computation.1 | async-start | bytes 4194304 | tf_op jit(solution)/shard_map/all_to_all | solution.py:979
  268.0 77.0 %collective-permute-start.18 = (bf16[2,512,512]{2,1,0:T(8,128)(2,1)}, bf16[2,512,512]{2,1,0:T(8,128)(2,1)}, u32[]{:S(2)}, u32[]{:S(2)}) collective-permute-start(bf16[2,512,512]{2,1,0:T(8,128)(2,1)} %pad_maximum_fusion.9), channel_id=1, source_target_pairs={{0,2},{2,0},{1,3},{3,1},{4,6},{6,4},{5,7},{7,5},{8,10},{10,8},{9,1... | collective-permute-start | bytes 3145736 | tf_op jit(solution)/shard_map/ppermute | solution.py:737
  269.5 79.1 %collective-permute-start.20 = (bf16[512,1024]{1,0:T(8,128)(2,1)}, bf16[512,1024]{1,0:T(8,128)(2,1)}, u32[]{:S(2)}, u32[]{:S(2)}) collective-permute-start(bf16[512,1024]{1,0:T(8,128)(2,1)} %slice.293), channel_id=1, source_target_pairs={{0,4},{4,0},{1,5},{5,1},{2,6},{6,2},{3,7},{7,3},{8,12},{12,8},{9,1... | collective-permute-start | bytes 3145736 | tf_op jit(solution)/shard_map/ppermute | solution.py:731
  270.7 71.4 %copy-start.24 = (bf16[2,8,128,128]{3,2,1,0:T(8,128)(2,1)S(1)}, bf16[2,8,128,128]{3,2,1,0:T(8,128)(2,1)}, u32[]{:S(2)}) copy-start(bf16[2,8,128,128]{3,2,1,0:T(8,128)(2,1)} %slice.456) | copy-start | bytes 1572868
  347.8 13.8 %collective-permute-start.19 = (bf16[512,512]{1,0:T(8,128)(2,1)}, bf16[512,512]{1,0:T(8,128)(2,1)}, u32[]{:S(2)}, u32[]{:S(2)}) collective-permute-start(bf16[512,512]{1,0:T(8,128)(2,1)} %get-tuple-element.72), channel_id=1, source_target_pairs={{0,4},{4,0},{1,5},{5,1},{2,6},{6,2},{3,7},{7,3},{8,12},{12,8},{9,1... | collective-permute-start | bytes 1572872 | tf_op jit(solution)/shard_map/ppermute | solution.py:731
  351.8 18.5 %collective-permute-start.21 = (bf16[512,512]{1,0:T(8,128)(2,1)}, bf16[512,512]{1,0:T(8,128)(2,1)}, u32[]{:S(2)}, u32[]{:S(2)}) collective-permute-start(bf16[512,512]{1,0:T(8,128)(2,1)} %slice.457), channel_id=1, source_target_pairs={{0,2},{2,0},{1,3},{3,1},{4,6},{6,4},{5,7},{7,5},{8,10},{10,8},{9,1... | collective-permute-start | bytes 1572872 | tf_op jit(solution)/shard_map/ppermute | solution.py:737
  353.6 71.3 %all-to-all-start.2 = ((bf16[4,128,2048]{2,1,0:T(8,128)(2,1)}), bf16[4,128,2048]{2,1,0:T(8,128)(2,1)S(1)}, u32[]{:S(2)}, u32[]{:S(2)}) async-start(bf16[4,128,2048]{2,1,0:T(8,128)(2,1)} %bitcast.195), calls=%async_computation.2 | async-start | bytes 4194304 | tf_op jit(solution)/shard_map/all_to_all | solution.py:980
  367.9 3.5 collective-permute-start.22
  369.3 24.4 %collective-permute-start.28 = (bf16[512,512]{1,0:T(8,128)(2,1)S(1)}, bf16[512,512]{1,0:T(8,128)(2,1)S(1)}, u32[]{:S(2)}, u32[]{:S(2)}) collective-permute-start(bf16[512,512]{1,0:T(8,128)(2,1)S(1)} %get-tuple-element.97), channel_id=1, source_target_pairs={{0,4},{4,0},{1,5},{5,1},{2,6},{6,2},{3,7},{7,3},{8,12},{12,8},{9,1... | collective-permute-start | bytes 1572872 | tf_op jit(solution)/shard_map/ppermute | solution.py:731
  371.6 6.3 %collective-permute-start.23 = (bf16[640,128]{1,0:T(8,128)(2,1)S(1)}, bf16[640,128]{1,0:T(8,128)(2,1)S(1)}, u32[]{:S(2)}, u32[]{:S(2)}) collective-permute-start(bf16[640,128]{1,0:T(8,128)(2,1)S(1)} %get-tuple-element.110), channel_id=1, source_target_pairs={{0,2},{2,0},{1,3},{3,1},{4,6},{6,4},{5,7},{7,5},{8,10},{10,8},{9,1... | collective-permute-start | bytes 491528 | tf_op jit(solution)/shard_map/ppermute | solution.py:737
  372.9 14.2 %collective-permute-start.25 = (bf16[640,128]{1,0:T(8,128)(2,1)S(1)}, bf16[640,128]{1,0:T(8,128)(2,1)S(1)}, u32[]{:S(2)}, u32[]{:S(2)}) collective-permute-start(bf16[640,128]{1,0:T(8,128)(2,1)S(1)} %get-tuple-element.111), channel_id=1, source_target_pairs={{0,4},{4,0},{1,5},{5,1},{2,6},{6,2},{3,7},{7,3},{8,12},{12,8},{9,1... | collective-permute-start | bytes 491528 | tf_op jit(solution)/shard_map/ppermute | solution.py:731
  387.2 5.7 %collective-permute-start.24 = (bf16[640,128]{1,0:T(8,128)(2,1)S(1)}, bf16[640,128]{1,0:T(8,128)(2,1)S(1)}, u32[]{:S(2)}, u32[]{:S(2)}) collective-permute-start(bf16[640,128]{1,0:T(8,128)(2,1)S(1)} %get-tuple-element.108), channel_id=1, source_target_pairs={{0,4},{4,0},{1,5},{5,1},{2,6},{6,2},{3,7},{7,3},{8,12},{12,8},{9,1... | collective-permute-start | bytes 491528 | tf_op jit(solution)/shard_map/ppermute | solution.py:731
  388.1 5.4 collective-permute-start.26
  393.6 1.7 collective-permute-start.27
  446.3 15.9 %collective-permute-start.30 = (bf16[1024,1024]{1,0:T(8,128)(2,1)}, bf16[1024,1024]{1,0:T(8,128)(2,1)S(1)}, u32[]{:S(2)}, u32[]{:S(2)}) collective-permute-start(bf16[1024,1024]{1,0:T(8,128)(2,1)} %get-tuple-element.65), channel_id=1, source_target_pairs={{0,1},{1,0},{2,3},{3,2},{4,5},{5,4},{6,7},{7,6},{8,9},{9,8},{10,11... | collective-permute-start | bytes 6291464 | tf_op jit(solution)/shard_map/ppermute | solution.py:734
  446.4 19.8 %collective-permute-start.29 = (bf16[1024,1024]{1,0:T(8,128)(2,1)}, bf16[1024,1024]{1,0:T(8,128)(2,1)}, u32[]{:S(2)}, u32[]{:S(2)}) collective-permute-start(bf16[1024,1024]{1,0:T(8,128)(2,1)} %get-tuple-element.63), channel_id=1, source_target_pairs={{0,1},{1,0},{2,3},{3,2},{4,5},{5,4},{6,7},{7,6},{8,9},{9,8},{10,11... | collective-permute-start | bytes 6291464 | tf_op jit(solution)/shard_map/ppermute | solution.py:734
  447.7 71.7 %all-to-all-start.3 = ((bf16[4,608,512]{2,1,0:T(8,128)(2,1)}), bf16[4,608,512]{2,1,0:T(8,128)(2,1)}, u32[]{:S(2)}, u32[]{:S(2)}) async-start(bf16[4,608,512]{2,1,0:T(8,128)(2,1)} %pad_maximum_fusion.refs_0_), calls=%async_computation.3 | async-start | bytes 4980736 | tf_op jit(solution)/shard_map/all_to_all | solution.py:720
  465.0 26.1 %collective-permute-start.33 = (bf16[512,1024]{1,0:T(8,128)(2,1)S(1)}, bf16[512,1024]{1,0:T(8,128)(2,1)S(1)}, u32[]{:S(2)}, u32[]{:S(2)}) collective-permute-start(bf16[512,1024]{1,0:T(8,128)(2,1)S(1)} %slice.310), channel_id=1, source_target_pairs={{0,4},{4,0},{1,5},{5,1},{2,6},{6,2},{3,7},{7,3},{8,12},{12,8},{9,1... | collective-permute-start | bytes 3145736 | tf_op jit(solution)/shard_map/ppermute | solution.py:731
  469.2 26.1 %collective-permute-start.31 = (bf16[2,512,512]{2,1,0:T(8,128)(2,1)S(1)}, bf16[2,512,512]{2,1,0:T(8,128)(2,1)S(1)}, u32[]{:S(2)}, u32[]{:S(2)}) collective-permute-start(bf16[2,512,512]{2,1,0:T(8,128)(2,1)S(1)} %pad_maximum_fusion.11), channel_id=1, source_target_pairs={{0,2},{2,0},{1,3},{3,1},{4,6},{6,4},{5,7},{7,5},{8,10},{10,8},{9,1... | collective-permute-start | bytes 3145736 | tf_op jit(solution)/shard_map/ppermute | solution.py:737
  471.9 30.4 %collective-permute-start.37 = (bf16[128,2048]{1,0:T(8,128)(2,1)S(1)}, bf16[128,2048]{1,0:T(8,128)(2,1)S(1)}, u32[]{:S(2)}, u32[]{:S(2)}) collective-permute-start(bf16[128,2048]{1,0:T(8,128)(2,1)S(1)} %add_convert_fusion.1), channel_id=1, source_target_pairs={{0,4},{4,0},{1,5},{5,1},{2,6},{6,2},{3,7},{7,3},{8,12},{12,8},{9,1... | collective-permute-start | bytes 1572872 | tf_op jit(solution)/shard_map/ppermute | solution.py:731
  491.5 13.9 %collective-permute-start.34 = (bf16[512,512]{1,0:T(8,128)(2,1)S(1)}, bf16[512,512]{1,0:T(8,128)(2,1)S(1)}, u32[]{:S(2)}, u32[]{:S(2)}) collective-permute-start(bf16[512,512]{1,0:T(8,128)(2,1)S(1)} %slice.455), channel_id=1, source_target_pairs={{0,2},{2,0},{1,3},{3,1},{4,6},{6,4},{5,7},{7,5},{8,10},{10,8},{9,1... | collective-permute-start | bytes 1572872 | tf_op jit(solution)/shard_map/ppermute | solution.py:737
  495.5 17.0 %collective-permute-start.32 = (bf16[512,512]{1,0:T(8,128)(2,1)S(1)}, bf16[512,512]{1,0:T(8,128)(2,1)S(1)}, u32[]{:S(2)}, u32[]{:S(2)}) collective-permute-start(bf16[512,512]{1,0:T(8,128)(2,1)S(1)} %fusion.9), channel_id=1, source_target_pairs={{0,4},{4,0},{1,5},{5,1},{2,6},{6,2},{3,7},{7,3},{8,12},{12,8},{9,1... | collective-permute-start | bytes 1572872 | tf_op jit(solution)/shard_map/ppermute | solution.py:731
  515.5 2.3 collective-permute-start.35
  517.9 8.8 %collective-permute-start.36 = (f32[2,512]{1,0:T(2,128)S(1)}, f32[2,512]{1,0:T(2,128)S(1)}, u32[]{:S(2)}, u32[]{:S(2)}) collective-permute-start(f32[2,512]{1,0:T(2,128)S(1)} %add.408), channel_id=1, source_target_pairs={{0,2},{2,0},{1,3},{3,1},{4,6},{6,4},{5,7},{7,5},{8,10},{10,8},{9,1... | collective-permute-start | bytes 12296 | tf_op jit(solution)/shard_map/ppermute | solution.py:737
  522.9 3.7 collective-permute-start.38
  525.5 15.9 %collective-permute-start.41 = (bf16[608,512]{1,0:T(8,128)(2,1)S(1)}, bf16[608,512]{1,0:T(8,128)(2,1)S(1)}, u32[]{:S(2)}, u32[]{:S(2)}) collective-permute-start(bf16[608,512]{1,0:T(8,128)(2,1)S(1)} %get-tuple-element.68), channel_id=1, source_target_pairs={{0,4},{4,0},{1,5},{5,1},{2,6},{6,2},{3,7},{7,3},{8,12},{12,8},{9,1... | collective-permute-start | bytes 1867784 | tf_op jit(solution)/shard_map/ppermute | solution.py:731
  526.7 1.2 collective-permute-start.39
  527.8 4.0 collective-permute-start.40
  (56 other events, 327.2 us)

commit v6 on v5

--- a/solution.py
+++ b/solution.py
@@ -185,7 +185,7 @@
             out_specs=[pl.BlockSpec((size, width), lambda j, i, blocks: (i, j))] * n,
         ),
         out_shape=[jax.ShapeDtypeStruct((count, width * blocks.shape[0]), bf16)] * n,
-        cost_estimate=cost(5),
+        cost_estimate=cost(0),
         compiler_params=PARAMS,
     )(blocks, *[lefts] * n, *[more_lefts] * n, right, more_right)
 

time: 563 us -> 563 us (level)
  no operation moved by 1% of the time
where the time goes in v6:
time: 563 us; the launch traced here: 555 us
  Pallas kernels  204 us (36%)
  waiting for transfers between devices  121 us (21%)
  starting transfers between devices  60.7 us (11%)
  local copies, waits for them, and re-layouts  55.7 us (10%)
  other arithmetic  51.3 us (9%)
  matrix products  46.5 us (8%)
  between operations  16.3 us (3%)
    pallas_call x1, Pallas kernels, scan_backward(): pl.pallas_call(functools.partial(backward_kernel, S, G), grid=(T // LANE,...  69.6 us
    ppermute x14, waiting for transfers between devices, across(): return lax.ppermute(array, 'context', [(0, 1), (1, 0)])  66.8 us
    pallas_call x1, Pallas kernels, scan_forward(): pl.pallas_call(functools.partial(forward_kernel, S, G), grid=(T // LANE,)...  33.7 us
    dot_general x6, matrix products, t_dot(): lax.dot_general(a, b, (((0,), (0,)), ((), ())), preferred_element_type=f32)  29.7 us
    ppermute x3, waiting for transfers between devices, line_gather(): lax.ppermute(left, axis, [(i, i - 1) for i in range(1, count - step + 1)])  25.6 us
    pallas_call x2, Pallas kernels, products(): pl.pallas_call(kernel, grid_spec=pltpu.PrefetchScalarGridSpec(num_scalar_...  18.9 us
    pallas_call x1, Pallas kernels, gates(): pl.pallas_call(kernel, grid_spec=pltpu.PrefetchScalarGridSpec(num_scalar_...  18.4 us
    dot_general x4, matrix products, dot(): return jnp.dot(a, b, preferred_element_type=f32).astype(out)  16.8 us
  transfers between devices with their start and end apart: 46, of which 22 were waited for; matrix products, arithmetic and copies ran while one was open for 21% of the time, Pallas kernels for 30%

profile of v6, /device:TPU:0, one launch (start us, length us, event | category | flops | bytes accessed | tf_op | source)
XLA Modules:
  0.0 555.0 jit_solution(6445196350861300841)
XLA Ops:
  0.7 3.2 constant_dynamic-slice_fusion.21.refs_0_
  3.9 2.9 collective-permute-start
  10.0 6.8 %fusion.58 = (bf16[512,1,1024]{2,1,0:T(2,128)(2,1)}, bf16[512,1,1024]{2,1,0:T(2,128)(2,1)}) fusion(bf16[512,2,1024]{2,1,0:T(2,128)(2,1)} %param.17), kind=kLoop, calls=%fused_computation.223 | loop fusion | bytes 4194304 | tf_op jit(solution)/shard_map/slice | solution.py:942
  20.4 3.5 collective-permute-start.2
  25.7 11.5 %collective-permute-done.2.refs_2_.refs_0_ = bf16[624,512]{1,0:T(8,128)(2,1)S(1)} collective-permute-done((bf16[624,512]{1,0:T(8,128)(2,1)S(1)}, bf16[624,512]{1,0:T(8,128)(2,1)S(1)}, u32[]{:S(2)}, u32[]{:S(2)}) %collective-permute-start.2) | collective-permute-done | bytes 639008 | tf_op jit(solution)/shard_map/ppermute | solution.py:708
  38.7 2.7 collective-permute-done.5.refs_4_
  51.0 8.3 %collective-permute-done.6.refs_5_ = bf16[624,512]{1,0:T(8,128)(2,1)} collective-permute-done((bf16[624,512]{1,0:T(8,128)(2,1)}, bf16[624,512]{1,0:T(8,128)(2,1)}, u32[]{:S(2)}, u32[]{:S(2)}) %collective-permute-start.6) | collective-permute-done | bytes 639008 | tf_op jit(solution)/shard_map/ppermute | solution.py:709
  60.9 14.6 %collective-permute-done.7.refs_6_ = bf16[624,512]{1,0:T(8,128)(2,1)S(1)} collective-permute-done((bf16[624,512]{1,0:T(8,128)(2,1)}, bf16[624,512]{1,0:T(8,128)(2,1)S(1)}, u32[]{:S(2)}, u32[]{:S(2)}) %collective-permute-start.7) | collective-permute-done | bytes 639008 | tf_op jit(solution)/shard_map/ppermute | solution.py:709
  76.3 4.2 shard_map.221
  84.1 5.5 all-to-all-start
  94.8 3.2 constant_dynamic-slice_fusion.9
  98.5 11.0 %shard_map.222 = (bf16[2,1024,2048]{2,1,0:T(8,128)(2,1)}, f32[1024,128]{1,0:T(8,128)}) custom-call(s32[1]{0:T(128)} %bitcast.1.place_ref, bf16[1024,2048]{1,0:T(8,128)(2,1)} %bitcast.189, bf16[512,2048]{1,0:T(8,128)(2,1)} %copy-done.17, bf16[512,2048]{1,0:T(8,128)(2,1)} %collective-permute-done.1.refs_2_, f32[1,2048]{1,0:T(1,128)} %bitcast.230), custom_call_target="tpu_custom_call" | custom-call | flops 920000000 | bytes 2880000 | tf_op jit(solution)/shard_map/pallas_call | solution.py:121
  109.5 13.3 %shard_map.227 = (bf16[2,1024,512]{2,1,0:T(8,128)(2,1)}, bf16[2,1024,512]{2,1,0:T(8,128)(2,1)}, f32[2,8,160,128]{3,2,1,0:T(8,128)}) custom-call(s32[1]{0:T(128)} %bitcast.place_ref, bf16[2,1024,2048]{2,1,0:T(8,128)(2,1)} %get-tuple-element.40.in_ref.a_ref, bf16[2048,512]{1,0:T(8,128)(2,1)} %bitcast.180, f32[8,512]{1,0:T(8,128)} %maximum_maximum_fusion.vec_ref, ...), custom_call_target="tpu_custom_call" | custom-call | flops 1035000000 | bytes 3240000 | tf_op jit(solution)/shard_map/pallas_call | solution.py:290
  130.0 3.2 collective-permute-done.11
  133.2 14.1 %collective-permute-done.13 = bf16[640,128]{1,0:T(8,128)(2,1)S(1)} collective-permute-done((bf16[640,128]{1,0:T(8,128)(2,1)S(1)}, bf16[640,128]{1,0:T(8,128)(2,1)S(1)}, u32[]{:S(2)}, u32[]{:S(2)}) %collective-permute-start.13) | collective-permute-done | bytes 163872 | tf_op jit(solution)/shard_map/ppermute | solution.py:731
  157.3 33.7 %shard_map.228 = (f32[2,1024,512]{2,1,0:T(8,128)}, f32[2,1024,512]{2,1,0:T(8,128)}, f32[8,128,128]{2,1,0:T(8,128)}) custom-call(f32[2,8,160,128]{3,2,1,0:T(8,128)} %bitcast.202, bf16[2,1024,512]{2,1,0:T(8,128)(2,1)} %get-tuple-element.44.u_ref, f32[2,1024,128]{2,1,0:T(8,128)} %and_convert_fusion.refs_7_.masks_ref, bf16[128,512]{1,0:T(8,128)(2,1)} %bitcast.240, ...), custom_call_target="tpu_custom_call" | custom-call | flops 3449999872 | bytes 10800000 | tf_op jit(solution)/shard_map/pallas_call | solution.py:639
  191.0 7.1 %shard_map.224.refs_1_ = bf16[1024,2048]{1,0:T(8,128)(2,1)} custom-call(s32[1]{0:T(128)} %bitcast.1.place_ref, bf16[512,2048]{1,0:T(8,128)(2,1)} %collective-permute-done.8.first_ref, bf16[512,2048]{1,0:T(8,128)(2,1)} %collective-permute-done.9.second_ref), custom_call_target="tpu_custom_call" | custom-call | flops 460000000 | bytes 1440000 | tf_op jit(solution)/shard_map/pallas_call | solution.py:71
  201.5 3.0 slice.272
  204.6 18.4 %shard_map.229 = (bf16[2,1024,512]{2,1,0:T(8,128)(2,1)}, bf16[2,1024,512]{2,1,0:T(8,128)(2,1)}, f32[2,1024,512]{2,1,0:T(8,128)}) custom-call(s32[1]{0:T(128)} %bitcast.place_ref, bf16[2,1024,2048]{2,1,0:T(8,128)(2,1)} %get-tuple-element.40.in_ref.a_ref, bf16[1024,2048]{1,0:T(8,128)(2,1)} %bitcast.177, bf16[1024,2048]{1,0:T(8,128)(2,1)} %shard_map.224.refs_1_, ...), custom_call_target="tpu_custom_call" | custom-call | flops 1610000000 | bytes 5040000 | tf_op jit(solution)/shard_map/pallas_call | solution.py:333
  223.2 4.0 convolution_convert_fusion
  227.2 2.6 convolution_convert_fusion.1
  230.3 5.9 %bitcast_convert_fusion.1 = bf16[2048,512]{1,0:T(8,128)(2,1)} fusion(bf16[2,1024,2048]{2,1,0:T(8,128)(2,1)S(1)} %bitcast.184, bf16[2,1024,512]{2,1,0:T(8,128)(2,1)S(1)} %copy-done.4), kind=kOutput, calls=%fused_computation.2 | convolution fusion | flops 4296015872 | bytes 12582912 | tf_op jit(solution)/shard_map/dot_general | solution.py:855
  236.2 5.1 all-to-all-start.1
  241.3 5.0 fusion.14
  246.3 3.7 add_convert_fusion
  250.0 5.4 fusion.63
  255.4 4.9 convert_add_fusion.3.refs_0_
  270.7 69.6 %shard_map.231 = (bf16[2,1024,512]{2,1,0:T(8,128)(2,1)}, f32[2,1024,512]{2,1,0:T(8,128)}, f32[2,8,160,128]{3,2,1,0:T(8,128)}, f32[16,512]{1,0:T(8,128)}, f32[8,512]{1,0:T(8,128)}) custom-call(f32[2,8,160,128]{3,2,1,0:T(8,128)} %bitcast.203, bf16[2,1024,512]{2,1,0:T(8,128)(2,1)} %get-tuple-element.44.u_ref, f32[2,1024,512]{2,1,0:T(8,128)} %get-tuple-element.49.step_ref, ...), custom_call_target="tpu_custom_call" | custom-call | flops 9774999552 | bytes 30600000 | tf_op jit(solution)/shard_map/pallas_call | solution.py:664
  342.2 2.9 convolution_convert_fusion.2
  345.0 2.8 fusion.56
  353.6 5.3 all-to-all-start.2
  361.6 3.2 convert_add_fusion.5
  373.9 3.9 collective-permute-done.23
  377.8 9.3 %collective-permute-done.25 = bf16[640,128]{1,0:T(8,128)(2,1)S(1)} collective-permute-done((bf16[640,128]{1,0:T(8,128)(2,1)S(1)}, bf16[640,128]{1,0:T(8,128)(2,1)S(1)}, u32[]{:S(2)}, u32[]{:S(2)}) %collective-permute-start.25) | collective-permute-done | bytes 163872 | tf_op jit(solution)/shard_map/ppermute | solution.py:731
  398.4 15.9 %shard_map.234 = (bf16[2,1024,512]{2,1,0:T(8,128)(2,1)}, f32[8,512]{1,0:T(8,128)}, bf16[2,1024,256]{2,1,0:T(8,128)(2,1)}) custom-call(s32[1]{0:T(128)} %bitcast.place_ref, f32[2,8,160,128]{3,2,1,0:T(8,128)} %bitcast.198, f32[2,1024,512]{2,1,0:T(8,128)} %get-tuple-element.54.d_ref, bf16[2,1024,512]{2,1,0:T(8,128)(2,1)} %get-tuple-element.55.x_ref.edge_ref, ...), custom_call_target="tpu_custom_call" | custom-call | flops 18400000000 | bytes 57600000 | tf_op jit(solution)/shard_map/pallas_call | solution.py:401
  415.1 9.9 %bitcast_convert_fusion = bf16[2048,512]{1,0:T(8,128)(2,1)} fusion(bf16[2,1024,2048]{2,1,0:T(8,128)(2,1)} %get-tuple-element.40.in_ref.a_ref, bf16[2,1024,512]{2,1,0:T(8,128)(2,1)} %get-tuple-element.56.refs_0_.refs_1_), kind=kOutput, calls=%fused_computation.1 | convolution fusion | flops 4296015872 | bytes 12582912 | tf_op jit(solution)/shard_map/dot_general | solution.py:855
  436.7 9.6 %shard_map.238 = (bf16[1024,1024]{1,0:T(8,128)(2,1)}, bf16[1024,1024]{1,0:T(8,128)(2,1)}) custom-call(s32[2]{0:T(128)} %get-tuple-element.132.blocks_ref, bf16[2,1024,512]{2,1,0:T(8,128)(2,1)} %get-tuple-element.56.refs_0_.refs_1_, bf16[2,1024,512]{2,1,0:T(8,128)(2,1)} %get-tuple-element.56.refs_0_.refs_1_, ...), custom_call_target="tpu_custom_call" | custom-call | tf_op jit(solution)/shard_map/pallas_call | solution.py:179
  447.7 5.1 all-to-all-start.3
  452.8 9.4 %shard_map.237 = (bf16[1024,1024]{1,0:T(8,128)(2,1)}, bf16[1024,1024]{1,0:T(8,128)(2,1)}) custom-call(s32[2]{0:T(128)} %get-tuple-element.131.blocks_ref, bf16[2,1024,512]{2,1,0:T(8,128)(2,1)} %get-tuple-element.56.refs_0_.refs_1_, bf16[2,1024,512]{2,1,0:T(8,128)(2,1)} %get-tuple-element.56.refs_0_.refs_1_, ...), custom_call_target="tpu_custom_call" | custom-call | tf_op jit(solution)/shard_map/pallas_call | solution.py:179
  462.2 2.7 convert_add_fusion
  472.9 18.2 %collective-permute-done.33 = bf16[512,1024]{1,0:T(8,128)(2,1)S(1)} collective-permute-done((bf16[512,1024]{1,0:T(8,128)(2,1)S(1)}, bf16[512,1024]{1,0:T(8,128)(2,1)S(1)}, u32[]{:S(2)}, u32[]{:S(2)}) %collective-permute-start.33) | collective-permute-done | bytes 1048608 | tf_op jit(solution)/shard_map/ppermute | solution.py:731
  496.7 5.6 %collective-permute-done.37 = bf16[128,2048]{1,0:T(8,128)(2,1)S(1)} collective-permute-done((bf16[128,2048]{1,0:T(8,128)(2,1)S(1)}, bf16[128,2048]{1,0:T(8,128)(2,1)S(1)}, u32[]{:S(2)}, u32[]{:S(2)}) %collective-permute-start.37) | collective-permute-done | bytes 524320 | tf_op jit(solution)/shard_map/ppermute | solution.py:731
  502.4 3.0 collective-permute-done.34
  505.6 6.8 %collective-permute-done.32 = bf16[512,512]{1,0:T(8,128)(2,1)S(1)} collective-permute-done((bf16[512,512]{1,0:T(8,128)(2,1)S(1)}, bf16[512,512]{1,0:T(8,128)(2,1)S(1)}, u32[]{:S(2)}, u32[]{:S(2)}) %collective-permute-start.32) | collective-permute-done | bytes 524320 | tf_op jit(solution)/shard_map/ppermute | solution.py:731
  512.9 2.6 fusion.2
  528.4 3.5 fusion.5
  532.5 8.9 %collective-permute-done.41 = bf16[608,512]{1,0:T(8,128)(2,1)S(1)} collective-permute-done((bf16[608,512]{1,0:T(8,128)(2,1)S(1)}, bf16[608,512]{1,0:T(8,128)(2,1)S(1)}, u32[]{:S(2)}, u32[]{:S(2)}) %collective-permute-start.41) | collective-permute-done | bytes 622624 | tf_op jit(solution)/shard_map/ppermute | solution.py:731
  548.1 6.5 %shard_map.240 = f32[512,2,1024]{2,1,0:T(2,128)} custom-call(bf16[2,608,512]{2,1,0:T(8,128)(2,1)} %pad_maximum_fusion.4.a_ref, bf16[2,512,512]{2,1,0:T(8,128)(2,1)} %pad_maximum_fusion.10.refs_1_.b_ref), custom_call_target="tpu_custom_call" | custom-call | flops 575000000 | bytes 1800000 | tf_op jit(solution)/shard_map/pallas_call | solution.py:205
  (359 shorter events, 127.6 us)
Async XLA Ops:
  3.9 56.9 %collective-permute-start = (bf16[512,2048]{1,0:T(8,128)(2,1)}, bf16[512,2048]{1,0:T(8,128)(2,1)S(1)}, u32[]{:S(2)}, u32[]{:S(2)}) collective-permute-start(bf16[512,2048]{1,0:T(8,128)(2,1)} %constant_dynamic-slice_fusion.21.refs_0_), channel_id=1, source_target_pairs={{0,4},{4,0},{1,5},{5,1},{2,6},{6,2},{3,7},{7,3},{8,12},{12,8},{9,1... | collective-permute-start | bytes 6291464 | tf_op jit(solution)/shard_map/ppermute | solution.py:731
  20.4 29.7 %copy-start.21 = (bf16[624,512]{1,0:T(8,128)(2,1)}, bf16[624,512]{1,0:T(8,128)(2,1)S(1)}, u32[]{:S(2)}) copy-start(bf16[624,512]{1,0:T(8,128)(2,1)S(1)} %fusion.24.refs_3_) | copy-start | bytes 1916932
  20.4 16.8 %collective-permute-start.2 = (bf16[624,512]{1,0:T(8,128)(2,1)S(1)}, bf16[624,512]{1,0:T(8,128)(2,1)S(1)}, u32[]{:S(2)}, u32[]{:S(2)}) collective-permute-start(bf16[624,512]{1,0:T(8,128)(2,1)S(1)} %fusion.24.refs_3_), channel_id=1, source_target_pairs={{0,8},{8,16},{16,24},{1,9},{9,17},{17,25},{2,10},{10,18},{18,26},{... | collective-permute-start | bytes 1916936 | tf_op jit(solution)/shard_map/ppermute | solution.py:708
  23.9 17.6 %collective-permute-start.5 = (bf16[624,512]{1,0:T(8,128)(2,1)S(1)}, bf16[624,512]{1,0:T(8,128)(2,1)}, u32[]{:S(2)}, u32[]{:S(2)}) collective-permute-start(bf16[624,512]{1,0:T(8,128)(2,1)S(1)} %fusion.24.refs_3_), channel_id=1, source_target_pairs={{8,0},{16,8},{24,16},{9,1},{17,9},{25,17},{10,2},{18,10},{26,18},{... | collective-permute-start | bytes 1916936 | tf_op jit(solution)/shard_map/ppermute | solution.py:709
  37.2 13.1 %collective-permute-start.3 = (bf16[624,512]{1,0:T(8,128)(2,1)S(1)}, bf16[624,512]{1,0:T(8,128)(2,1)}, u32[]{:S(2)}, u32[]{:S(2)}) collective-permute-start(bf16[624,512]{1,0:T(8,128)(2,1)S(1)} %collective-permute-done.2.refs_2_.refs_0_), channel_id=1, source_target_pairs={{8,16},{16,24},{9,17},{17,25},{10,18},{18,26},{11,19},{19,27},{12,... | collective-permute-start | bytes 1916936 | tf_op jit(solution)/shard_map/ppermute | solution.py:708
  41.5 17.8 %collective-permute-start.6 = (bf16[624,512]{1,0:T(8,128)(2,1)}, bf16[624,512]{1,0:T(8,128)(2,1)}, u32[]{:S(2)}, u32[]{:S(2)}) collective-permute-start(bf16[624,512]{1,0:T(8,128)(2,1)} %collective-permute-done.5.refs_4_), channel_id=1, source_target_pairs={{8,0},{16,8},{9,1},{17,9},{10,2},{18,10},{11,3},{19,11},{12,4},{20... | collective-permute-start | bytes 1916936 | tf_op jit(solution)/shard_map/ppermute | solution.py:709
  50.3 10.6 %collective-permute-start.4 = (bf16[624,512]{1,0:T(8,128)(2,1)}, bf16[624,512]{1,0:T(8,128)(2,1)S(1)}, u32[]{:S(2)}, u32[]{:S(2)}) collective-permute-start(bf16[624,512]{1,0:T(8,128)(2,1)} %collective-permute-done.3.refs_1_), channel_id=1, source_target_pairs={{16,24},{17,25},{18,26},{19,27},{20,28},{21,29},{22,30},{23,31}} | collective-permute-start | bytes 1916936 | tf_op jit(solution)/shard_map/ppermute | solution.py:708
  59.3 16.2 %collective-permute-start.7 = (bf16[624,512]{1,0:T(8,128)(2,1)}, bf16[624,512]{1,0:T(8,128)(2,1)S(1)}, u32[]{:S(2)}, u32[]{:S(2)}) collective-permute-start(bf16[624,512]{1,0:T(8,128)(2,1)} %collective-permute-done.6.refs_5_), channel_id=1, source_target_pairs={{8,0},{9,1},{10,2},{11,3},{12,4},{13,5},{14,6},{15,7}} | collective-permute-start | bytes 1916936 | tf_op jit(solution)/shard_map/ppermute | solution.py:709
  60.8 37.7 %collective-permute-start.1 = (bf16[512,2048]{1,0:T(8,128)(2,1)S(1)}, bf16[512,2048]{1,0:T(8,128)(2,1)}, u32[]{:S(2)}, u32[]{:S(2)}) collective-permute-start(bf16[512,2048]{1,0:T(8,128)(2,1)S(1)} %collective-permute-done.refs_1_.refs_0_), channel_id=1, source_target_pairs={{0,1},{1,0},{2,3},{3,2},{4,5},{5,4},{6,7},{7,6},{8,9},{9,8},{10,11... | collective-permute-start | bytes 6291464 | tf_op jit(solution)/shard_map/ppermute | solution.py:734
  84.1 114.1 %all-to-all-start = ((bf16[4,1024,512]{2,1,0:T(8,128)(2,1)}), bf16[4,1024,512]{2,1,0:T(8,128)(2,1)}, u32[]{:S(2)}, u32[]{:S(2)}) async-start(bf16[4,1024,512]{2,1,0:T(8,128)(2,1)} %broadcast_in_dim.45), calls=%async_computation | async-start | bytes 8388608 | tf_op jit(solution)/shard_map/all_to_all | solution.py:716
  98.0 52.3 %collective-permute-start.8 = (bf16[512,2048]{1,0:T(8,128)(2,1)}, bf16[512,2048]{1,0:T(8,128)(2,1)}, u32[]{:S(2)}, u32[]{:S(2)}) collective-permute-start(bf16[512,2048]{1,0:T(8,128)(2,1)} %constant_dynamic-slice_fusion.9), channel_id=1, source_target_pairs={{0,4},{4,0},{1,5},{5,1},{2,6},{6,2},{3,7},{7,3},{8,12},{12,8},{9,1... | collective-permute-start | bytes 6291464 | tf_op jit(solution)/shard_map/ppermute | solution.py:731
  124.0 1.7 collective-permute-start.10
  126.9 6.3 %collective-permute-start.11 = (bf16[640,128]{1,0:T(8,128)(2,1)S(1)}, bf16[640,128]{1,0:T(8,128)(2,1)S(1)}, u32[]{:S(2)}, u32[]{:S(2)}) collective-permute-start(bf16[640,128]{1,0:T(8,128)(2,1)S(1)} %get-tuple-element.116), channel_id=1, source_target_pairs={{0,2},{2,0},{1,3},{3,1},{4,6},{6,4},{5,7},{7,5},{8,10},{10,8},{9,1... | collective-permute-start | bytes 491528 | tf_op jit(solution)/shard_map/ppermute | solution.py:737
  128.5 18.8 %collective-permute-start.13 = (bf16[640,128]{1,0:T(8,128)(2,1)S(1)}, bf16[640,128]{1,0:T(8,128)(2,1)S(1)}, u32[]{:S(2)}, u32[]{:S(2)}) collective-permute-start(bf16[640,128]{1,0:T(8,128)(2,1)S(1)} %get-tuple-element.117), channel_id=1, source_target_pairs={{0,4},{4,0},{1,5},{5,1},{2,6},{6,2},{3,7},{7,3},{8,12},{12,8},{9,1... | collective-permute-start | bytes 491528 | tf_op jit(solution)/shard_map/ppermute | solution.py:731
  147.3 5.4 collective-permute-start.12
  147.9 5.3 collective-permute-start.14
  150.3 40.7 %collective-permute-start.9 = (bf16[512,2048]{1,0:T(8,128)(2,1)}, bf16[512,2048]{1,0:T(8,128)(2,1)}, u32[]{:S(2)}, u32[]{:S(2)}) collective-permute-start(bf16[512,2048]{1,0:T(8,128)(2,1)} %collective-permute-done.8.first_ref), channel_id=1, source_target_pairs={{0,1},{1,0},{2,3},{3,2},{4,5},{5,4},{6,7},{7,6},{8,9},{9,8},{10,11... | collective-permute-start | bytes 6291464 | tf_op jit(solution)/shard_map/ppermute | solution.py:734
  153.4 2.5 collective-permute-start.15
  229.8 20.3 %collective-permute-start.17 = (bf16[1024,1024]{1,0:T(8,128)(2,1)}, bf16[1024,1024]{1,0:T(8,128)(2,1)}, u32[]{:S(2)}, u32[]{:S(2)}) collective-permute-start(bf16[1024,1024]{1,0:T(8,128)(2,1)} %convolution_convert_fusion), channel_id=1, source_target_pairs={{0,1},{1,0},{2,3},{3,2},{4,5},{5,4},{6,7},{7,6},{8,9},{9,8},{10,11... | collective-permute-start | bytes 6291464 | tf_op jit(solution)/shard_map/ppermute | solution.py:734
  230.3 25.2 %collective-permute-start.16 = (bf16[1024,1024]{1,0:T(8,128)(2,1)}, bf16[1024,1024]{1,0:T(8,128)(2,1)}, u32[]{:S(2)}, u32[]{:S(2)}) collective-permute-start(bf16[1024,1024]{1,0:T(8,128)(2,1)} %convolution_convert_fusion.1), channel_id=1, source_target_pairs={{0,1},{1,0},{2,3},{3,2},{4,5},{5,4},{6,7},{7,6},{8,9},{9,8},{10,11... | collective-permute-start | bytes 6291464 | tf_op jit(solution)/shard_map/ppermute | solution.py:734
  236.2 116.1 %all-to-all-start.1 = ((bf16[4,512,512]{2,1,0:T(8,128)(2,1)}), bf16[4,512,512]{2,1,0:T(8,128)(2,1)S(1)}, u32[]{:S(2)}, u32[]{:S(2)}) async-start(bf16[4,512,512]{2,1,0:T(8,128)(2,1)} %bitcast.204), calls=%async_computation.1 | async-start | bytes 4194304 | tf_op jit(solution)/shard_map/all_to_all | solution.py:979
  268.0 77.0 %collective-permute-start.18 = (bf16[2,512,512]{2,1,0:T(8,128)(2,1)}, bf16[2,512,512]{2,1,0:T(8,128)(2,1)}, u32[]{:S(2)}, u32[]{:S(2)}) collective-permute-start(bf16[2,512,512]{2,1,0:T(8,128)(2,1)} %pad_maximum_fusion.9), channel_id=1, source_target_pairs={{0,2},{2,0},{1,3},{3,1},{4,6},{6,4},{5,7},{7,5},{8,10},{10,8},{9,1... | collective-permute-start | bytes 3145736 | tf_op jit(solution)/shard_map/ppermute | solution.py:737
  269.5 79.1 %collective-permute-start.20 = (bf16[512,1024]{1,0:T(8,128)(2,1)}, bf16[512,1024]{1,0:T(8,128)(2,1)}, u32[]{:S(2)}, u32[]{:S(2)}) collective-permute-start(bf16[512,1024]{1,0:T(8,128)(2,1)} %slice.293), channel_id=1, source_target_pairs={{0,4},{4,0},{1,5},{5,1},{2,6},{6,2},{3,7},{7,3},{8,12},{12,8},{9,1... | collective-permute-start | bytes 3145736 | tf_op jit(solution)/shard_map/ppermute | solution.py:731
  270.7 71.4 %copy-start.24 = (bf16[2,8,128,128]{3,2,1,0:T(8,128)(2,1)S(1)}, bf16[2,8,128,128]{3,2,1,0:T(8,128)(2,1)}, u32[]{:S(2)}) copy-start(bf16[2,8,128,128]{3,2,1,0:T(8,128)(2,1)} %slice.456) | copy-start | bytes 1572868
  347.8 13.8 %collective-permute-start.19 = (bf16[512,512]{1,0:T(8,128)(2,1)}, bf16[512,512]{1,0:T(8,128)(2,1)}, u32[]{:S(2)}, u32[]{:S(2)}) collective-permute-start(bf16[512,512]{1,0:T(8,128)(2,1)} %get-tuple-element.72), channel_id=1, source_target_pairs={{0,4},{4,0},{1,5},{5,1},{2,6},{6,2},{3,7},{7,3},{8,12},{12,8},{9,1... | collective-permute-start | bytes 1572872 | tf_op jit(solution)/shard_map/ppermute | solution.py:731
  351.8 18.5 %collective-permute-start.21 = (bf16[512,512]{1,0:T(8,128)(2,1)}, bf16[512,512]{1,0:T(8,128)(2,1)}, u32[]{:S(2)}, u32[]{:S(2)}) collective-permute-start(bf16[512,512]{1,0:T(8,128)(2,1)} %slice.457), channel_id=1, source_target_pairs={{0,2},{2,0},{1,3},{3,1},{4,6},{6,4},{5,7},{7,5},{8,10},{10,8},{9,1... | collective-permute-start | bytes 1572872 | tf_op jit(solution)/shard_map/ppermute | solution.py:737
  353.6 71.3 %all-to-all-start.2 = ((bf16[4,128,2048]{2,1,0:T(8,128)(2,1)}), bf16[4,128,2048]{2,1,0:T(8,128)(2,1)S(1)}, u32[]{:S(2)}, u32[]{:S(2)}) async-start(bf16[4,128,2048]{2,1,0:T(8,128)(2,1)} %bitcast.195), calls=%async_computation.2 | async-start | bytes 4194304 | tf_op jit(solution)/shard_map/all_to_all | solution.py:980
  367.9 3.5 collective-permute-start.22
  369.3 24.4 %collective-permute-start.28 = (bf16[512,512]{1,0:T(8,128)(2,1)S(1)}, bf16[512,512]{1,0:T(8,128)(2,1)S(1)}, u32[]{:S(2)}, u32[]{:S(2)}) collective-permute-start(bf16[512,512]{1,0:T(8,128)(2,1)S(1)} %get-tuple-element.97), channel_id=1, source_target_pairs={{0,4},{4,0},{1,5},{5,1},{2,6},{6,2},{3,7},{7,3},{8,12},{12,8},{9,1... | collective-permute-start | bytes 1572872 | tf_op jit(solution)/shard_map/ppermute | solution.py:731
  371.6 6.3 %collective-permute-start.23 = (bf16[640,128]{1,0:T(8,128)(2,1)S(1)}, bf16[640,128]{1,0:T(8,128)(2,1)S(1)}, u32[]{:S(2)}, u32[]{:S(2)}) collective-permute-start(bf16[640,128]{1,0:T(8,128)(2,1)S(1)} %get-tuple-element.110), channel_id=1, source_target_pairs={{0,2},{2,0},{1,3},{3,1},{4,6},{6,4},{5,7},{7,5},{8,10},{10,8},{9,1... | collective-permute-start | bytes 491528 | tf_op jit(solution)/shard_map/ppermute | solution.py:737
  372.9 14.2 %collective-permute-start.25 = (bf16[640,128]{1,0:T(8,128)(2,1)S(1)}, bf16[640,128]{1,0:T(8,128)(2,1)S(1)}, u32[]{:S(2)}, u32[]{:S(2)}) collective-permute-start(bf16[640,128]{1,0:T(8,128)(2,1)S(1)} %get-tuple-element.111), channel_id=1, source_target_pairs={{0,4},{4,0},{1,5},{5,1},{2,6},{6,2},{3,7},{7,3},{8,12},{12,8},{9,1... | collective-permute-start | bytes 491528 | tf_op jit(solution)/shard_map/ppermute | solution.py:731
  387.2 5.7 %collective-permute-start.24 = (bf16[640,128]{1,0:T(8,128)(2,1)S(1)}, bf16[640,128]{1,0:T(8,128)(2,1)S(1)}, u32[]{:S(2)}, u32[]{:S(2)}) collective-permute-start(bf16[640,128]{1,0:T(8,128)(2,1)S(1)} %get-tuple-element.108), channel_id=1, source_target_pairs={{0,4},{4,0},{1,5},{5,1},{2,6},{6,2},{3,7},{7,3},{8,12},{12,8},{9,1... | collective-permute-start | bytes 491528 | tf_op jit(solution)/shard_map/ppermute | solution.py:731
  388.1 5.4 collective-permute-start.26
  393.6 1.7 collective-permute-start.27
  446.3 15.9 %collective-permute-start.30 = (bf16[1024,1024]{1,0:T(8,128)(2,1)}, bf16[1024,1024]{1,0:T(8,128)(2,1)S(1)}, u32[]{:S(2)}, u32[]{:S(2)}) collective-permute-start(bf16[1024,1024]{1,0:T(8,128)(2,1)} %get-tuple-element.65), channel_id=1, source_target_pairs={{0,1},{1,0},{2,3},{3,2},{4,5},{5,4},{6,7},{7,6},{8,9},{9,8},{10,11... | collective-permute-start | bytes 6291464 | tf_op jit(solution)/shard_map/ppermute | solution.py:734
  446.4 19.8 %collective-permute-start.29 = (bf16[1024,1024]{1,0:T(8,128)(2,1)}, bf16[1024,1024]{1,0:T(8,128)(2,1)}, u32[]{:S(2)}, u32[]{:S(2)}) collective-permute-start(bf16[1024,1024]{1,0:T(8,128)(2,1)} %get-tuple-element.63), channel_id=1, source_target_pairs={{0,1},{1,0},{2,3},{3,2},{4,5},{5,4},{6,7},{7,6},{8,9},{9,8},{10,11... | collective-permute-start | bytes 6291464 | tf_op jit(solution)/shard_map/ppermute | solution.py:734
  447.7 71.7 %all-to-all-start.3 = ((bf16[4,608,512]{2,1,0:T(8,128)(2,1)}), bf16[4,608,512]{2,1,0:T(8,128)(2,1)}, u32[]{:S(2)}, u32[]{:S(2)}) async-start(bf16[4,608,512]{2,1,0:T(8,128)(2,1)} %pad_maximum_fusion.refs_0_), calls=%async_computation.3 | async-start | bytes 4980736 | tf_op jit(solution)/shard_map/all_to_all | solution.py:720
  465.0 26.1 %collective-permute-start.33 = (bf16[512,1024]{1,0:T(8,128)(2,1)S(1)}, bf16[512,1024]{1,0:T(8,128)(2,1)S(1)}, u32[]{:S(2)}, u32[]{:S(2)}) collective-permute-start(bf16[512,1024]{1,0:T(8,128)(2,1)S(1)} %slice.310), channel_id=1, source_target_pairs={{0,4},{4,0},{1,5},{5,1},{2,6},{6,2},{3,7},{7,3},{8,12},{12,8},{9,1... | collective-permute-start | bytes 3145736 | tf_op jit(solution)/shard_map/ppermute | solution.py:731
  469.2 26.1 %collective-permute-start.31 = (bf16[2,512,512]{2,1,0:T(8,128)(2,1)S(1)}, bf16[2,512,512]{2,1,0:T(8,128)(2,1)S(1)}, u32[]{:S(2)}, u32[]{:S(2)}) collective-permute-start(bf16[2,512,512]{2,1,0:T(8,128)(2,1)S(1)} %pad_maximum_fusion.11), channel_id=1, source_target_pairs={{0,2},{2,0},{1,3},{3,1},{4,6},{6,4},{5,7},{7,5},{8,10},{10,8},{9,1... | collective-permute-start | bytes 3145736 | tf_op jit(solution)/shard_map/ppermute | solution.py:737
  471.9 30.4 %collective-permute-start.37 = (bf16[128,2048]{1,0:T(8,128)(2,1)S(1)}, bf16[128,2048]{1,0:T(8,128)(2,1)S(1)}, u32[]{:S(2)}, u32[]{:S(2)}) collective-permute-start(bf16[128,2048]{1,0:T(8,128)(2,1)S(1)} %add_convert_fusion.1), channel_id=1, source_target_pairs={{0,4},{4,0},{1,5},{5,1},{2,6},{6,2},{3,7},{7,3},{8,12},{12,8},{9,1... | collective-permute-start | bytes 1572872 | tf_op jit(solution)/shard_map/ppermute | solution.py:731
  491.5 13.9 %collective-permute-start.34 = (bf16[512,512]{1,0:T(8,128)(2,1)S(1)}, bf16[512,512]{1,0:T(8,128)(2,1)S(1)}, u32[]{:S(2)}, u32[]{:S(2)}) collective-permute-start(bf16[512,512]{1,0:T(8,128)(2,1)S(1)} %slice.455), channel_id=1, source_target_pairs={{0,2},{2,0},{1,3},{3,1},{4,6},{6,4},{5,7},{7,5},{8,10},{10,8},{9,1... | collective-permute-start | bytes 1572872 | tf_op jit(solution)/shard_map/ppermute | solution.py:737
  495.5 17.0 %collective-permute-start.32 = (bf16[512,512]{1,0:T(8,128)(2,1)S(1)}, bf16[512,512]{1,0:T(8,128)(2,1)S(1)}, u32[]{:S(2)}, u32[]{:S(2)}) collective-permute-start(bf16[512,512]{1,0:T(8,128)(2,1)S(1)} %fusion.9), channel_id=1, source_target_pairs={{0,4},{4,0},{1,5},{5,1},{2,6},{6,2},{3,7},{7,3},{8,12},{12,8},{9,1... | collective-permute-start | bytes 1572872 | tf_op jit(solution)/shard_map/ppermute | solution.py:731
  515.5 2.3 collective-permute-start.35
  517.9 8.8 %collective-permute-start.36 = (f32[2,512]{1,0:T(2,128)S(1)}, f32[2,512]{1,0:T(2,128)S(1)}, u32[]{:S(2)}, u32[]{:S(2)}) collective-permute-start(f32[2,512]{1,0:T(2,128)S(1)} %add.408), channel_id=1, source_target_pairs={{0,2},{2,0},{1,3},{3,1},{4,6},{6,4},{5,7},{7,5},{8,10},{10,8},{9,1... | collective-permute-start | bytes 12296 | tf_op jit(solution)/shard_map/ppermute | solution.py:737
  522.9 3.7 collective-permute-start.38
  525.5 15.9 %collective-permute-start.41 = (bf16[608,512]{1,0:T(8,128)(2,1)S(1)}, bf16[608,512]{1,0:T(8,128)(2,1)S(1)}, u32[]{:S(2)}, u32[]{:S(2)}) collective-permute-start(bf16[608,512]{1,0:T(8,128)(2,1)S(1)} %get-tuple-element.68), channel_id=1, source_target_pairs={{0,4},{4,0},{1,5},{5,1},{2,6},{6,2},{3,7},{7,3},{8,12},{12,8},{9,1... | collective-permute-start | bytes 1867784 | tf_op jit(solution)/shard_map/ppermute | solution.py:731
  526.7 1.2 collective-permute-start.39
  527.8 4.0 collective-permute-start.40
  (56 other events, 327.2 us)
